TPU v7x, 256 devices: a whole 4x4x8 slice. The times are simulated.
256 devices in a mesh: dom: 64 (over z_hi, y, x), rep: 4 (over z_lo, core).
Axes of the slice: x: 4, y: 4, z: 8 (z_hi: 4, z_lo: 2; z = z_hi * 2 + z_lo), core: 2. Of those that a mesh axis runs over, the one named last changes fastest.
Arguments:
- entity_slab: bfloat16 [262144, 400], P('dom'), may hold values from -1.796875 to 1.796875
- entity_state: float32 [262144], P(('dom', 'rep')), may hold values from 0.02 to 0.2
- relation_diag: float32 [1345, 400], replicated, may hold values from -4 to 4
- relation_state: float32 [1345], replicated, may hold values from 0.05 to 0.5
- edge_source: int32 [1048576], P(('dom', 'rep')), may hold values from 0 to 4095
- edge_target: int32 [1048576], P(('dom', 'rep')), may hold values from 0 to 4095
- edge_relation: int32 [1048576], P(('dom', 'rep')), may hold values from 0 to 1344
- edge_count: int32 [256], P(('dom', 'rep')), may hold values from 1 to 4096, 524288 in all
- negatives: int32 [65536], P('dom'), may hold values from 0 to 4095
Outputs:
- new_slab: bfloat16 [262144, 400], P(('dom', 'rep'))
- new_state: float32 [262144], P(('dom', 'rep'))
- new_relation: float32 [1345, 400], replicated
- new_relation_state: float32 [1345], replicated
Inputs may be any that keep to these rules, and one draw needn't show every extreme that they name: `edge_count`: a device's count; some device has exactly 4096 live slots.
All inputs are finite; a program needn't handle non-finite values.
Results may differ from a plain program's by a relative error of at most 0.003.
Values may be sent and summed in bfloat16 or wider, within the bound.
No kernel may reach another device: no remote copies, remote signals or barrier semaphores. Data moves between devices by JAX's collectives and lax.ppermute only.
A program may use at most 128 MiB of HBM per device.

v0:
```python
import jax
import jax.numpy as jnp
from jax import lax
from jax.sharding import PartitionSpec as P

BLOCK = 512


def swapped(x, axis, apart):
    return lax.ppermute(x, axis, [(i, i ^ 1 << apart) for i in range(lax.axis_size(axis))])


def score_edges(s_rows, t_rows, r_rows, negative_rows, valid):
    source = s_rows.astype(jnp.float32)
    target = t_rows.astype(jnp.float32)
    lifted = source * r_rows
    pos = jnp.sum(lifted * target, axis=1)
    lifted_b = lifted.astype(jnp.bfloat16)
    neg = lax.dot_general(
        lifted_b, negative_rows, (((1,), (1,)), ((), ())), preferred_element_type=jnp.float32
    )
    gpos = -jax.nn.sigmoid(-pos) * valid
    gneg = (jax.nn.sigmoid(neg) * (valid[:, None] / neg.shape[1])).astype(jnp.bfloat16)
    grad_u = gpos[:, None] * target + jnp.dot(
        gneg, negative_rows, preferred_element_type=jnp.float32
    )
    grad_t = gpos[:, None] * lifted
    grad_n = lax.dot_general(
        gneg, lifted_b, (((0,), (0,)), ((), ())), preferred_element_type=jnp.float32
    )
    return (grad_u * r_rows, grad_t, grad_u * source, grad_n)


def body(
    entity_slab,
    entity_state,
    relation_diag,
    relation_state,
    edge_source,
    edge_target,
    edge_relation,
    edge_count,
    negatives,
):
    rows_part, width = entity_slab.shape
    groups = lax.axis_size("rep")
    share_rows = rows_part // groups
    rank = lax.axis_index("rep")
    bit = lax.axis_size("dom").bit_length() - 2
    partner = swapped(entity_slab, "dom", bit)
    src, dst, rel, count = (edge_source, edge_target, edge_relation, edge_count[0])
    negative_rows = partner[negatives]
    blocks = (count + BLOCK - 1) // BLOCK
    lanes = jnp.arange(BLOCK, dtype=jnp.int32)

    def one_block(index, carry):
        grad_src, grad_dst, rel_grad, grad_neg = carry
        start = index * BLOCK
        s_idx = lax.dynamic_slice_in_dim(src, start, BLOCK, 0)
        t_idx = lax.dynamic_slice_in_dim(dst, start, BLOCK, 0)
        r_idx = lax.dynamic_slice_in_dim(rel, start, BLOCK, 0)
        valid = (start + lanes < count).astype(jnp.float32)
        grad_s, grad_t, grad_r, grad_n = score_edges(
            entity_slab[s_idx], partner[t_idx], relation_diag[r_idx], negative_rows, valid
        )
        return (
            grad_src.at[s_idx].add(grad_s),
            grad_dst.at[t_idx].add(grad_t),
            rel_grad.at[r_idx].add(grad_r),
            grad_neg + grad_n,
        )

    start_carry = (
        jnp.zeros((rows_part, width), jnp.float32),
        jnp.zeros((rows_part, width), jnp.float32),
        jnp.zeros(relation_diag.shape, jnp.float32),
        jnp.zeros((negatives.shape[0], width), jnp.float32),
    )
    grad_src, grad_dst, rel_grad, grad_neg = lax.fori_loop(0, blocks, one_block, start_carry)
    grad_dst = grad_dst.at[negatives].add(grad_neg)
    returned = swapped(grad_dst, "dom", bit)
    grads = lax.psum_scatter(grad_src + returned, "rep", scatter_dimension=0, tiled=True)
    rel_total = lax.psum(rel_grad, ("dom", "rep"))
    own_rows = lax.dynamic_slice_in_dim(entity_slab, rank * share_rows, share_rows, 0)
    new_state = entity_state + jnp.mean(grads * grads, axis=1)
    new_slab = (own_rows.astype(jnp.float32) - 0.1 * grads / jnp.sqrt(new_state)[:, None]).astype(
        jnp.bfloat16
    )
    new_relation_state = relation_state + jnp.mean(rel_total * rel_total, axis=1)
    new_relation = relation_diag - 0.1 * rel_total / jnp.sqrt(new_relation_state)[:, None]
    return (new_slab, new_state, new_relation, new_relation_state)


def solution(mesh):
    in_specs = (
        P("dom", None),
        P(("dom", "rep")),
        P(),
        P(),
        P(("dom", "rep")),
        P(("dom", "rep")),
        P(("dom", "rep")),
        P(("dom", "rep")),
        P("dom"),
    )
    out_specs = (P(("dom", "rep"), None), P(("dom", "rep")), P(), P())
    return jax.shard_map(body, mesh=mesh, in_specs=in_specs, out_specs=out_specs, check_vma=False)
```

profile of v0, /device:TPU:1, one launch (start us, length us, event | category | flops | bytes accessed | tf_op | source)
XLA Modules:
  0.0 1231.9 jit_solution(2204612959957258623)
XLA Ops:
  8.0 7.8 collective-permute-start
  16.5 6.2 copy.45
  25.5 98.4 %collective-permute-done = bf16[4096,400]{0,1:T(8,128)(2,1)} collective-permute-done((bf16[4096,400]{0,1:T(8,128)(2,1)}, bf16[4096,400]{0,1:T(8,128)(2,1)}, u32[]{:S(2)}, u32[]{:S(2)}) %collective-permute-start) | collective-permute-done | bytes 3276832 | tf_op jit(solution)/shard_map/ppermute | solution.py:10
  123.9 6.0 copy.47
  129.9 7.8 gather_fusion.3
  137.8 4.3 broadcast.71
  142.1 4.3 broadcast.71.clone
  148.1 199.4 %while.17 = (s32[]{:T(128)}, f32[4096,400]{1,0:T(8,128)}, f32[4096,400]{1,0:T(8,128)}, f32[1345,400]{1,0:T(8,128)S(1)}, f32[1024,400]{0,1:T(8,128)}, /*index=5*/...) while((s32[]{:T(128)}, f32[4096,400]{1,0:T(8,128)}, ...), condition=%wide.region_5.6_spmd.clone, body=%wide.region_0.5_spmd.clone.sunk | while | flops 1265839616 | bytes 47536476 | solution.py:79
  148.9 4.5 gather_fusion.1
  155.9 4.7 gather_fusion.2
  162.3 5.4 gather_fusion
  171.7 2.7 multiply_convert_fusion.2
  176.6 2.4 copy.62
  179.1 10.8 scatter_fusion.1
  189.9 2.4 copy.61
  192.3 10.8 scatter_fusion
  203.1 2.4 copy.63
  205.5 5.2 scatter_fusion.2
  210.8 3.8 convolution_add_fusion.3
  215.3 4.5 gather_fusion.1
  222.3 4.7 gather_fusion.2
  228.7 5.4 gather_fusion
  238.1 2.7 multiply_convert_fusion.2
  243.1 2.4 copy.62
  245.5 10.8 scatter_fusion.1
  256.3 2.4 copy.61
  258.7 10.8 scatter_fusion
  269.5 2.4 copy.63
  272.0 5.2 scatter_fusion.2
  277.2 3.8 convolution_add_fusion.3
  281.8 4.5 gather_fusion.1
  288.8 4.7 gather_fusion.2
  295.2 5.4 gather_fusion
  304.6 2.7 multiply_convert_fusion.2
  309.5 2.4 copy.62
  312.0 10.8 scatter_fusion.1
  322.8 2.4 copy.61
  325.2 10.8 scatter_fusion
  338.4 5.2 scatter_fusion.2
  343.7 3.8 convolution_add_fusion.3
  347.5 2.8 copy.48
  350.3 13.8 %scatter_fusion.3 = f32[4096,400]{1,0:T(8,128)} fusion(f32[4096,400]{1,0:T(8,128)} %get-tuple-element.86, s32[1024]{0:T(1024)S(1)} %copy-done.7, f32[1024,400]{1,0:T(8,128)} %copy.48), kind=kCustom, calls=%fused_computation.7 | custom fusion | flops 409600 | bytes 4919296 | tf_op jit(solution)/shard_map/scatter-add | solution.py:80
  364.1 8.6 copy.49
  374.9 8.6 copy.50
  383.4 66.1 %collective-permute-done.1 = f32[4096,400]{0,1:T(8,128)} collective-permute-done((f32[4096,400]{0,1:T(8,128)}, f32[4096,400]{0,1:T(8,128)}, u32[]{:S(2)}, u32[]{:S(2)}) %collective-permute-start.1) | collective-permute-done | bytes 6553632 | tf_op jit(solution)/shard_map/ppermute | solution.py:10
  449.5 8.9 add.84
  458.5 755.6 %all-reduce.2.cloned.1.call-done = f32[1345,400]{0,1:T(8,128)} async-done(((f32[1345,400]{0,1:T(8,128)}), f32[1345,400]{0,1:T(8,128)}) %all-reduce.2.cloned.1.call-update) | async-done | bytes 2152016 | tf_op jit(solution)/shard_map/psum | solution.py:83
  1216.5 3.3 divide_subtract_fusion
  (91 shorter events, 49.6 us)
Async XLA Ops:
  8.0 1206.0 %all-reduce.2.cloned.1.call-start = ((), (), s32[]{:S(2)}) async-start(), calls=%async_computation.2 | async-start | bytes 4505600 | tf_op jit(solution)/shard_map/psum | solution.py:83
  8.0 115.9 %collective-permute-start = (bf16[4096,400]{0,1:T(8,128)(2,1)}, bf16[4096,400]{0,1:T(8,128)(2,1)}, u32[]{:S(2)}, u32[]{:S(2)}) collective-permute-start(bf16[4096,400]{0,1:T(8,128)(2,1)} %param.11), channel_id=1, source_target_pairs={{0,128},{4,132},{8,136},{12,140},{16,144},{20,148},{24,152},{28,15... | collective-permute-start | bytes 9830408 | tf_op jit(solution)/shard_map/ppermute | solution.py:10
  16.5 6.2 copy-start.4
  22.7 2.3 copy-start.9
  171.7 2.8 copy-start
  171.7 2.7 copy-start.2
  171.7 2.7 copy-start.3
  174.4 2.2 copy-start.1
  238.1 2.7 copy-start
  238.1 2.7 copy-start.2
  238.1 2.7 copy-start.3
  240.9 2.2 copy-start.1
  304.6 2.8 copy-start
  304.6 2.7 copy-start.2
  304.6 2.7 copy-start.3
  307.3 2.2 copy-start.1
  347.5 2.8 copy-start.7
  372.7 76.9 %collective-permute-start.1 = (f32[4096,400]{0,1:T(8,128)}, f32[4096,400]{0,1:T(8,128)}, u32[]{:S(2)}, u32[]{:S(2)}) collective-permute-start(f32[4096,400]{0,1:T(8,128)} %copy.49), channel_id=1, source_target_pairs={{0,128},{4,132},{8,136},{12,140},{16,144},{20,148},{24,152},{28,15... | collective-permute-start | bytes 19660808 | tf_op jit(solution)/shard_map/ppermute | solution.py:10
  374.8 845.0 %reduce-scatter.2.cloned.1.call-start = ((), (), s32[]{:S(2)}) async-start(), calls=%async_computation.1 | async-start | bytes 8192000 | tf_op jit(solution)/shard_map/reduce_scatter | solution.py:82
  458.4 757.4 %copy-start.8 = (f32[1345]{0:T(1024)S(1)}, f32[1345]{0:T(1024)}, u32[]{:S(2)}) copy-start(f32[1345]{0:T(1024)} %param.14) | copy-start | bytes 16144
  458.4 758.0 %copy-start.5 = (f32[1345,400]{0,1:T(8,128)S(1)}, f32[1345,400]{0,1:T(8,128)}, u32[]{:S(2)}) copy-start(f32[1345,400]{0,1:T(8,128)} %param.13) | copy-start | bytes 6456004
  1216.5 5.0 copy-start.10
  1219.8 2.3 copy-start.6
Sparse Core Ops, SparseCore 0:
  374.9 839.0 all-reduce.1
Sparse Core Ops, SparseCore 1:
  458.5 586.1 reduce-scatter.1
where the time goes:
time: 1240 us; the launch traced here: 1230 us
  waiting for transfers between devices  920 us (74%)
  local copies, waits for them, and re-layouts  134 us (11%)
  other arithmetic  127 us (10%)
  matrix products  25.9 us (2%)
  between operations  16.2 us (1%)
    psum x1, waiting for transfers between devices, body(): rel_total = lax.psum(rel_grad, ('dom', 'rep'))  756 us
    ppermute x2, waiting for transfers between devices, swapped(): lax.ppermute(x, axis, [(i, i ^ 1 << apart) for i in range(lax.axis_size(a...  164 us
    scatter-add x3, other arithmetic, one_block(): grad_src.at[s_idx].add(grad_s)  32.4 us
    scatter-add x3, other arithmetic, one_block(): grad_dst.at[t_idx].add(grad_t)  32.4 us
  transfers between devices with their start and end apart: 4, of which 3 were waited for; matrix products, arithmetic and copies ran while one was open for 3% of the time, Pallas kernels for 0%

commit v1 on v0

v1 whole, which is shorter than its diff:
```python
import functools

import jax
import jax.numpy as jnp
from jax import lax
from jax.experimental import pallas as pl
from jax.experimental.pallas import tpu as pltpu
from jax.sharding import PartitionSpec as P

BLOCK = 512
LANES = 128
SUBLANES = 8
VMEM_BYTES = 56 << 20
RATE = 0.1
BF16, F32, I32 = jnp.bfloat16, jnp.float32, jnp.int32


def swapped(x, axis, mask):
    return lax.ppermute(x, axis, [(i, i ^ mask) for i in range(lax.axis_size(axis))])


def swapped_far(x, dom_mask, rep_mask):
    doms, reps = lax.axis_size("dom"), lax.axis_size("rep")
    pairs = [
        (d * reps + r, (d ^ dom_mask) * reps + (r ^ rep_mask))
        for d in range(doms)
        for r in range(reps)
    ]
    return lax.ppermute(x, ("dom", "rep"), pairs)


def one_hot(idx, base, rows):
    row = lax.broadcasted_iota(I32, (rows, idx.shape[1]), 0)
    return jnp.where(row == idx - base, 1.0, 0.0).astype(BF16)


def mm(a, b):
    return jnp.dot(a, b, preferred_element_type=F32)


def mm_nt(a, b):
    return lax.dot_general(a, b, (((1,), (1,)), ((), ())), preferred_element_type=F32)


def call(kernel, name, grid, in_specs, out_specs, out_shape, scratch, flops, *args):
    moved = sum(a.size * a.dtype.itemsize for a in args)
    moved += sum(o.size * o.dtype.itemsize for o in jax.tree.leaves(out_shape))
    return pl.pallas_call(
        kernel,
        grid_spec=pltpu.PrefetchScalarGridSpec(
            num_scalar_prefetch=1,
            grid=(grid,),
            in_specs=in_specs,
            out_specs=out_specs,
            scratch_shapes=scratch,
        ),
        out_shape=out_shape,
        compiler_params=pltpu.CompilerParams(vmem_limit_bytes=VMEM_BYTES),
        cost_estimate=pl.CostEstimate(flops=flops, bytes_accessed=moved, transcendentals=0),
        name=name,
    )(*args)


def whole(shape):
    return pl.BlockSpec(shape, lambda i, c: (0,) * len(shape))


def edge_block(rows):
    return pl.BlockSpec((rows, BLOCK), lambda i, c: (0, i))


def live(scal):
    return pl.program_id(0) * BLOCK < scal[0]


def gather_kernel(order, scal, idx_ref, *refs):
    tables, out_ref = refs[:-1], refs[-1]

    @pl.when(live(scal))
    def _():
        idx = idx_ref[...]
        out_ref[...] = gathered(order, scal, idx, tables).astype(out_ref.dtype)


def gathered(order, scal, idx, tables):
    total = None
    for apart, table in zip(order, tables, strict=True):
        rows = table.shape[1]
        base = apart * rows if isinstance(scal, int) else (scal[1] ^ apart) * rows
        y = mm(table[...], one_hot(idx, base, rows))
        total = y if total is None else total + y
    return total


def own_gather_kernel(scal, idx_ref, table_ref, out_ref):
    @pl.when(live(scal))
    def _():
        idx, chunk = idx_ref[...], 1024
        total = None
        for base in range(0, table_ref.shape[1], chunk):
            y = mm(table_ref[:, base : base + chunk], one_hot(idx, base, chunk))
            total = y if total is None else total + y
        out_ref[...] = total.astype(out_ref.dtype)


def relation_gather_kernel(scal, idx_ref, table_ref, out_ref):
    @pl.when(live(scal))
    def _():
        both = mm(table_ref[...], one_hot(idx_ref[...], 0, table_ref.shape[1]))
        half = both.shape[0] // 2
        out_ref[...] = both[:half] + both[half:]


def edge_kernel(
    order,
    scal,
    s_ref,
    r_ref,
    t_idx_ref,
    r_idx_ref,
    neg_t_ref,
    neg_ref,
    *refs,
):
    tables = refs[: len(order)]
    gs_ref, gt_ref, rel_ref, gn_ref, rel_acc, gn_acc = refs[len(order) :]
    i = pl.program_id(0)

    @pl.when(i == 0)
    def _():
        rel_acc[...] = jnp.zeros_like(rel_acc)
        gn_acc[...] = jnp.zeros_like(gn_acc)

    @pl.when(live(scal))
    def _():
        t = gathered(order, scal, t_idx_ref[...], tables)
        s = s_ref[...].astype(F32)
        r = r_ref[...]
        u = s * r
        ub = u.astype(BF16)
        lane = lax.broadcasted_iota(I32, (1, BLOCK), 1) + i * BLOCK
        valid = jnp.where(lane < scal[0], 1.0, 0.0)
        pos = jnp.sum(u * t, axis=0, keepdims=True)
        gpos = -jax.nn.sigmoid(-pos) * valid
        neg = mm(neg_ref[...], ub)
        gneg = (jax.nn.sigmoid(neg) * (valid * (1.0 / neg.shape[0]))).astype(BF16)
        gu = gpos * t + mm(neg_t_ref[...], gneg)
        gs_ref[...] = (gu * r).astype(BF16)
        gt_ref[...] = (gpos * u).astype(BF16)
        gn_acc[...] += mm_nt(ub, gneg)
        hot = one_hot(r_idx_ref[...], 0, rel_acc.shape[1])
        rel_acc[...] += mm_nt((gu * s).astype(BF16), hot)

    @pl.when(i == pl.num_programs(0) - 1)
    def _():
        gn_ref[...] = gn_acc[...].astype(BF16)
        for part, cell, slot, rows, cols in tiles(rel_ref.shape, rel_acc.shape):
            to = (part ^ scal[1], cell ^ (scal[2] & 15), pl.ds(slot * SUBLANES, SUBLANES))
            if rows is None:
                rel_ref[to] = jnp.zeros((SUBLANES, LANES), F32)
            else:
                rel_ref[to] = rel_acc[rows, cols]


def tiles(packed, flat):
    parts, cells, rows, _ = packed
    slots = rows // SUBLANES
    wide = flat[1] // parts // LANES
    for part in range(parts):
        for cell in range(cells):
            for slot in range(slots):
                tile = cell * slots + slot
                row, col = divmod(tile, wide)
                if row * SUBLANES >= flat[0]:
                    yield part, cell, slot, None, None
                else:
                    col = (part * wide + col) * LANES
                    yield (
                        part,
                        cell,
                        slot,
                        slice(row * SUBLANES, (row + 1) * SUBLANES),
                        slice(col, col + LANES),
                    )


def scatter_kernel(with_neg, scal, g_ref, idx_ref, *refs):
    if with_neg:
        gn_ref, n_idx_ref, *refs = refs
    keep_ref, send_ref, acc = refs
    i = pl.program_id(0)
    parts, _, rows = acc.shape

    @pl.when(i == 0)
    def _():
        for apart in range(parts):
            if not with_neg:
                acc[apart] = jnp.zeros(acc.shape[1:], F32)
                continue
            base = (scal[1] ^ apart) * rows
            acc[apart] = mm_nt(gn_ref[...], one_hot(n_idx_ref[...], base, rows))

    @pl.when(live(scal))
    def _():
        idx = idx_ref[...]
        for apart in range(parts):
            base = (scal[1] ^ apart) * rows
            acc[apart] += mm_nt(g_ref[...], one_hot(idx, base, rows))

    @pl.when(i == pl.num_programs(0) - 1)
    def _():
        for apart in range(0, parts, 2):
            keep_ref[apart // 2] = acc[apart]
            send_ref[apart // 2] = acc[apart + 1].astype(BF16)


def scatter(name, scal, g, idx, parts, rows, *neg):
    width, edges = g.shape
    half = (parts // 2, width, rows)
    return call(
        functools.partial(scatter_kernel, bool(neg)),
        name,
        edges // BLOCK,
        [edge_block(width), edge_block(1)] + [whole(x.shape) for x in neg],
        [whole(half), whole(half)],
        [jax.ShapeDtypeStruct(half, F32), jax.ShapeDtypeStruct(half, BF16)],
        [pltpu.VMEM((parts, width, rows), F32)],
        2 * width * parts * rows * edges,
        scal,
        g,
        idx,
        *neg,
    )


def relation_update_kernel(scal, rel_ref, state_ref, *refs):
    g_refs, (new_rel_ref, new_state_ref, flat) = refs[:-3], refs[-3:]
    cells, rows = 16, g_refs[0].shape[2]
    rep = scal[1]
    for k, g_ref in enumerate(g_refs):
        for cell in range(cells):
            away = cell ^ (scal[2] & 15)
            flat[rep ^ k, cell] = g_ref[away & 3, away >> 2].astype(F32)
    parts = len(g_refs)
    wide = 3
    packed = (parts, cells, rows, LANES)
    width, count = rel_ref.shape
    pieces = {}
    for part, cell, slot, trows, tcols in tiles(packed, (width, parts * wide * LANES)):
        if trows is not None:
            pieces[trows.start, tcols.start] = (part, cell, slot)
    for col in range(0, count, LANES):
        n = min(LANES, count - col)
        total = jnp.zeros((1, LANES), F32)
        square = jnp.zeros((SUBLANES, LANES), F32)
        for row in range(0, width, SUBLANES):
            part, cell, slot = pieces[row, col]
            g = flat[part, cell, slot * SUBLANES : (slot + 1) * SUBLANES]
            square = square + g * g
        total = jnp.sum(square, axis=0, keepdims=True) * (1.0 / width)
        state = state_ref[:, col : col + n] + total[:, :n]
        new_state_ref[:, col : col + n] = state
        scale = RATE / jnp.sqrt(state)
        for row in range(0, width, SUBLANES):
            part, cell, slot = pieces[row, col]
            g = flat[part, cell, slot * SUBLANES : (slot + 1) * SUBLANES]
            at = (slice(row, row + SUBLANES), slice(col, col + n))
            new_rel_ref[at] = rel_ref[at] - g[:, :n] * scale


def body(
    entity_slab,
    entity_state,
    relation_diag,
    relation_state,
    edge_source,
    edge_target,
    edge_relation,
    edge_count,
    negatives,
):
    slab = entity_slab.T
    relations = relation_diag.T
    width, rows_part = slab.shape
    reps = lax.axis_size("rep")
    half = lax.axis_size("dom") // 2
    quarter = rows_part // reps
    rep, dom = lax.axis_index("rep"), lax.axis_index("dom")
    edges, n_neg, n_rel = edge_source.shape[0], negatives.shape[0], relation_diag.shape[0]
    scal = jnp.stack([edge_count[0], rep.astype(I32), dom.astype(I32)])
    all_neg = jnp.stack([jnp.int32(n_neg), rep.astype(I32), dom.astype(I32)])
    src, dst, rel = (x.reshape(1, edges) for x in (edge_source, edge_target, edge_relation))
    neg_idx = negatives.reshape(1, n_neg)

    own = lax.dynamic_slice_in_dim(slab, rep * quarter, quarter, 1)
    far = swapped_far(own, half, 2)
    near = swapped(far, "rep", 2)
    far_core = swapped(far, "rep", 1)
    near_core = swapped(near, "rep", 1)
    order = (2, 0, 3, 1)
    tables = (far, near, far_core, near_core)

    s_rows = call(
        own_gather_kernel,
        "source_rows",
        edges // BLOCK,
        [edge_block(1), whole(slab.shape)],
        edge_block(width),
        jax.ShapeDtypeStruct((width, edges), BF16),
        [],
        2 * width * rows_part * edges,
        scal,
        src,
        slab,
    )
    wide = -(-n_rel // (reps * LANES)) * reps * LANES
    padded = jnp.pad(relations, ((0, 0), (0, wide - n_rel)))
    high = padded.astype(BF16)
    low = (padded - high.astype(F32)).astype(BF16)
    split = jnp.concatenate([high, low], axis=0)
    r_rows = call(
        relation_gather_kernel,
        "relation_rows",
        edges // BLOCK,
        [edge_block(1), whole(split.shape)],
        edge_block(width),
        jax.ShapeDtypeStruct((width, edges), F32),
        [],
        4 * width * wide * edges,
        scal,
        rel,
        split,
    )
    neg_t = call(
        functools.partial(gather_kernel, order),
        "negative_rows",
        n_neg // BLOCK,
        [edge_block(1)] + [whole(t.shape) for t in tables],
        edge_block(width),
        jax.ShapeDtypeStruct((width, n_neg), BF16),
        [],
        2 * width * rows_part * n_neg,
        all_neg,
        neg_idx,
        *tables,
    )
    cells = 16
    slots = -(-(width // SUBLANES * wide // reps // LANES) // cells)
    packed = (reps, cells, slots * SUBLANES, LANES)
    grad_s, grad_t, grad_r, grad_n = call(
        functools.partial(edge_kernel, order),
        "edges",
        edges // BLOCK,
        [
            edge_block(width),
            edge_block(width),
            edge_block(1),
            edge_block(1),
            whole((width, n_neg)),
            whole((n_neg, width)),
        ]
        + [whole(t.shape) for t in tables],
        [edge_block(width), edge_block(width), whole(packed), whole((width, n_neg))],
        [
            jax.ShapeDtypeStruct((width, edges), BF16),
            jax.ShapeDtypeStruct((width, edges), BF16),
            jax.ShapeDtypeStruct(packed, F32),
            jax.ShapeDtypeStruct((width, n_neg), BF16),
        ],
        [pltpu.VMEM((width, wide), F32), pltpu.VMEM((width, n_neg), F32)],
        2 * width * edges * (rows_part + 3 * n_neg + wide),
        scal,
        s_rows,
        r_rows,
        dst,
        rel,
        neg_t,
        neg_t.T,
        *tables,
    )

    apart = grad_r.reshape(2, 2, *packed[1:])
    pair = apart[:, 0] + swapped(apart[:, 1], "rep", 1)
    grid = (pair[0] + swapped(pair[1], "rep", 2)).reshape(4, 4, *packed[2:])
    line = (grid[:, 0] + swapped(grid[:, 1], "dom", 1)) + (
        swapped(grid[:, 2], "dom", 2) + swapped(grid[:, 3], "dom", 3)
    )
    cell = (line[0] + swapped(line[1], "dom", 4)) + (
        swapped(line[2], "dom", 8) + swapped(line[3], "dom", 12)
    )
    total = (cell + swapped(cell, "dom", 16)) + (
        swapped(cell, "dom", 32) + swapped(cell, "dom", 48)
    )
    total = total.astype(BF16)
    line = jnp.stack([total] + [swapped(total, "dom", 4 * k) for k in (1, 2, 3)])
    grid = jnp.stack([line] + [swapped(line, "dom", k) for k in (1, 2, 3)])
    other = swapped(grid, "rep", 2)
    grad_rel = (grid, swapped(grid, "rep", 1), other, swapped(other, "rep", 1))

    dst_keep, dst_send = scatter(
        "target_grads", scal, grad_t, dst, reps, quarter, grad_n, neg_idx
    )
    src_keep, src_send = scatter("source_grads", scal, grad_s, src, reps, quarter)
    got = dst_keep + swapped(dst_send, "rep", 1).astype(F32)
    got = got[1] + swapped(got[0].astype(BF16), "rep", 2).astype(F32)
    returned = swapped_far(got.astype(BF16), half, 2)
    kept = src_keep + swapped(src_send, "rep", 1).astype(F32)
    kept = kept[0] + swapped(kept[1].astype(BF16), "rep", 2).astype(F32)
    grads = kept + returned.astype(F32)

    new_state = entity_state + jnp.mean(grads * grads, axis=0)
    new_slab = (own.astype(F32) - RATE * grads / jnp.sqrt(new_state)[None, :]).astype(BF16)
    new_relation, new_relation_state = call(
        relation_update_kernel,
        "relation_update",
        1,
        [whole((width, n_rel)), whole((1, n_rel))] + [whole(g.shape) for g in grad_rel],
        [whole((width, n_rel)), whole((1, n_rel))],
        [jax.ShapeDtypeStruct((width, n_rel), F32), jax.ShapeDtypeStruct((1, n_rel), F32)],
        [pltpu.VMEM((reps, cells, packed[2], LANES), F32)],
        width * n_rel * 8,
        scal,
        relations,
        relation_state.reshape(1, n_rel),
        *grad_rel,
    )
    return (new_slab.T, new_state, new_relation.T, new_relation_state.reshape(n_rel))


def solution(mesh):
    in_specs = (
        P("dom", None),
        P(("dom", "rep")),
        P(),
        P(),
        P(("dom", "rep")),
        P(("dom", "rep")),
        P(("dom", "rep")),
        P(("dom", "rep")),
        P("dom"),
    )
    out_specs = (P(("dom", "rep"), None), P(("dom", "rep")), P(), P())
    return jax.shard_map(body, mesh=mesh, in_specs=in_specs, out_specs=out_specs, check_vma=False)
```

time: 1240 us -> 286 us (0.23)
  waiting for transfers between devices: 920 us -> 88.5 us
  local copies, waits for them, and re-layouts: 134 us -> 11 us
  other arithmetic: 127 us -> 12 us
  starting transfers between devices: 7.91 us -> 93.6 us
  Pallas kernels: 0 us -> 78.8 us
  matrix products: 25.9 us -> 0 us
  between operations: 16.2 us -> 1.49 us
    psum x1 -> x0, waiting for transfers between devices: 756 us -> none  [body(): rel_total = lax.psum(rel_grad, ('dom', 'rep'))]
    scatter-add x10 -> x0, other arithmetic: 94.2 us -> none  [the longest x3 32.4 us: one_block(): grad_src.at[s_idx].add(grad_s)]
    ppermute x2 -> x29, starting transfers between devices: 7.83 us -> 93.6 us  [the longest x27 85.8 us: swapped(): lax.ppermute(x, axis, [(i, i ^ mask) for i in range(lax.axis_size(axis))])]
    pallas_call x0 -> x7, Pallas kernels: none -> 78.8 us  [call(): pl.pallas_call(kernel, grid_spec=pltpu.PrefetchScalarGridSpec(num_scalar_...]
    ppermute x2 -> x29, waiting for transfers between devices: 164 us -> 88.5 us  [the longest x27 59.4 us: swapped(): lax.ppermute(x, axis, [(i, i ^ mask) for i in range(lax.axis_size(axis))])]
    gather x19 -> x0, local copies, waits for them, and re-layouts: 65.5 us -> none  [the longest x6 20.9 us: one_block(): relation_diag[r_idx]]
    dot_general x9 -> x0, matrix products: 25.9 us -> none  [the longest x3 11.3 us: score_edges(): lax.dot_general(gneg, lifted_b, (((0,), (0,)), ((), ())), preferred_eleme...]
    mul x9 -> x0, local copies, waits for them, and re-layouts: 22 us -> none  [the longest x6 14.7 us: score_edges(): return (grad_u * r_rows, grad_t, grad_u * source, grad_n)]
  transfers between devices with their start and end apart: 4 -> 29, of which waited for: 3 -> 14; matrix products, arithmetic and copies ran while one was open for 3% -> 4% of each run, Pallas kernels for 0% -> 18%
where the time goes in v1:
time: 286 us; the launch traced here: 285 us
  starting transfers between devices  93.6 us (33%)
  waiting for transfers between devices  88.5 us (31%)
  Pallas kernels  78.8 us (28%)
  other arithmetic  12 us (4%)
  local copies, waits for them, and re-layouts  11 us (4%)
    ppermute x27, starting transfers between devices, swapped(): lax.ppermute(x, axis, [(i, i ^ mask) for i in range(lax.axis_size(axis))])  85.8 us
    pallas_call x7, Pallas kernels, call(): pl.pallas_call(kernel, grid_spec=pltpu.PrefetchScalarGridSpec(num_scalar_...  78.8 us
    ppermute x27, waiting for transfers between devices, swapped(): lax.ppermute(x, axis, [(i, i ^ mask) for i in range(lax.axis_size(axis))])  59.4 us
    ppermute x2, waiting for transfers between devices, swapped_far(): return lax.ppermute(x, ('dom', 'rep'), pairs)  29.1 us
    ppermute x2, starting transfers between devices, swapped_far(): return lax.ppermute(x, ('dom', 'rep'), pairs)  7.79 us
  transfers between devices with their start and end apart: 29, of which 14 were waited for; matrix products, arithmetic and copies ran while one was open for 4% of the time, Pallas kernels for 18%

profile of v1, /device:TPU:1, one launch (start us, length us, event | category | flops | bytes accessed | tf_op | source)
XLA Modules:
  0.0 285.4 jit_solution(7694732393680440095)
XLA Ops:
  0.6 1.2 dynamic-slice_bitcast_fusion
  1.8 7.4 %collective-permute-start = (bf16[400,1024]{1,0:T(8,128)(2,1)S(1)}, bf16[400,1024]{1,0:T(8,128)(2,1)}, u32[]{:S(2)}, u32[]{:S(2)}) collective-permute-start(bf16[400,1024]{1,0:T(8,128)(2,1)S(1)} %dynamic-slice_bitcast_fusion), channel_id=1, source_target_pairs={{0,130},{1,131},{2,128},{3,129},{4,134},{5,135},{6,132},{7,133},{8... | collective-permute-start | bytes 2457608 | tf_op jit(solution)/shard_map/ppermute | solution.py:29
  10.5 1.9 pad_convert_fusion
  13.0 1.7 pad_maximum_fusion.table_ref
  14.6 29.1 %collective-permute-done.refs_0_ = bf16[400,1024]{1,0:T(8,128)(2,1)} collective-permute-done((bf16[400,1024]{1,0:T(8,128)(2,1)S(1)}, bf16[400,1024]{1,0:T(8,128)(2,1)}, u32[]{:S(2)}, u32[]{:S(2)}) %collective-permute-start) | collective-permute-done | bytes 819232 | tf_op jit(solution)/shard_map/ppermute | solution.py:29
  43.7 1.9 collective-permute-start.1
  45.6 10.1 %source_rows.1.s_ref = bf16[400,4096]{1,0:T(8,128)(2,1)} custom-call(s32[3]{0:T(128)} %get-tuple-element.34.scal, s32[1,4096]{1,0:T(1,128)} %bitcast.116, bf16[400,4096]{1,0:T(8,128)(2,1)} %bitcast.103), custom_call_target="tpu_custom_call" | custom-call | flops 13421772800 | bytes 6569996 | tf_op jit(solution)/shard_map/source_rows/pallas_call | solution.py:48
  55.7 4.0 %collective-permute-start.2 = (bf16[400,1024]{1,0:T(8,128)(2,1)}, bf16[400,1024]{1,0:T(8,128)(2,1)S(1)}, u32[]{:S(2)}, u32[]{:S(2)}) collective-permute-start(bf16[400,1024]{1,0:T(8,128)(2,1)} %collective-permute-done.refs_0_), channel_id=1, source_target_pairs={{0,1},{1,0},{2,3},{3,2},{4,5},{5,4},{6,7},{7,6},{8,9},{9,8},{10,11... | collective-permute-start | bytes 2457608 | tf_op jit(solution)/shard_map/ppermute | solution.py:19
  59.7 3.2 %collective-permute-done.1.refs_1_ = bf16[400,1024]{1,0:T(8,128)(2,1)S(1)} collective-permute-done((bf16[400,1024]{1,0:T(8,128)(2,1)}, bf16[400,1024]{1,0:T(8,128)(2,1)S(1)}, u32[]{:S(2)}, u32[]{:S(2)}) %collective-permute-start.1) | collective-permute-done | bytes 819232 | tf_op jit(solution)/shard_map/ppermute | solution.py:19
  63.0 2.0 collective-permute-start.3
  65.0 9.4 %relation_rows.1.r_ref = f32[400,4096]{1,0:T(8,128)} custom-call(s32[3]{0:T(128)} %get-tuple-element.34.scal, s32[1,4096]{1,0:T(1,128)} %bitcast.112, bf16[800,1536]{1,0:T(8,128)(2,1)} %pad_maximum_fusion.table_ref), custom_call_target="tpu_custom_call" | custom-call | flops 10066329600 | bytes 9027596 | tf_op jit(solution)/shard_map/relation_rows/pallas_call | solution.py:48
  74.4 0.9 copy-done.11
  75.6 7.2 %negative_rows.1.neg_t_ref = bf16[400,1024]{1,0:T(8,128)(2,1)} custom-call(s32[3]{0:T(128)} %get-tuple-element.35.scal, s32[1,1024]{1,0:T(1,128)} %bitcast.118, bf16[400,1024]{1,0:T(8,128)(2,1)} %collective-permute-done.refs_0_, bf16[400,1024]{1,0:T(8,128)(2,1)} %copy-done.10, bf16[400,1024]{1,0:T(8,128)(2,1)} %copy-done.11, bf16[400,1024]{1,0:T(8,128)(2,1)} %copy-done.12), custom_call_target="tpu_custom_call" | custom-call | flops 3355443200 | bytes 4100108 | tf_op jit(solution)/shard_map/negative_rows/pallas_call | solution.py:48
  82.8 2.2 copy.15
  85.0 20.3 %edges.1 = (bf16[400,4096]{1,0:T(8,128)(2,1)}, bf16[400,4096]{1,0:T(8,128)(2,1)}, f32[4,16,80,128]{3,2,1,0:T(8,128)}, bf16[400,1024]{1,0:T(8,128)(2,1)}) custom-call(s32[3]{0:T(128)} %get-tuple-element.34.scal, bf16[400,4096]{1,0:T(8,128)(2,1)} %source_rows.1.s_ref, f32[400,4096]{1,0:T(8,128)} %relation_rows.1.r_ref, s32[1,4096]{1,0:T(1,128)} %bitcast.114, ...), custom_call_target="tpu_custom_call" | custom-call | flops 28521267200 | bytes 24772620 | tf_op jit(solution)/shard_map/edges/pallas_call | solution.py:48
  105.3 1.4 slice_bitcast_fusion.2
  106.7 8.3 %collective-permute-start.9 = (f32[2,16,80,128]{3,2,1,0:T(8,128)S(1)}, f32[2,16,80,128]{3,2,1,0:T(8,128)S(1)}, u32[]{:S(2)}, u32[]{:S(2)}) collective-permute-start(f32[2,16,80,128]{3,2,1,0:T(8,128)S(1)} %slice_bitcast_fusion.2), channel_id=1, source_target_pairs={{0,1},{1,0},{2,3},{3,2},{4,5},{5,4},{6,7},{7,6},{8,9},{9,8},{10,11... | collective-permute-start | bytes 3932168 | tf_op jit(solution)/shard_map/ppermute | solution.py:19
  115.0 15.3 %target_grads.1 = (f32[2,400,1024]{2,1,0:T(8,128)}, bf16[2,400,1024]{2,1,0:T(8,128)(2,1)}) custom-call(s32[3]{0:T(128)} %get-tuple-element.34.scal, bf16[400,4096]{1,0:T(8,128)(2,1)} %get-tuple-element.17.g_ref, s32[1,4096]{1,0:T(1,128)} %bitcast.115, bf16[400,1024]{1,0:T(8,128)(2,1)} %get-tuple-element.18.refs_0_, s32[1,1024]{1,0:T(1,128)} %bitcast.119), custom_call_target="tpu_custom_call" | custom-call | flops 13421772800 | bytes 9031692 | tf_op jit(solution)/shard_map/target_grads/pallas_call | solution.py:48
  130.2 2.9 %collective-permute-start.6 = (bf16[2,400,1024]{2,1,0:T(8,128)(2,1)}, bf16[2,400,1024]{2,1,0:T(8,128)(2,1)S(1)}, u32[]{:S(2)}, u32[]{:S(2)}) collective-permute-start(bf16[2,400,1024]{2,1,0:T(8,128)(2,1)} %get-tuple-element.20), channel_id=1, source_target_pairs={{0,1},{1,0},{2,3},{3,2},{4,5},{5,4},{6,7},{7,6},{8,9},{9,8},{10,11... | collective-permute-start | bytes 4915208 | tf_op jit(solution)/shard_map/ppermute | solution.py:19
  133.3 23.9 %collective-permute-start.10 = (f32[16,80,128]{2,1,0:T(8,128)S(1)}, f32[16,80,128]{2,1,0:T(8,128)S(1)}, u32[]{:S(2)}, u32[]{:S(2)}) collective-permute-start(f32[16,80,128]{2,1,0:T(8,128)S(1)} %slice_bitcast_fusion.4), channel_id=1, source_target_pairs={{0,2},{1,3},{2,0},{3,1},{4,6},{5,7},{6,4},{7,5},{8,10},{9,11},{10,... | collective-permute-start | bytes 1966088 | tf_op jit(solution)/shard_map/ppermute | solution.py:19
  157.2 11.9 %source_grads.1 = (f32[2,400,1024]{2,1,0:T(8,128)}, bf16[2,400,1024]{2,1,0:T(8,128)(2,1)}) custom-call(s32[3]{0:T(128)} %get-tuple-element.34.scal, bf16[400,4096]{1,0:T(8,128)(2,1)} %get-tuple-element.14.g_ref, s32[1,4096]{1,0:T(1,128)} %bitcast.117), custom_call_target="tpu_custom_call" | custom-call | flops 13421772800 | bytes 8208396 | tf_op jit(solution)/shard_map/source_grads/pallas_call | solution.py:48
  169.1 3.6 %collective-permute-start.4 = (bf16[2,400,1024]{2,1,0:T(8,128)(2,1)}, bf16[2,400,1024]{2,1,0:T(8,128)(2,1)S(1)}, u32[]{:S(2)}, u32[]{:S(2)}) collective-permute-start(bf16[2,400,1024]{2,1,0:T(8,128)(2,1)} %get-tuple-element.16), channel_id=1, source_target_pairs={{0,1},{1,0},{2,3},{3,2},{4,5},{5,4},{6,7},{7,6},{8,9},{9,8},{10,11... | collective-permute-start | bytes 4915208 | tf_op jit(solution)/shard_map/ppermute | solution.py:19
  172.9 4.8 %collective-permute-start.11 = (f32[4,80,128]{2,1,0:T(8,128)S(1)}, f32[4,80,128]{2,1,0:T(8,128)S(1)}, u32[]{:S(2)}, u32[]{:S(2)}) collective-permute-start(f32[4,80,128]{2,1,0:T(8,128)S(1)} %get-tuple-element.28), channel_id=1, source_target_pairs={{0,4},{4,0},{8,12},{12,8},{16,20},{20,16},{24,28},{28,24},{32,36},... | collective-permute-start | bytes 491528 | tf_op jit(solution)/shard_map/ppermute | solution.py:19
  177.7 2.9 %collective-permute-start.12 = (f32[4,80,128]{2,1,0:T(8,128)S(1)}, f32[4,80,128]{2,1,0:T(8,128)S(1)}, u32[]{:S(2)}, u32[]{:S(2)}) collective-permute-start(f32[4,80,128]{2,1,0:T(8,128)S(1)} %get-tuple-element.27), channel_id=1, source_target_pairs={{0,8},{4,12},{8,0},{12,4},{16,24},{20,28},{24,16},{28,20},{32,40},... | collective-permute-start | bytes 491528 | tf_op jit(solution)/shard_map/ppermute | solution.py:19
  181.8 6.8 %collective-permute-done.12 = f32[4,80,128]{2,1,0:T(8,128)S(1)} collective-permute-done((f32[4,80,128]{2,1,0:T(8,128)S(1)}, f32[4,80,128]{2,1,0:T(8,128)S(1)}, u32[]{:S(2)}, u32[]{:S(2)}) %collective-permute-start.12) | collective-permute-done | bytes 163872 | tf_op jit(solution)/shard_map/ppermute | solution.py:19
  188.6 2.3 collective-permute-done.13
  191.6 4.3 %collective-permute-start.15 = (f32[80,128]{1,0:T(8,128)S(1)}, f32[80,128]{1,0:T(8,128)S(1)}, u32[]{:S(2)}, u32[]{:S(2)}) collective-permute-start(f32[80,128]{1,0:T(8,128)S(1)} %get-tuple-element.30), channel_id=1, source_target_pairs={{0,32},{4,36},{8,40},{12,44},{16,48},{20,52},{24,56},{28,60},{32,0... | collective-permute-start | bytes 122888 | tf_op jit(solution)/shard_map/ppermute | solution.py:19
  196.5 1.2 collective-permute-done.15
  197.7 2.2 collective-permute-done.16
  200.1 4.5 %collective-permute-start.18 = (f32[80,128]{1,0:T(8,128)S(1)}, f32[80,128]{1,0:T(8,128)S(1)}, u32[]{:S(2)}, u32[]{:S(2)}) collective-permute-start(f32[80,128]{1,0:T(8,128)S(1)} %fusion.12), channel_id=1, source_target_pairs={{0,128},{4,132},{8,136},{12,140},{16,144},{20,148},{24,152},{28,15... | collective-permute-start | bytes 122888 | tf_op jit(solution)/shard_map/ppermute | solution.py:19
  204.5 1.2 collective-permute-start.19
  206.5 7.5 %collective-permute-done.17 = f32[80,128]{1,0:T(8,128)S(1)} collective-permute-done((f32[80,128]{1,0:T(8,128)S(1)}, f32[80,128]{1,0:T(8,128)S(1)}, u32[]{:S(2)}, u32[]{:S(2)}) %collective-permute-start.17) | collective-permute-done | bytes 40992 | tf_op jit(solution)/shard_map/ppermute | solution.py:19
  214.0 7.4 %collective-permute-done.18 = f32[80,128]{1,0:T(8,128)S(1)} collective-permute-done((f32[80,128]{1,0:T(8,128)S(1)}, f32[80,128]{1,0:T(8,128)S(1)}, u32[]{:S(2)}, u32[]{:S(2)}) %collective-permute-start.18) | collective-permute-done | bytes 40992 | tf_op jit(solution)/shard_map/ppermute | solution.py:19
  221.9 1.8 collective-permute-start.21
  223.7 1.8 collective-permute-start.22
  225.4 1.0 fusion.5
  226.5 1.0 collective-permute-done.22
  227.6 3.5 %collective-permute-start.24 = (bf16[4,80,128]{2,1,0:T(8,128)(2,1)S(1)}, bf16[4,80,128]{2,1,0:T(8,128)(2,1)S(1)}, u32[]{:S(2)}, u32[]{:S(2)}) collective-permute-start(bf16[4,80,128]{2,1,0:T(8,128)(2,1)S(1)} %get-tuple-element.33), channel_id=1, source_target_pairs={{0,8},{4,12},{8,0},{12,4},{16,24},{20,28},{24,16},{28,20},{32,40},... | collective-permute-start | bytes 245768 | tf_op jit(solution)/shard_map/ppermute | solution.py:19
  231.5 1.2 fusion.1
  233.1 0.8 collective-permute-done.24
  233.9 1.8 collective-permute-done.25
  235.8 7.1 %collective-permute-start.26 = (bf16[4,4,80,128]{3,2,1,0:T(8,128)(2,1)S(1)}, bf16[4,4,80,128]{3,2,1,0:T(8,128)(2,1)S(1)}, u32[]{:S(2)}, u32[]{:S(2)}) collective-permute-start(bf16[4,4,80,128]{3,2,1,0:T(8,128)(2,1)S(1)} %pad_maximum_fusion.1.refs_0_), channel_id=1, source_target_pairs={{0,1},{1,0},{2,3},{3,2},{4,5},{5,4},{6,7},{7,6},{8,9},{9,8},{10,11... | collective-permute-start | bytes 983048 | tf_op jit(solution)/shard_map/ppermute | solution.py:19
  242.9 23.9 %collective-permute-done.27.refs_2_ = bf16[4,4,80,128]{3,2,1,0:T(8,128)(2,1)S(1)} collective-permute-done((bf16[4,4,80,128]{3,2,1,0:T(8,128)(2,1)S(1)}, bf16[4,4,80,128]{3,2,1,0:T(8,128)(2,1)S(1)}, u32[]{:S(2)}, u32[]{:S(2)}) %collective-permute-start.27) | collective-permute-done | bytes 327712 | tf_op jit(solution)/shard_map/ppermute | solution.py:19
  266.8 5.1 %collective-permute-start.28 = (bf16[4,4,80,128]{3,2,1,0:T(8,128)(2,1)S(1)}, bf16[4,4,80,128]{3,2,1,0:T(8,128)(2,1)S(1)}, u32[]{:S(2)}, u32[]{:S(2)}) collective-permute-start(bf16[4,4,80,128]{3,2,1,0:T(8,128)(2,1)S(1)} %collective-permute-done.27.refs_2_), channel_id=1, source_target_pairs={{0,1},{1,0},{2,3},{3,2},{4,5},{5,4},{6,7},{7,6},{8,9},{9,8},{10,11... | collective-permute-start | bytes 983048 | tf_op jit(solution)/shard_map/ppermute | solution.py:19
  274.0 4.6 %relation_update.1 = (f32[400,1345]{1,0:T(8,128)}, f32[1,1345]{1,0:T(1,128)}) custom-call(s32[3]{0:T(128)} %get-tuple-element.34.scal, f32[400,1345]{1,0:T(8,128)} %bitcast.96, f32[1,1345]{1,0:T(1,128)} %reshape.39.state_ref, bf16[4,4,80,128]{3,2,1,0:T(8,128)(2,1)} %copy-done.4, bf16[4,4,80,128]{3,2,1,0:T(8,128)(2,1)} %copy-done.6, ...), custom_call_target="tpu_custom_call" | custom-call | flops 4304000 | bytes 5625492 | tf_op jit(solution)/shard_map/relation_update/pallas_call | solution.py:48
  278.6 1.3 reduce
  279.9 1.8 multiply_reduce_fusion
  282.3 3.1 %fusion.7 = bf16[1024,400]{0,1:T(8,128)(2,1)} fusion(f32[1024]{0:T(1024)S(1)} %get-tuple-element.24, bf16[400,1024]{1,0:T(8,128)(2,1)} %collective-permute-done.8, bf16[400,1024]{1,0:T(8,128)(2,1)} %collective-permute-done.5, f32[2,400,1024]{2,1,0:T(8,128)S(1)} %convert_add_fusion.1, bf16[4096,400]{0,1:T(8,128)(2,1)} %param.9, s32[]{:T(128)S(6)} %select_n.3), kind=kLoop, calls=%fused_computation.21 | loop fusion | flops 3686400 | bytes 4919300 | tf_op jit(solution)/shard_map/transpose | solution.py:427
  (70 shorter events, 9.2 us)
Async XLA Ops:
  1.8 41.9 %collective-permute-start = (bf16[400,1024]{1,0:T(8,128)(2,1)S(1)}, bf16[400,1024]{1,0:T(8,128)(2,1)}, u32[]{:S(2)}, u32[]{:S(2)}) collective-permute-start(bf16[400,1024]{1,0:T(8,128)(2,1)S(1)} %dynamic-slice_bitcast_fusion), channel_id=1, source_target_pairs={{0,130},{1,131},{2,128},{3,129},{4,134},{5,135},{6,132},{7,133},{8... | collective-permute-start | bytes 2457608 | tf_op jit(solution)/shard_map/ppermute | solution.py:29
  10.5 2.3 copy-start
  43.7 19.2 %collective-permute-start.1 = (bf16[400,1024]{1,0:T(8,128)(2,1)}, bf16[400,1024]{1,0:T(8,128)(2,1)S(1)}, u32[]{:S(2)}, u32[]{:S(2)}) collective-permute-start(bf16[400,1024]{1,0:T(8,128)(2,1)} %collective-permute-done.refs_0_), channel_id=1, source_target_pairs={{0,2},{1,3},{2,0},{3,1},{4,6},{5,7},{6,4},{7,5},{8,10},{9,11},{10,... | collective-permute-start | bytes 2457608 | tf_op jit(solution)/shard_map/ppermute | solution.py:19
  55.7 18.6 %collective-permute-start.2 = (bf16[400,1024]{1,0:T(8,128)(2,1)}, bf16[400,1024]{1,0:T(8,128)(2,1)S(1)}, u32[]{:S(2)}, u32[]{:S(2)}) collective-permute-start(bf16[400,1024]{1,0:T(8,128)(2,1)} %collective-permute-done.refs_0_), channel_id=1, source_target_pairs={{0,1},{1,0},{2,3},{3,2},{4,5},{5,4},{6,7},{7,6},{8,9},{9,8},{10,11... | collective-permute-start | bytes 2457608 | tf_op jit(solution)/shard_map/ppermute | solution.py:19
  63.0 11.4 %copy-start.10 = (bf16[400,1024]{1,0:T(8,128)(2,1)}, bf16[400,1024]{1,0:T(8,128)(2,1)S(1)}, u32[]{:S(2)}) copy-start(bf16[400,1024]{1,0:T(8,128)(2,1)S(1)} %collective-permute-done.1.refs_1_) | copy-start | bytes 2457604
  63.0 11.4 %collective-permute-start.3 = (bf16[400,1024]{1,0:T(8,128)(2,1)S(1)}, bf16[400,1024]{1,0:T(8,128)(2,1)S(1)}, u32[]{:S(2)}, u32[]{:S(2)}) collective-permute-start(bf16[400,1024]{1,0:T(8,128)(2,1)S(1)} %collective-permute-done.1.refs_1_), channel_id=1, source_target_pairs={{0,1},{1,0},{2,3},{3,2},{4,5},{5,4},{6,7},{7,6},{8,9},{9,8},{10,11... | collective-permute-start | bytes 2457608 | tf_op jit(solution)/shard_map/ppermute | solution.py:19
  74.4 0.9 copy-start.11
  74.4 1.2 copy-start.12
  106.7 26.4 %collective-permute-start.9 = (f32[2,16,80,128]{3,2,1,0:T(8,128)S(1)}, f32[2,16,80,128]{3,2,1,0:T(8,128)S(1)}, u32[]{:S(2)}, u32[]{:S(2)}) collective-permute-start(f32[2,16,80,128]{3,2,1,0:T(8,128)S(1)} %slice_bitcast_fusion.2), channel_id=1, source_target_pairs={{0,1},{1,0},{2,3},{3,2},{4,5},{5,4},{6,7},{7,6},{8,9},{9,8},{10,11... | collective-permute-start | bytes 3932168 | tf_op jit(solution)/shard_map/ppermute | solution.py:19
  115.0 18.1 %copy-start.3 = (f32[4,16,80,128]{3,2,1,0:T(8,128)S(1)}, f32[4,16,80,128]{3,2,1,0:T(8,128)}, u32[]{:S(2)}) copy-start(f32[4,16,80,128]{3,2,1,0:T(8,128)} %get-tuple-element.21) | copy-start | bytes 7864324
  130.2 50.5 %collective-permute-start.6 = (bf16[2,400,1024]{2,1,0:T(8,128)(2,1)}, bf16[2,400,1024]{2,1,0:T(8,128)(2,1)S(1)}, u32[]{:S(2)}, u32[]{:S(2)}) collective-permute-start(bf16[2,400,1024]{2,1,0:T(8,128)(2,1)} %get-tuple-element.20), channel_id=1, source_target_pairs={{0,1},{1,0},{2,3},{3,2},{4,5},{5,4},{6,7},{7,6},{8,9},{9,8},{10,11... | collective-permute-start | bytes 4915208 | tf_op jit(solution)/shard_map/ppermute | solution.py:19
  133.3 39.5 %collective-permute-start.10 = (f32[16,80,128]{2,1,0:T(8,128)S(1)}, f32[16,80,128]{2,1,0:T(8,128)S(1)}, u32[]{:S(2)}, u32[]{:S(2)}) collective-permute-start(f32[16,80,128]{2,1,0:T(8,128)S(1)} %slice_bitcast_fusion.4), channel_id=1, source_target_pairs={{0,2},{1,3},{2,0},{3,1},{4,6},{5,7},{6,4},{7,5},{8,10},{9,11},{10,... | collective-permute-start | bytes 1966088 | tf_op jit(solution)/shard_map/ppermute | solution.py:19
  157.2 23.6 %copy-start.2 = (f32[2,400,1024]{2,1,0:T(8,128)S(1)}, f32[2,400,1024]{2,1,0:T(8,128)}, u32[]{:S(2)}) copy-start(f32[2,400,1024]{2,1,0:T(8,128)} %get-tuple-element.19) | copy-start | bytes 9830404
  169.1 36.6 %collective-permute-start.4 = (bf16[2,400,1024]{2,1,0:T(8,128)(2,1)}, bf16[2,400,1024]{2,1,0:T(8,128)(2,1)S(1)}, u32[]{:S(2)}, u32[]{:S(2)}) collective-permute-start(bf16[2,400,1024]{2,1,0:T(8,128)(2,1)} %get-tuple-element.16), channel_id=1, source_target_pairs={{0,1},{1,0},{2,3},{3,2},{4,5},{5,4},{6,7},{7,6},{8,9},{9,8},{10,11... | collective-permute-start | bytes 4915208 | tf_op jit(solution)/shard_map/ppermute | solution.py:19
  172.9 8.9 %collective-permute-start.11 = (f32[4,80,128]{2,1,0:T(8,128)S(1)}, f32[4,80,128]{2,1,0:T(8,128)S(1)}, u32[]{:S(2)}, u32[]{:S(2)}) collective-permute-start(f32[4,80,128]{2,1,0:T(8,128)S(1)} %get-tuple-element.28), channel_id=1, source_target_pairs={{0,4},{4,0},{8,12},{12,8},{16,20},{20,16},{24,28},{28,24},{32,36},... | collective-permute-start | bytes 491528 | tf_op jit(solution)/shard_map/ppermute | solution.py:19
  177.7 10.9 %collective-permute-start.12 = (f32[4,80,128]{2,1,0:T(8,128)S(1)}, f32[4,80,128]{2,1,0:T(8,128)S(1)}, u32[]{:S(2)}, u32[]{:S(2)}) collective-permute-start(f32[4,80,128]{2,1,0:T(8,128)S(1)} %get-tuple-element.27), channel_id=1, source_target_pairs={{0,8},{4,12},{8,0},{12,4},{16,24},{20,28},{24,16},{28,20},{32,40},... | collective-permute-start | bytes 491528 | tf_op jit(solution)/shard_map/ppermute | solution.py:19
  180.6 10.3 %collective-permute-start.13 = (f32[4,80,128]{2,1,0:T(8,128)S(1)}, f32[4,80,128]{2,1,0:T(8,128)S(1)}, u32[]{:S(2)}, u32[]{:S(2)}) collective-permute-start(f32[4,80,128]{2,1,0:T(8,128)S(1)} %get-tuple-element.26), channel_id=1, source_target_pairs={{0,12},{4,8},{8,4},{12,0},{16,28},{20,24},{24,20},{28,16},{32,44},... | collective-permute-start | bytes 491528 | tf_op jit(solution)/shard_map/ppermute | solution.py:19
  180.8 24.9 %copy-start.1 = (f32[2,400,1024]{2,1,0:T(8,128)S(1)}, f32[2,400,1024]{2,1,0:T(8,128)}, u32[]{:S(2)}) copy-start(f32[2,400,1024]{2,1,0:T(8,128)} %get-tuple-element.15) | copy-start | bytes 9830404
  191.0 5.5 %collective-permute-start.14 = (f32[80,128]{1,0:T(8,128)S(1)}, f32[80,128]{1,0:T(8,128)S(1)}, u32[]{:S(2)}, u32[]{:S(2)}) collective-permute-start(f32[80,128]{1,0:T(8,128)S(1)} %get-tuple-element.31), channel_id=1, source_target_pairs={{0,16},{4,20},{8,24},{12,28},{16,0},{20,4},{24,8},{28,12},{32,48},... | collective-permute-start | bytes 122888 | tf_op jit(solution)/shard_map/ppermute | solution.py:19
  191.6 6.1 %collective-permute-start.15 = (f32[80,128]{1,0:T(8,128)S(1)}, f32[80,128]{1,0:T(8,128)S(1)}, u32[]{:S(2)}, u32[]{:S(2)}) collective-permute-start(f32[80,128]{1,0:T(8,128)S(1)} %get-tuple-element.30), channel_id=1, source_target_pairs={{0,32},{4,36},{8,40},{12,44},{16,48},{20,52},{24,56},{28,60},{32,0... | collective-permute-start | bytes 122888 | tf_op jit(solution)/shard_map/ppermute | solution.py:19
  195.9 4.1 %collective-permute-start.16 = (f32[80,128]{1,0:T(8,128)S(1)}, f32[80,128]{1,0:T(8,128)S(1)}, u32[]{:S(2)}, u32[]{:S(2)}) collective-permute-start(f32[80,128]{1,0:T(8,128)S(1)} %get-tuple-element.29), channel_id=1, source_target_pairs={{0,48},{4,52},{8,56},{12,60},{16,32},{20,36},{24,40},{28,44},{32,1... | collective-permute-start | bytes 122888 | tf_op jit(solution)/shard_map/ppermute | solution.py:19
  196.0 35.5 %collective-permute-start.7 = (bf16[400,1024]{1,0:T(8,128)(2,1)S(1)}, bf16[400,1024]{1,0:T(8,128)(2,1)S(1)}, u32[]{:S(2)}, u32[]{:S(2)}) collective-permute-start(bf16[400,1024]{1,0:T(8,128)(2,1)S(1)} %fusion.6), channel_id=1, source_target_pairs={{0,2},{1,3},{2,0},{3,1},{4,6},{5,7},{6,4},{7,5},{8,10},{9,11},{10,... | collective-permute-start | bytes 2457608 | tf_op jit(solution)/shard_map/ppermute | solution.py:19
  200.0 14.1 %collective-permute-start.17 = (f32[80,128]{1,0:T(8,128)S(1)}, f32[80,128]{1,0:T(8,128)S(1)}, u32[]{:S(2)}, u32[]{:S(2)}) collective-permute-start(f32[80,128]{1,0:T(8,128)S(1)} %fusion.12), channel_id=1, source_target_pairs={{0,64},{4,68},{8,72},{12,76},{16,80},{20,84},{24,88},{28,92},{32,9... | collective-permute-start | bytes 122888 | tf_op jit(solution)/shard_map/ppermute | solution.py:19
  200.1 21.4 %collective-permute-start.18 = (f32[80,128]{1,0:T(8,128)S(1)}, f32[80,128]{1,0:T(8,128)S(1)}, u32[]{:S(2)}, u32[]{:S(2)}) collective-permute-start(f32[80,128]{1,0:T(8,128)S(1)} %fusion.12), channel_id=1, source_target_pairs={{0,128},{4,132},{8,136},{12,140},{16,144},{20,148},{24,152},{28,15... | collective-permute-start | bytes 122888 | tf_op jit(solution)/shard_map/ppermute | solution.py:19
  204.5 16.9 %collective-permute-start.19 = (f32[80,128]{1,0:T(8,128)S(1)}, f32[80,128]{1,0:T(8,128)S(1)}, u32[]{:S(2)}, u32[]{:S(2)}) collective-permute-start(f32[80,128]{1,0:T(8,128)S(1)} %fusion.12), channel_id=1, source_target_pairs={{0,192},{4,196},{8,200},{12,204},{16,208},{20,212},{24,216},{28,22... | collective-permute-start | bytes 122888 | tf_op jit(solution)/shard_map/ppermute | solution.py:19
  221.5 5.0 %collective-permute-start.20 = (bf16[80,128]{1,0:T(8,128)(2,1)S(1)}, bf16[80,128]{1,0:T(8,128)(2,1)S(1)}, u32[]{:S(2)}, u32[]{:S(2)}) collective-permute-start(bf16[80,128]{1,0:T(8,128)(2,1)S(1)} %add_convert_fusion), channel_id=1, source_target_pairs={{0,16},{4,20},{8,24},{12,28},{16,0},{20,4},{24,8},{28,12},{32,48},... | collective-permute-start | bytes 61448 | tf_op jit(solution)/shard_map/ppermute | solution.py:19
  221.9 4.6 %collective-permute-start.21 = (bf16[80,128]{1,0:T(8,128)(2,1)S(1)}, bf16[80,128]{1,0:T(8,128)(2,1)S(1)}, u32[]{:S(2)}, u32[]{:S(2)}) collective-permute-start(bf16[80,128]{1,0:T(8,128)(2,1)S(1)} %add_convert_fusion), channel_id=1, source_target_pairs={{0,32},{4,36},{8,40},{12,44},{16,48},{20,52},{24,56},{28,60},{32,0... | collective-permute-start | bytes 61448 | tf_op jit(solution)/shard_map/ppermute | solution.py:19
  223.7 3.8 %collective-permute-start.22 = (bf16[80,128]{1,0:T(8,128)(2,1)S(1)}, bf16[80,128]{1,0:T(8,128)(2,1)S(1)}, u32[]{:S(2)}, u32[]{:S(2)}) collective-permute-start(bf16[80,128]{1,0:T(8,128)(2,1)S(1)} %add_convert_fusion), channel_id=1, source_target_pairs={{0,48},{4,52},{8,56},{12,60},{16,32},{20,36},{24,40},{28,44},{32,1... | collective-permute-start | bytes 61448 | tf_op jit(solution)/shard_map/ppermute | solution.py:19
  226.5 53.4 %collective-permute-start.5 = (bf16[400,1024]{1,0:T(8,128)(2,1)}, bf16[400,1024]{1,0:T(8,128)(2,1)}, u32[]{:S(2)}, u32[]{:S(2)}) collective-permute-start(bf16[400,1024]{1,0:T(8,128)(2,1)} %fusion.5), channel_id=1, source_target_pairs={{0,2},{1,3},{2,0},{3,1},{4,6},{5,7},{6,4},{7,5},{8,10},{9,11},{10,... | collective-permute-start | bytes 2457608 | tf_op jit(solution)/shard_map/ppermute | solution.py:19
  227.5 44.4 %copy-start.8 = (f32[1345]{0:T(1024)S(1)}, f32[1345]{0:T(1024)}, u32[]{:S(2)}) copy-start(f32[1345]{0:T(1024)} %param.12) | copy-start | bytes 16144
  227.5 5.5 %collective-permute-start.23 = (bf16[4,80,128]{2,1,0:T(8,128)(2,1)S(1)}, bf16[4,80,128]{2,1,0:T(8,128)(2,1)S(1)}, u32[]{:S(2)}, u32[]{:S(2)}) collective-permute-start(bf16[4,80,128]{2,1,0:T(8,128)(2,1)S(1)} %get-tuple-element.33), channel_id=1, source_target_pairs={{0,4},{4,0},{8,12},{12,8},{16,20},{20,16},{24,28},{28,24},{32,36},... | collective-permute-start | bytes 245768 | tf_op jit(solution)/shard_map/ppermute | solution.py:19
  227.6 6.2 %collective-permute-start.24 = (bf16[4,80,128]{2,1,0:T(8,128)(2,1)S(1)}, bf16[4,80,128]{2,1,0:T(8,128)(2,1)S(1)}, u32[]{:S(2)}, u32[]{:S(2)}) collective-permute-start(bf16[4,80,128]{2,1,0:T(8,128)(2,1)S(1)} %get-tuple-element.33), channel_id=1, source_target_pairs={{0,8},{4,12},{8,0},{12,4},{16,24},{20,28},{24,16},{28,20},{32,40},... | collective-permute-start | bytes 245768 | tf_op jit(solution)/shard_map/ppermute | solution.py:19
  231.2 4.5 %collective-permute-start.25 = (bf16[4,80,128]{2,1,0:T(8,128)(2,1)S(1)}, bf16[4,80,128]{2,1,0:T(8,128)(2,1)S(1)}, u32[]{:S(2)}, u32[]{:S(2)}) collective-permute-start(bf16[4,80,128]{2,1,0:T(8,128)(2,1)S(1)} %get-tuple-element.33), channel_id=1, source_target_pairs={{0,12},{4,8},{8,4},{12,0},{16,28},{20,24},{24,20},{28,16},{32,44},... | collective-permute-start | bytes 245768 | tf_op jit(solution)/shard_map/ppermute | solution.py:19
  232.6 47.2 %collective-permute-start.8 = (bf16[400,1024]{1,0:T(8,128)(2,1)}, bf16[400,1024]{1,0:T(8,128)(2,1)}, u32[]{:S(2)}, u32[]{:S(2)}) collective-permute-start(bf16[400,1024]{1,0:T(8,128)(2,1)} %fusion.1), channel_id=1, source_target_pairs={{0,130},{1,131},{2,128},{3,129},{4,134},{5,135},{6,132},{7,133},{8... | collective-permute-start | bytes 2457608 | tf_op jit(solution)/shard_map/ppermute | solution.py:29
  235.7 37.5 %copy-start.4 = (bf16[4,4,80,128]{3,2,1,0:T(8,128)(2,1)}, bf16[4,4,80,128]{3,2,1,0:T(8,128)(2,1)S(1)}, u32[]{:S(2)}) copy-start(bf16[4,4,80,128]{3,2,1,0:T(8,128)(2,1)S(1)} %pad_maximum_fusion.1.refs_0_) | copy-start | bytes 983044
  235.7 31.1 %collective-permute-start.27 = (bf16[4,4,80,128]{3,2,1,0:T(8,128)(2,1)S(1)}, bf16[4,4,80,128]{3,2,1,0:T(8,128)(2,1)S(1)}, u32[]{:S(2)}, u32[]{:S(2)}) collective-permute-start(bf16[4,4,80,128]{3,2,1,0:T(8,128)(2,1)S(1)} %pad_maximum_fusion.1.refs_0_), channel_id=1, source_target_pairs={{0,2},{1,3},{2,0},{3,1},{4,6},{5,7},{6,4},{7,5},{8,10},{9,11},{10,... | collective-permute-start | bytes 983048 | tf_op jit(solution)/shard_map/ppermute | solution.py:19
  235.8 36.7 %collective-permute-start.26 = (bf16[4,4,80,128]{3,2,1,0:T(8,128)(2,1)S(1)}, bf16[4,4,80,128]{3,2,1,0:T(8,128)(2,1)S(1)}, u32[]{:S(2)}, u32[]{:S(2)}) collective-permute-start(bf16[4,4,80,128]{3,2,1,0:T(8,128)(2,1)S(1)} %pad_maximum_fusion.1.refs_0_), channel_id=1, source_target_pairs={{0,1},{1,0},{2,3},{3,2},{4,5},{5,4},{6,7},{7,6},{8,9},{9,8},{10,11... | collective-permute-start | bytes 983048 | tf_op jit(solution)/shard_map/ppermute | solution.py:19
  266.8 6.4 %copy-start.5 = (bf16[4,4,80,128]{3,2,1,0:T(8,128)(2,1)}, bf16[4,4,80,128]{3,2,1,0:T(8,128)(2,1)S(1)}, u32[]{:S(2)}) copy-start(bf16[4,4,80,128]{3,2,1,0:T(8,128)(2,1)S(1)} %collective-permute-done.27.refs_2_) | copy-start | bytes 983044
  266.8 6.4 %collective-permute-start.28 = (bf16[4,4,80,128]{3,2,1,0:T(8,128)(2,1)S(1)}, bf16[4,4,80,128]{3,2,1,0:T(8,128)(2,1)S(1)}, u32[]{:S(2)}, u32[]{:S(2)}) collective-permute-start(bf16[4,4,80,128]{3,2,1,0:T(8,128)(2,1)S(1)} %collective-permute-done.27.refs_2_), channel_id=1, source_target_pairs={{0,1},{1,0},{2,3},{3,2},{4,5},{5,4},{6,7},{7,6},{8,9},{9,8},{10,11... | collective-permute-start | bytes 983048 | tf_op jit(solution)/shard_map/ppermute | solution.py:19
  272.5 0.7 copy-start.6
  273.3 0.7 copy-start.7
  279.9 1.8 copy-start.9

commit v2 on v0

v2 whole, which is shorter than its diff:
```python
import functools

import jax
import jax.numpy as jnp
from jax import lax
from jax.experimental import pallas as pl
from jax.experimental.pallas import tpu as pltpu
from jax.sharding import PartitionSpec as P

BLOCK = 512
FINE = 256
WIDE = 1024
WINDOW = 1280
LANES = 128
SUBLANES = 8
PIECES = 2
RETURNS = 2
VMEM_BYTES = 56 << 20
RATE = 0.1
BF16, F32, I32 = jnp.bfloat16, jnp.float32, jnp.int32


def swapped(x, axis, mask):
    return lax.ppermute(x, axis, [(i, i ^ mask) for i in range(lax.axis_size(axis))])


def swapped_far(x, dom_mask, rep_mask):
    doms, reps = lax.axis_size("dom"), lax.axis_size("rep")
    pairs = [
        (d * reps + r, (d ^ dom_mask) * reps + (r ^ rep_mask))
        for d in range(doms)
        for r in range(reps)
    ]
    return lax.ppermute(x, ("dom", "rep"), pairs)


def one_hot(idx, base, rows):
    row = lax.broadcasted_iota(I32, (rows, idx.shape[1]), 0)
    return jnp.where(row == idx - base, 1.0, 0.0).astype(BF16)


def mm(a, b):
    return jnp.dot(a, b, preferred_element_type=F32)


def mm_nt(a, b):
    return lax.dot_general(a, b, (((1,), (1,)), ((), ())), preferred_element_type=F32)


def call(kernel, name, grid, in_specs, out_specs, out_shape, scratch, *args):
    return pl.pallas_call(
        kernel,
        grid_spec=pltpu.PrefetchScalarGridSpec(
            num_scalar_prefetch=1,
            grid=(grid,),
            in_specs=in_specs,
            out_specs=out_specs,
            scratch_shapes=scratch,
        ),
        out_shape=out_shape,
        compiler_params=pltpu.CompilerParams(vmem_limit_bytes=VMEM_BYTES),
        cost_estimate=pl.CostEstimate(flops=0, bytes_accessed=0, transcendentals=0),
        name=name,
    )(*args)


def whole(shape):
    return pl.BlockSpec(shape, lambda i, c: (0,) * len(shape))


def edge_block(rows, block=BLOCK):
    return pl.BlockSpec((rows, block), lambda i, c: (0, i))


def live(scal, block=BLOCK):
    return pl.program_id(0) * block < scal[0]


def span(scal, which, block):
    each = block // FINE
    at = 3 + which
    first, last = None, None
    for k in range(each):
        cell = at + 4 * (pl.program_id(0) * each + k)
        low, high = scal[cell], scal[cell + 1]
        first = low if first is None else jnp.minimum(first, low)
        last = high if last is None else jnp.maximum(last, high)
    return first, last


def meets(spanned, base, rows):
    return (spanned[0] < base + rows) & (spanned[1] >= base)


def table_rows(idx, pieces):
    total = None
    for base, piece in pieces:
        y = mm(piece, one_hot(idx, base, piece.shape[1]))
        total = y if total is None else total + y
    return total


def over_windows(scal, rows, idx_ref, visit):
    cells = []
    for k in range(WIDE // FINE):
        at = 3 + 4 * (pl.program_id(0) * (WIDE // FINE) + k)
        low, high = scal[at], scal[at + 1]
        base = jnp.minimum(low // LANES * LANES, rows - WINDOW)
        cells.append((slice(k * FINE, (k + 1) * FINE), base, high))

    def one(lanes, base, w):
        low = base + w * WINDOW
        first = pl.multiple_of(jnp.minimum(low, rows - WINDOW), LANES)
        idx = idx_ref[:, lanes]
        idx = jnp.where(idx >= low, idx - first, -1)
        visit(lanes, pl.ds(first, WINDOW), one_hot(idx, 0, WINDOW))

    for lanes, base, _ in cells:
        one(lanes, base, 0)
    for lanes, base, high in cells:

        @pl.when(high >= base + WINDOW)
        def _():
            turns = (high - base) // WINDOW + 1
            lax.fori_loop(1, turns, lambda w, _: one(lanes, base, w), None)


def gather_kernel(scal, idx_ref, table_ref, out_ref, acc):
    @pl.when(live(scal, WIDE))
    def _():
        acc[...] = jnp.zeros_like(acc)

        def visit(lanes, rows, hot):
            acc[:, lanes] += mm(table_ref[:, rows], hot)

        over_windows(scal, table_ref.shape[1], idx_ref, visit)
        out_ref[...] = acc[...].astype(out_ref.dtype)


def negatives_kernel(scal, idx_ref, table_ref, out_ref):
    rows, chunk = table_ref.shape[1], 1024
    pieces = [(b, table_ref[:, b : b + chunk]) for b in range(0, rows, chunk)]
    out_ref[...] = table_rows(idx_ref[...], pieces).astype(out_ref.dtype)


def relation_gather_kernel(scal, idx_ref, table_ref, out_ref):
    @pl.when(live(scal))
    def _():
        both = table_rows(idx_ref[...], [(0, table_ref[...])])
        half = both.shape[0] // 2
        out_ref[...] = both[:half] + both[half:]


def valid_lanes(scal):
    lane = lax.broadcasted_iota(I32, (1, BLOCK), 1) + pl.program_id(0) * BLOCK
    return jnp.where(lane < scal[0], 1.0, 0.0)


def negative_scores_kernel(scal, s_ref, r_ref, neg_t_ref, half_neg_ref, gu_ref, gn_ref, acc):
    i = pl.program_id(0)

    @pl.when(i == 0)
    def _():
        acc[...] = jnp.zeros_like(acc)

    @pl.when(live(scal))
    def _():
        ub = (s_ref[...].astype(F32) * r_ref[...]).astype(BF16)
        half = mm(half_neg_ref[...], ub)
        weight = valid_lanes(scal) * (0.5 / half.shape[0])
        gneg = (jnp.tanh(half) * weight + weight).astype(BF16)
        gu_ref[...] = mm(neg_t_ref[...], gneg)
        acc[...] += mm_nt(ub, gneg)

    @pl.when(i == pl.num_programs(0) - 1)
    def _():
        gn_ref[...] = acc[...].astype(BF16)


def target_kernel(order, rows, scal, s_ref, r_ref, gun_ref, idx_ref, *refs):
    gn_ref, n_idx_ref, tables = refs[0], refs[1], refs[2 : 2 + len(order)]
    gs_ref, gr_ref, keep_ref, send_ref, t_acc, gt_scr, acc = refs[2 + len(order) :]
    i = pl.program_id(0)
    parts = 2 * acc.shape[0]
    sums = [(keep_ref, acc)[apart % 2].at[apart // 2] for apart in range(parts)]
    bases = [(scal[1] ^ apart) * rows for apart in range(parts)]

    @pl.when(i == 0)
    def _():
        for total, base in zip(sums, bases, strict=True):
            total[...] = mm_nt(gn_ref[...], one_hot(n_idx_ref[...], base, rows))

    @pl.when(live(scal))
    def _():
        spanned = span(scal, 2, BLOCK)
        t_acc[...] = jnp.zeros_like(t_acc)
        for apart, base in enumerate(bases):

            @pl.when(meets(spanned, base, rows))
            def _():
                pieces = [
                    (base + first, table[...])
                    for (k, first), table in zip(order, tables, strict=True)
                    if k == apart
                ]
                t_acc[...] += table_rows(idx_ref[...], pieces)

        t = t_acc[...]
        s = s_ref[...].astype(F32)
        r = r_ref[...]
        u = s * r
        pos = jnp.sum(u * t, axis=0, keepdims=True)
        gpos = -jax.nn.sigmoid(-pos) * valid_lanes(scal)
        gu = gpos * t + gun_ref[...]
        gs_ref[...] = (gu * r).astype(BF16)
        gr_ref[...] = (gu * s).astype(BF16)
        gt_scr[...] = (gpos * u).astype(BF16)
        for total, base in zip(sums, bases, strict=True):

            @pl.when(meets(spanned, base, rows))
            def _():
                total[...] += mm_nt(gt_scr[...], one_hot(idx_ref[...], base, rows))

    @pl.when(jnp.logical_not(live(scal)))
    def _():
        gs_ref[...] = jnp.zeros_like(gs_ref)
        gr_ref[...] = jnp.zeros_like(gr_ref)

    @pl.when(i == pl.num_programs(0) - 1)
    def _():
        send_ref[...] = acc[...].astype(BF16)


def relation_scatter_kernel(scal, g_ref, idx_ref, keep_ref, send_ref, acc):
    i = pl.program_id(0)

    @pl.when(i == 0)
    def _():
        acc[...] = jnp.zeros_like(acc)

    @pl.when(live(scal, WIDE))
    def _():
        acc[...] += mm_nt(g_ref[...], one_hot(idx_ref[...], 0, acc.shape[1]))

    def copy(core):
        for part, cell, slot, rows, cols in tiles((2, *keep_ref.shape), acc.shape):
            to = (keep_ref, send_ref)[part ^ core]
            at = (cell ^ (scal[2] & 15), pl.ds(slot * SUBLANES, SUBLANES))
            if rows is None:
                to[at] = jnp.zeros((SUBLANES, LANES), F32)
            else:
                to[at] = acc[rows, cols]

    for core in range(2):

        @pl.when((i == pl.num_programs(0) - 1) & (scal[1] & 1 == core))
        def _():
            copy(core)


def tiles(packed, flat):
    parts, cells, rows, _ = packed
    slots = rows // SUBLANES
    wide = flat[1] // parts // LANES
    for part in range(parts):
        for tile in range(cells * slots):
            cell, slot = divmod(tile, slots)
            row, col = divmod(tile, wide)
            if row * SUBLANES >= flat[0]:
                yield part, cell, slot, None, None
            else:
                row, col = row * SUBLANES, (part * wide + col) * LANES
                yield part, cell, slot, slice(row, row + SUBLANES), slice(col, col + LANES)


def scatter_kernel(scal, g_ref, idx_ref, keep_ref, send_ref, acc):
    i = pl.program_id(0)

    @pl.when(i == 0)
    def _():
        acc[...] = jnp.zeros_like(acc)

    @pl.when(live(scal, WIDE))
    def _():
        def visit(lanes, rows, hot):
            acc[:, rows] += mm_nt(g_ref[:, lanes], hot)

        over_windows(scal, acc.shape[1], idx_ref, visit)

    @pl.when(i == pl.num_programs(0) - 1)
    def _():
        rows = keep_ref.shape[2]
        for apart in range(acc.shape[1] // rows):
            part = acc[:, pl.ds(pl.multiple_of((scal[1] ^ apart) * rows, rows), rows)]
            to = (keep_ref, send_ref)[apart % 2]
            to[apart // 2] = part.astype(to.dtype)


def relation_update_kernel(scal, rel_ref, state_ref, near_ref, core_ref, *refs):
    new_rel_ref, new_state_ref, flat = refs
    parts, cells, rows, _ = flat.shape
    for k, g_ref in enumerate((near_ref, core_ref)):
        for cell in range(cells):
            away = cell ^ (scal[2] & 15)
            flat[(scal[1] & 1) ^ k, cell] = g_ref[away & 3, away >> 2].astype(F32)
    width, count = rel_ref.shape
    wide = -(-count // (parts * LANES)) * parts * LANES
    pieces = {}
    for part, cell, slot, trows, tcols in tiles(flat.shape, (width, wide)):
        if trows is not None:
            pieces[trows.start, tcols.start] = (part, cell, pl.ds(slot * SUBLANES, SUBLANES))
    for col in range(0, count, LANES):
        n = min(LANES, count - col)
        square = jnp.zeros((SUBLANES, LANES), F32)
        for row in range(0, width, SUBLANES):
            g = flat[pieces[row, col]]
            square = square + g * g
        mean = jnp.sum(square, axis=0, keepdims=True) * (1.0 / width)
        state = state_ref[:, col : col + n] + mean[:, :n]
        new_state_ref[:, col : col + n] = state
        scale = RATE / jnp.sqrt(state)
        for row in range(0, width, SUBLANES):
            at = (slice(row, row + SUBLANES), slice(col, col + n))
            new_rel_ref[at] = rel_ref[at] - flat[pieces[row, col]][:, :n] * scale


def after(x, *others):
    return lax.optimization_barrier((x, *others))[0]


def summed(x, axis, step):
    got = [swapped(x[k], axis, k * step).astype(F32) for k in (1, 2, 3)]
    return (x[0] + got[0]) + (got[1] + got[2])


def collected(x, axis, step):
    return jnp.stack([x] + [swapped(x, axis, k * step) for k in (1, 2, 3)])


def body(
    entity_slab,
    entity_state,
    relation_diag,
    relation_state,
    edge_source,
    edge_target,
    edge_relation,
    edge_count,
    negatives,
):
    slab = entity_slab.T
    relations = relation_diag.T
    width, rows_part = slab.shape
    reps = lax.axis_size("rep")
    half = lax.axis_size("dom") // 2
    quarter = rows_part // reps
    rep, dom = lax.axis_index("rep"), lax.axis_index("dom")
    edges, n_neg, n_rel = edge_source.shape[0], negatives.shape[0], relation_diag.shape[0]
    f32_of = lambda *shape: jax.ShapeDtypeStruct(shape, F32)
    bf16_of = lambda *shape: jax.ShapeDtypeStruct(shape, BF16)

    asked = swapped(negatives, "dom", half).reshape(1, n_neg)
    own = lax.dynamic_slice_in_dim(slab, rep * quarter, quarter, 1)
    step = quarter // PIECES
    own_pieces = [own[:, k * step : (k + 1) * step] for k in range(PIECES)]

    lane = jnp.arange(edges, dtype=I32)
    is_live = lane < edge_count[0]
    group = edge_target // quarter
    along = jnp.where(group % 2 == 0, edge_source, rows_part - 1 - edge_source)
    key = jnp.where(is_live, group * rows_part + along, reps * rows_part)
    _, src, dst, rel = lax.sort((key, edge_source, edge_target, edge_relation), num_keys=1)
    spans = []
    for idx in (src, dst):
        by_cell = idx.reshape(-1, FINE)
        cell_live = is_live.reshape(-1, FINE)
        spans.append(jnp.min(jnp.where(cell_live, by_cell, rows_part), axis=1))
        spans.append(jnp.max(jnp.where(cell_live, by_cell, -1), axis=1))
    fixed = jnp.stack([edge_count[0], rep.astype(I32), dom.astype(I32)])
    scal = jnp.concatenate([fixed, jnp.stack(spans, axis=1).reshape(-1)])
    src, dst, rel = (x.reshape(1, edges) for x in (src, dst, rel))

    quarter_neg = n_neg // reps
    found = call(
        negatives_kernel,
        "partner_negatives",
        1,
        [whole((1, quarter_neg)), whole(slab.shape)],
        whole((width, quarter_neg)),
        bf16_of(width, quarter_neg),
        [],
        fixed,
        lax.dynamic_slice_in_dim(asked, rep * quarter_neg, quarter_neg, 1),
        slab,
    )
    neg_far = swapped_far(found, half, 2)
    own_pieces[1:] = [after(x, found) for x in own_pieces[1:]]
    far = [swapped_far(x, half, 2) for x in own_pieces]
    s_rows = call(
        gather_kernel,
        "source_rows",
        edges // WIDE,
        [edge_block(1, WIDE), whole(slab.shape)],
        edge_block(width, WIDE),
        bf16_of(width, edges),
        [pltpu.VMEM((width, WIDE), F32)],
        scal,
        after(src, found),
        slab,
    )
    wide = -(-n_rel // (2 * LANES)) * 2 * LANES
    padded = jnp.pad(relations, ((0, 0), (0, wide - n_rel)))
    high = padded.astype(BF16)
    low = (padded - high.astype(F32)).astype(BF16)
    split = jnp.concatenate([high, low], axis=0)
    split = after(split, s_rows)
    r_rows = call(
        relation_gather_kernel,
        "relation_rows",
        edges // BLOCK,
        [edge_block(1), whole(split.shape)],
        edge_block(width),
        f32_of(width, edges),
        [],
        scal,
        rel,
        split,
    )
    neg_far = after(neg_far, split)
    neg_near = swapped(neg_far, "rep", 2)
    neg_far_core = swapped(neg_far, "rep", 1)
    neg_near = after(neg_near, r_rows)
    neg_near_core = swapped(neg_near, "rep", 1)
    neg_t = jnp.concatenate([neg_far, neg_near, neg_far_core, neg_near_core], axis=1)
    apart_by = (2, 0, 3, 1)
    neg_idx = jnp.concatenate(
        [
            lax.dynamic_slice_in_dim(negatives, (rep ^ k) * quarter_neg, quarter_neg, 0)
            for k in apart_by
        ]
    ).reshape(1, n_neg)
    half_neg = 0.5 * neg_t.T
    far = [after(x, r_rows) for x in far]
    near = [swapped(x, "rep", 2) for x in far]
    far_core = [swapped(x, "rep", 1) for x in far]
    gu_neg, grad_n = call(
        negative_scores_kernel,
        "negative_scores",
        edges // BLOCK,
        [edge_block(width), edge_block(width), whole((width, n_neg)), whole((n_neg, width))],
        [edge_block(width), whole((width, n_neg))],
        [f32_of(width, edges), bf16_of(width, n_neg)],
        [pltpu.VMEM((width, n_neg), F32)],
        scal,
        s_rows,
        r_rows,
        after(neg_t, *far),
        half_neg,
    )
    near = [after(x, gu_neg) for x in near]
    near_core = [swapped(x, "rep", 1) for x in near]
    tables = [*far, *near, *far_core, *near_core]
    order = tuple((k, piece * step) for k in apart_by for piece in range(PIECES))

    cells = 16
    slots = -(-(width // SUBLANES * wide // 2 // LANES) // cells)
    packed = (2, cells, slots * SUBLANES, LANES)
    half_parts = (reps // 2, width, quarter)
    grad_s, grad_r, dst_keep, dst_send = call(
        functools.partial(target_kernel, order, quarter),
        "targets",
        edges // BLOCK,
        [edge_block(width)] * 3
        + [edge_block(1)]
        + [whole((width, n_neg)), whole((1, n_neg))]
        + [whole(t.shape) for t in tables],
        [edge_block(width)] * 2 + [whole(half_parts)] * 2,
        [bf16_of(width, edges)] * 2 + [f32_of(*half_parts), bf16_of(*half_parts)],
        [
            pltpu.VMEM((width, BLOCK), F32),
            pltpu.VMEM((width, BLOCK), BF16),
            pltpu.VMEM(half_parts, F32),
        ],
        scal,
        s_rows,
        r_rows,
        gu_neg,
        dst,
        grad_n,
        neg_idx,
        *tables,
    )
    dst_sum = dst_keep + swapped(dst_send, "rep", 1).astype(F32)
    rel_keep, rel_send = call(
        relation_scatter_kernel,
        "relation_grads",
        edges // WIDE,
        [edge_block(width, WIDE), edge_block(1, WIDE)],
        [whole(packed[1:])] * 2,
        [f32_of(*packed[1:])] * 2,
        [pltpu.VMEM((width, wide), F32)],
        scal,
        after(grad_r, dst_sum),
        rel,
    )
    sent = [
        swapped(dst_sum[0, :, k * step : (k + 1) * step].astype(BF16), "rep", 2)
        for k in range(PIECES)
    ]
    sent = jnp.concatenate([after(x, rel_keep) for x in sent], axis=1)
    mine = (dst_sum[1] + sent.astype(F32)).astype(BF16)
    small = quarter // RETURNS
    returned = [
        swapped_far(mine[:, k * small : (k + 1) * small], half, 2) for k in range(RETURNS)
    ]
    src_keep, src_send = call(
        scatter_kernel,
        "source_grads",
        edges // WIDE,
        [edge_block(width, WIDE), edge_block(1, WIDE)],
        [whole(half_parts)] * 2,
        [f32_of(*half_parts), bf16_of(*half_parts)],
        [pltpu.VMEM((width, rows_part), F32)],
        scal,
        after(grad_s, mine),
        src,
    )

    grid = rel_keep + after(swapped(rel_send, "rep", 1), src_keep, *returned[: RETURNS // 2])
    grid = grid.reshape(4, 4, *packed[2:]).swapaxes(0, 1)
    line = summed([grid[0], *(grid[k].astype(BF16) for k in (1, 2, 3))], "dom", 1)
    cell = summed(line, "dom", 4)
    cell = after(cell, *returned[RETURNS // 2 :])
    cell = cell + swapped(cell, "rep", 2)
    total = summed([cell] * 4, "dom", 16).astype(BF16)
    src_sum = src_keep + swapped(src_send, "rep", 1).astype(F32)
    src_got = swapped(after(src_sum[1], total).astype(BF16), "rep", 2)
    line = collected(total, "dom", 4)
    grid = after(collected(line, "dom", 1), src_got)
    grid_core = swapped(grid, "rep", 1)

    kept = src_sum[0] + src_got.astype(F32)
    grads = kept + jnp.concatenate(returned, axis=1).astype(F32)

    new_state = entity_state + jnp.mean(grads * grads, axis=0)
    new_slab = (own.astype(F32) - RATE * grads / jnp.sqrt(new_state)[None, :]).astype(BF16)
    new_relation, new_relation_state = call(
        relation_update_kernel,
        "relation_update",
        1,
        [whole((width, n_rel)), whole((1, n_rel))] + [whole(grid.shape)] * 2,
        [whole((width, n_rel)), whole((1, n_rel))],
        [f32_of(width, n_rel), f32_of(1, n_rel)],
        [pltpu.VMEM(packed, F32)],
        fixed,
        relations,
        relation_state.reshape(1, n_rel),
        grid,
        grid_core,
    )
    return (new_slab.T, new_state, new_relation.T, new_relation_state.reshape(n_rel))


def solution(mesh):
    in_specs = (
        P("dom", None),
        P(("dom", "rep")),
        P(),
        P(),
        P(("dom", "rep")),
        P(("dom", "rep")),
        P(("dom", "rep")),
        P(("dom", "rep")),
        P("dom"),
    )
    out_specs = (P(("dom", "rep"), None), P(("dom", "rep")), P(), P())
    return jax.shard_map(body, mesh=mesh, in_specs=in_specs, out_specs=out_specs, check_vma=False)
```

time: 1240 us -> 260 us (0.21)
  waiting for transfers between devices: 920 us -> 43 us
  local copies, waits for them, and re-layouts: 134 us -> 7.88 us
  other arithmetic: 127 us -> 20 us
  Pallas kernels: 0 us -> 88.4 us
  starting transfers between devices: 7.91 us -> 94.9 us
  matrix products: 25.9 us -> 0 us
  between operations: 16.2 us -> 1.94 us
    psum x1 -> x0, waiting for transfers between devices: 756 us -> none  [body(): rel_total = lax.psum(rel_grad, ('dom', 'rep'))]
    ppermute x2 -> x38, waiting for transfers between devices: 164 us -> 43 us  [the longest x33 39.7 us: swapped(): lax.ppermute(x, axis, [(i, i ^ mask) for i in range(lax.axis_size(axis))])]
    scatter-add x10 -> x0, other arithmetic: 94.2 us -> none  [the longest x3 32.4 us: one_block(): grad_src.at[s_idx].add(grad_s)]
    pallas_call x0 -> x8, Pallas kernels: none -> 88.4 us  [call(): pl.pallas_call(kernel, grid_spec=pltpu.PrefetchScalarGridSpec(num_scalar_...]
    ppermute x2 -> x38, starting transfers between devices: 7.83 us -> 94.9 us  [the longest x33 89.2 us: swapped(): lax.ppermute(x, axis, [(i, i ^ mask) for i in range(lax.axis_size(axis))])]
    gather x19 -> x0, local copies, waits for them, and re-layouts: 65.5 us -> none  [the longest x6 20.9 us: one_block(): relation_diag[r_idx]]
    dot_general x9 -> x0, matrix products: 25.9 us -> none  [the longest x3 11.3 us: score_edges(): lax.dot_general(gneg, lifted_b, (((0,), (0,)), ((), ())), preferred_eleme...]
    mul x9 -> x0, local copies, waits for them, and re-layouts: 22 us -> none  [the longest x6 14.7 us: score_edges(): return (grad_u * r_rows, grad_t, grad_u * source, grad_n)]
  transfers between devices with their start and end apart: 4 -> 38, of which waited for: 3 -> 16; matrix products, arithmetic and copies ran while one was open for 3% -> 8% of each run, Pallas kernels for 0% -> 23%
where the time goes in v2:
time: 260 us; the launch traced here: 256 us
  starting transfers between devices  94.9 us (36%)
  Pallas kernels  88.4 us (34%)
  waiting for transfers between devices  43 us (17%)
  other arithmetic  20 us (8%)
  local copies, waits for them, and re-layouts  7.88 us (3%)
    ppermute x33, starting transfers between devices, swapped(): lax.ppermute(x, axis, [(i, i ^ mask) for i in range(lax.axis_size(axis))])  89.2 us
    pallas_call x8, Pallas kernels, call(): pl.pallas_call(kernel, grid_spec=pltpu.PrefetchScalarGridSpec(num_scalar_...  88.4 us
    ppermute x33, waiting for transfers between devices, swapped(): lax.ppermute(x, axis, [(i, i ^ mask) for i in range(lax.axis_size(axis))])  39.7 us
    sort x1, other arithmetic, body(): lax.sort((key, edge_source, edge_target, edge_relation), num_keys=1)  6 us
    ppermute x5, starting transfers between devices, swapped_far(): return lax.ppermute(x, ('dom', 'rep'), pairs)  5.71 us
  transfers between devices with their start and end apart: 38, of which 16 were waited for; matrix products, arithmetic and copies ran while one was open for 8% of the time, Pallas kernels for 23%

profile of v2, /device:TPU:1, one launch (start us, length us, event | category | flops | bytes accessed | tf_op | source)
XLA Modules:
  0.0 256.1 jit_solution(11664331426458534000)
XLA Ops:
  0.6 7.8 %collective-permute-start = (s32[1024]{0:T(1024)}, s32[1024]{0:T(1024)S(1)}, u32[]{:S(2)}, u32[]{:S(2)}) collective-permute-start(s32[1024]{0:T(1024)} %param.17), channel_id=1, source_target_pairs={{0,128},{4,132},{8,136},{12,140},{16,144},{20,148},{24,152},{28,15... | collective-permute-start | bytes 12296 | tf_op jit(solution)/shard_map/ppermute | solution.py:24
  8.5 1.3 dynamic-slice_bitcast_fusion
  11.4 6.0 %sort.39 = (s32[4096]{0:T(1024)}, s32[4096]{0:T(1024)S(1)}, s32[4096]{0:T(1024)S(1)}, s32[4096]{0:T(1024)}, s32[4096]{0:T(1024)}) sort(s32[4096]{0:T(1024)S(1)} %fusion.13, s32[4096]{0:T(1024)S(1)} %copy-done.13, s32[4096]{0:T(1024)S(1)} %copy-done.14, s32[4096]{0:T(1024)S(1)} %copy-done.16, s32[4096]{0:T(1024)S(1)} %iota.25), dimensions={0}, to_apply=%region_0.1 | sort | flops 49152 | bytes 163840 | tf_op jit(solution)/shard_map/sort | solution.py:372
  17.4 1.7 pad_maximum_fusion.table_ref
  20.5 4.3 %partner_negatives.1 = bf16[400,256]{1,0:T(8,128)(2,1)} custom-call(s32[3]{0:T(128)} %pad_add_fusion.3.scal, s32[1,256]{1,0:T(1,128)} %bitcast.109, bf16[400,4096]{1,0:T(8,128)(2,1)} %bitcast.87), custom_call_target="tpu_custom_call" | custom-call | tf_op jit(solution)/shard_map/partner_negatives/pallas_call | solution.py:51
  25.9 4.2 %collective-permute-start.1 = (bf16[400,256]{0,1:T(8,128)(2,1)S(1)}, bf16[400,256]{0,1:T(8,128)(2,1)S(1)}, u32[]{:S(2)}, u32[]{:S(2)}) collective-permute-start(bf16[400,256]{0,1:T(8,128)(2,1)S(1)} %copy.21), channel_id=1, source_target_pairs={{0,130},{1,131},{2,128},{3,129},{4,134},{5,135},{6,132},{7,133},{8... | collective-permute-start | bytes 614408 | tf_op jit(solution)/shard_map/ppermute | solution.py:34
  31.3 11.0 %source_rows.1.s_ref = bf16[400,4096]{1,0:T(8,128)(2,1)} custom-call(s32[67]{0:T(128)} %pad_add_fusion.2.scal, s32[1,4096]{1,0:T(1,128)} %bitcast.100, bf16[400,4096]{1,0:T(8,128)(2,1)} %bitcast.88), custom_call_target="tpu_custom_call" | custom-call | tf_op jit(solution)/shard_map/source_rows/pallas_call | solution.py:51
  43.3 10.3 %relation_rows.1.r_ref = f32[400,4096]{1,0:T(8,128)} custom-call(s32[67]{0:T(128)} %pad_add_fusion.2.scal, s32[1,4096]{1,0:T(1,128)} %bitcast.102, bf16[800,1536]{1,0:T(8,128)(2,1)} %pad_maximum_fusion.table_ref), custom_call_target="tpu_custom_call" | custom-call | tf_op jit(solution)/shard_map/relation_rows/pallas_call | solution.py:51
  53.5 9.6 %collective-permute-start.3 = (bf16[400,256]{0,1:T(8,128)(2,1)S(1)}, bf16[400,256]{0,1:T(8,128)(2,1)S(1)}, u32[]{:S(2)}, u32[]{:S(2)}) collective-permute-start(bf16[400,256]{0,1:T(8,128)(2,1)S(1)} %collective-permute-done.1), channel_id=1, source_target_pairs={{0,1},{1,0},{2,3},{3,2},{4,5},{5,4},{6,7},{7,6},{8,9},{9,8},{10,11... | collective-permute-start | bytes 614408 | tf_op jit(solution)/shard_map/ppermute | solution.py:24
  63.2 12.5 %collective-permute-start.7 = (bf16[400,512]{1,0:T(8,128)(2,1)}, bf16[400,512]{1,0:T(8,128)(2,1)S(1)}, u32[]{:S(2)}, u32[]{:S(2)}) collective-permute-start(bf16[400,512]{1,0:T(8,128)(2,1)} %collective-permute-done.5.refs_2_), channel_id=1, source_target_pairs={{0,2},{1,3},{2,0},{3,1},{4,6},{5,7},{6,4},{7,5},{8,10},{9,11},{10,... | collective-permute-start | bytes 1228808 | tf_op jit(solution)/shard_map/ppermute | solution.py:24
  76.3 1.4 collective-permute-start.8
  78.4 1.2 copy.22.neg_t_ref
  80.7 13.4 %negative_scores.1 = (f32[400,4096]{1,0:T(8,128)}, bf16[400,1024]{1,0:T(8,128)(2,1)}) custom-call(s32[67]{0:T(128)} %pad_add_fusion.2.scal, bf16[400,4096]{1,0:T(8,128)(2,1)} %source_rows.1.s_ref, f32[400,4096]{1,0:T(8,128)} %relation_rows.1.r_ref, bf16[400,1024]{1,0:T(8,128)(2,1)} %copy.22.neg_t_ref, bf16[1024,400]{1,0:T(8,128)(2,1)} %multiply_bitcast_fusion.half_neg_ref), custom_call_target="tpu_custom_call" | custom-call | tf_op jit(solution)/shard_map/negative_scores/pallas_call | solution.py:51
  94.1 3.0 %collective-permute-start.11 = (bf16[400,512]{1,0:T(8,128)(2,1)S(1)}, bf16[400,512]{1,0:T(8,128)(2,1)S(1)}, u32[]{:S(2)}, u32[]{:S(2)}) collective-permute-start(bf16[400,512]{1,0:T(8,128)(2,1)S(1)} %collective-permute-done.7.refs_4_), channel_id=1, source_target_pairs={{0,1},{1,0},{2,3},{3,2},{4,5},{5,4},{6,7},{7,6},{8,9},{9,8},{10,11... | collective-permute-start | bytes 1228808 | tf_op jit(solution)/shard_map/ppermute | solution.py:24
  99.8 24.2 %targets.1 = (bf16[400,4096]{1,0:T(8,128)(2,1)}, bf16[400,4096]{1,0:T(8,128)(2,1)}, f32[2,400,1024]{2,1,0:T(8,128)}, bf16[2,400,1024]{2,1,0:T(8,128)(2,1)}) custom-call(s32[67]{0:T(128)} %pad_add_fusion.2.scal, bf16[400,4096]{1,0:T(8,128)(2,1)} %source_rows.1.s_ref, f32[400,4096]{1,0:T(8,128)} %relation_rows.1.r_ref, f32[400,4096]{1,0:T(8,128)} %get-tuple-element.52.gun_ref, ...), custom_call_target="tpu_custom_call" | custom-call | tf_op jit(solution)/shard_map/targets/pallas_call | solution.py:51
  124.0 2.9 %collective-permute-start.13 = (bf16[2,400,1024]{2,1,0:T(8,128)(2,1)}, bf16[2,400,1024]{2,1,0:T(8,128)(2,1)S(1)}, u32[]{:S(2)}, u32[]{:S(2)}) collective-permute-start(bf16[2,400,1024]{2,1,0:T(8,128)(2,1)} %get-tuple-element.58), channel_id=1, source_target_pairs={{0,1},{1,0},{2,3},{3,2},{4,5},{5,4},{6,7},{7,6},{8,9},{9,8},{10,11... | collective-permute-start | bytes 4915208 | tf_op jit(solution)/shard_map/ppermute | solution.py:24
  126.9 3.3 %collective-permute-done.13 = bf16[2,400,1024]{2,1,0:T(8,128)(2,1)S(1)} collective-permute-done((bf16[2,400,1024]{2,1,0:T(8,128)(2,1)}, bf16[2,400,1024]{2,1,0:T(8,128)(2,1)S(1)}, u32[]{:S(2)}, u32[]{:S(2)}) %collective-permute-start.13) | collective-permute-done | bytes 1638432 | tf_op jit(solution)/shard_map/ppermute | solution.py:24
  130.3 2.8 %fusion.19 = (bf16[2,400,1024]{2,1,0:T(8,128)(2,1)S(1)}, f32[2,400,1024]{2,1,0:T(8,128)S(1)}) fusion(f32[2,400,1024]{2,1,0:T(8,128)} %get-tuple-element.57, bf16[2,400,1024]{2,1,0:T(8,128)(2,1)S(1)} %collective-permute-done.13), kind=kLoop, calls=%fused_computation.69 | loop fusion | flops 2457600 | bytes 9830400 | tf_op jit(solution)/shard_map/convert.4
  133.3 1.5 collective-permute-start.15
  134.7 7.8 %relation_grads.1 = (f32[16,152,128]{2,1,0:T(8,128)}, f32[16,152,128]{2,1,0:T(8,128)}) custom-call(s32[67]{0:T(128)} %pad_add_fusion.2.scal, bf16[400,4096]{1,0:T(8,128)(2,1)} %get-tuple-element.60.g_ref, s32[1,4096]{1,0:T(1,128)} %bitcast.103), custom_call_target="tpu_custom_call" | custom-call | tf_op jit(solution)/shard_map/relation_grads/pallas_call | solution.py:51
  142.5 3.2 %collective-permute-start.17 = (f32[16,152,128]{2,1,0:T(8,128)}, f32[16,152,128]{2,1,0:T(8,128)S(1)}, u32[]{:S(2)}, u32[]{:S(2)}) collective-permute-start(f32[16,152,128]{2,1,0:T(8,128)} %get-tuple-element.67), channel_id=1, source_target_pairs={{0,1},{1,0},{2,3},{3,2},{4,5},{5,4},{6,7},{7,6},{8,9},{9,8},{10,11... | collective-permute-start | bytes 3735560 | tf_op jit(solution)/shard_map/ppermute | solution.py:24
  145.7 7.0 %collective-permute-done.15 = bf16[400,512]{1,0:T(8,128)(2,1)S(1)} collective-permute-done((bf16[400,512]{1,0:T(8,128)(2,1)S(1)}, bf16[400,512]{1,0:T(8,128)(2,1)S(1)}, u32[]{:S(2)}, u32[]{:S(2)}) %collective-permute-start.15) | collective-permute-done | bytes 409632 | tf_op jit(solution)/shard_map/ppermute | solution.py:24
  153.6 12.9 %source_grads.1 = (f32[2,400,1024]{2,1,0:T(8,128)}, bf16[2,400,1024]{2,1,0:T(8,128)(2,1)}) custom-call(s32[67]{0:T(128)} %pad_add_fusion.2.scal, bf16[400,4096]{1,0:T(8,128)(2,1)} %get-tuple-element.64.g_ref, s32[1,4096]{1,0:T(1,128)} %bitcast.101), custom_call_target="tpu_custom_call" | custom-call | tf_op jit(solution)/shard_map/source_grads/pallas_call | solution.py:51
  167.3 4.7 %collective-permute-start.19 = (bf16[4,152,128]{2,1,0:T(8,128)(2,1)S(1)}, bf16[4,152,128]{2,1,0:T(8,128)(2,1)S(1)}, u32[]{:S(2)}, u32[]{:S(2)}) collective-permute-start(bf16[4,152,128]{2,1,0:T(8,128)(2,1)S(1)} %get-tuple-element.88), channel_id=1, source_target_pairs={{0,4},{4,0},{8,12},{12,8},{16,20},{20,16},{24,28},{28,24},{32,36},... | collective-permute-start | bytes 466952 | tf_op jit(solution)/shard_map/ppermute | solution.py:24
  172.0 12.0 %collective-permute-start.20 = (bf16[4,152,128]{2,1,0:T(8,128)(2,1)S(1)}, bf16[4,152,128]{2,1,0:T(8,128)(2,1)S(1)}, u32[]{:S(2)}, u32[]{:S(2)}) collective-permute-start(bf16[4,152,128]{2,1,0:T(8,128)(2,1)S(1)} %get-tuple-element.90), channel_id=1, source_target_pairs={{0,8},{4,12},{8,0},{12,4},{16,24},{20,28},{24,16},{28,20},{32,40},... | collective-permute-start | bytes 466952 | tf_op jit(solution)/shard_map/ppermute | solution.py:24
  184.6 6.4 %collective-permute-done.20 = bf16[4,152,128]{2,1,0:T(8,128)(2,1)S(1)} collective-permute-done((bf16[4,152,128]{2,1,0:T(8,128)(2,1)S(1)}, bf16[4,152,128]{2,1,0:T(8,128)(2,1)S(1)}, u32[]{:S(2)}, u32[]{:S(2)}) %collective-permute-start.20) | collective-permute-done | bytes 155680 | tf_op jit(solution)/shard_map/ppermute | solution.py:24
  191.0 2.6 %collective-permute-done.21 = bf16[4,152,128]{2,1,0:T(8,128)(2,1)S(1)} collective-permute-done((bf16[4,152,128]{2,1,0:T(8,128)(2,1)S(1)}, bf16[4,152,128]{2,1,0:T(8,128)(2,1)S(1)}, u32[]{:S(2)}, u32[]{:S(2)}) %collective-permute-start.21) | collective-permute-done | bytes 155680 | tf_op jit(solution)/shard_map/ppermute | solution.py:24
  193.8 3.0 %collective-permute-start.23 = (f32[152,128]{1,0:T(8,128)S(1)}, f32[152,128]{1,0:T(8,128)S(1)}, u32[]{:S(2)}, u32[]{:S(2)}) collective-permute-start(f32[152,128]{1,0:T(8,128)S(1)} %get-tuple-element.92), channel_id=1, source_target_pairs={{0,32},{4,36},{8,40},{12,44},{16,48},{20,52},{24,56},{28,60},{32,0... | collective-permute-start | bytes 233480 | tf_op jit(solution)/shard_map/ppermute | solution.py:24
  197.7 2.0 collective-permute-done.23
  199.7 2.7 %collective-permute-done.24 = f32[152,128]{1,0:T(8,128)S(1)} collective-permute-done((f32[152,128]{1,0:T(8,128)S(1)}, f32[152,128]{1,0:T(8,128)S(1)}, u32[]{:S(2)}, u32[]{:S(2)}) %collective-permute-start.24) | collective-permute-done | bytes 77856 | tf_op jit(solution)/shard_map/ppermute | solution.py:24
  202.4 3.2 %collective-permute-done.25 = bf16[400,512]{1,0:T(8,128)(2,1)S(1)} collective-permute-done((bf16[400,512]{1,0:T(8,128)(2,1)S(1)}, bf16[400,512]{1,0:T(8,128)(2,1)S(1)}, u32[]{:S(2)}, u32[]{:S(2)}) %collective-permute-start.25) | collective-permute-done | bytes 409632 | tf_op jit(solution)/shard_map/ppermute | solution.py:34
  205.6 3.2 %collective-permute-done.26 = f32[152,128]{1,0:T(8,128)S(1)} collective-permute-done((f32[152,128]{1,0:T(8,128)S(1)}, f32[152,128]{1,0:T(8,128)S(1)}, u32[]{:S(2)}, u32[]{:S(2)}) %collective-permute-start.26) | collective-permute-done | bytes 77856 | tf_op jit(solution)/shard_map/ppermute | solution.py:24
  209.0 2.0 collective-permute-start.28
  211.0 3.8 %collective-permute-start.29 = (f32[152,128]{1,0:T(8,128)S(1)}, f32[152,128]{1,0:T(8,128)S(1)}, u32[]{:S(2)}, u32[]{:S(2)}) collective-permute-start(f32[152,128]{1,0:T(8,128)S(1)} %add.97), channel_id=1, source_target_pairs={{0,192},{4,196},{8,200},{12,204},{16,208},{20,212},{24,216},{28,22... | collective-permute-start | bytes 233480 | tf_op jit(solution)/shard_map/ppermute | solution.py:24
  214.8 2.9 %collective-permute-done.28 = f32[152,128]{1,0:T(8,128)S(1)} collective-permute-done((f32[152,128]{1,0:T(8,128)S(1)}, f32[152,128]{1,0:T(8,128)S(1)}, u32[]{:S(2)}, u32[]{:S(2)}) %collective-permute-start.28) | collective-permute-done | bytes 77856 | tf_op jit(solution)/shard_map/ppermute | solution.py:24
  219.0 2.3 collective-permute-start.30
  221.3 4.0 %collective-permute-start.31 = (bf16[152,128]{1,0:T(8,128)(2,1)S(1)}, bf16[152,128]{1,0:T(8,128)(2,1)S(1)}, u32[]{:S(2)}, u32[]{:S(2)}) collective-permute-start(bf16[152,128]{1,0:T(8,128)(2,1)S(1)} %add_convert_fusion), channel_id=1, source_target_pairs={{0,16},{4,20},{8,24},{12,28},{16,0},{20,4},{24,8},{28,12},{32,48},... | collective-permute-start | bytes 116744 | tf_op jit(solution)/shard_map/ppermute | solution.py:24
  225.3 3.3 %collective-permute-start.32 = (bf16[152,128]{1,0:T(8,128)(2,1)S(1)}, bf16[152,128]{1,0:T(8,128)(2,1)S(1)}, u32[]{:S(2)}, u32[]{:S(2)}) collective-permute-start(bf16[152,128]{1,0:T(8,128)(2,1)S(1)} %add_convert_fusion), channel_id=1, source_target_pairs={{0,32},{4,36},{8,40},{12,44},{16,48},{20,52},{24,56},{28,60},{32,0... | collective-permute-start | bytes 116744 | tf_op jit(solution)/shard_map/ppermute | solution.py:24
  228.6 1.8 collective-permute-done.32
  230.4 2.3 collective-permute-done.33
  233.0 2.3 collective-permute-start.35
  235.3 1.3 collective-permute-start.36
  237.2 2.7 %collective-permute-done.35 = bf16[4,152,128]{2,1,0:T(8,128)(2,1)S(1)} collective-permute-done((bf16[4,152,128]{2,1,0:T(8,128)(2,1)S(1)}, bf16[4,152,128]{2,1,0:T(8,128)(2,1)S(1)}, u32[]{:S(2)}, u32[]{:S(2)}) %collective-permute-start.35) | collective-permute-done | bytes 155680 | tf_op jit(solution)/shard_map/ppermute | solution.py:24
  239.9 1.3 collective-permute-done.36
  241.4 4.3 %collective-permute-start.37 = (bf16[4,4,152,128]{3,2,1,0:T(8,128)(2,1)S(1)}, bf16[4,4,152,128]{3,2,1,0:T(8,128)(2,1)S(1)}, u32[]{:S(2)}, u32[]{:S(2)}) collective-permute-start(bf16[4,4,152,128]{3,2,1,0:T(8,128)(2,1)S(1)} %pad_maximum_fusion.1.near_ref), channel_id=1, source_target_pairs={{0,1},{1,0},{2,3},{3,2},{4,5},{5,4},{6,7},{7,6},{8,9},{9,8},{10,11... | collective-permute-start | bytes 1867784 | tf_op jit(solution)/shard_map/ppermute | solution.py:24
  246.6 2.6 fusion.4
  250.1 4.6 %relation_update.1 = (f32[400,1345]{1,0:T(8,128)}, f32[1,1345]{1,0:T(1,128)}) custom-call(s32[3]{0:T(128)} %pad_add_fusion.3.scal, f32[400,1345]{1,0:T(8,128)} %bitcast.89, f32[1,1345]{1,0:T(1,128)} %reshape.57.state_ref, bf16[4,4,152,128]{3,2,1,0:T(8,128)(2,1)} %copy-done.2, bf16[4,4,152,128]{3,2,1,0:T(8,128)(2,1)} %copy-done.4), custom_call_target="tpu_custom_call" | custom-call | tf_op jit(solution)/shard_map/relation_update/pallas_call | solution.py:51
  254.6 1.3 reduce
  (124 shorter events, 18.2 us)
Async XLA Ops:
  0.6 19.3 %collective-permute-start = (s32[1024]{0:T(1024)}, s32[1024]{0:T(1024)S(1)}, u32[]{:S(2)}, u32[]{:S(2)}) collective-permute-start(s32[1024]{0:T(1024)} %param.17), channel_id=1, source_target_pairs={{0,128},{4,132},{8,136},{12,140},{16,144},{20,148},{24,152},{28,15... | collective-permute-start | bytes 12296 | tf_op jit(solution)/shard_map/ppermute | solution.py:24
  8.5 1.9 copy-start
  9.9 53.3 %collective-permute-start.5 = (bf16[400,512]{1,0:T(8,128)(2,1)S(1)}, bf16[400,512]{1,0:T(8,128)(2,1)}, u32[]{:S(2)}, u32[]{:S(2)}) collective-permute-start(bf16[400,512]{1,0:T(8,128)(2,1)S(1)} %get-tuple-element.87), channel_id=1, source_target_pairs={{0,130},{1,131},{2,128},{3,129},{4,134},{5,135},{6,132},{7,133},{8... | collective-permute-start | bytes 1228808 | tf_op jit(solution)/shard_map/ppermute | solution.py:34
  25.9 16.5 %collective-permute-start.1 = (bf16[400,256]{0,1:T(8,128)(2,1)S(1)}, bf16[400,256]{0,1:T(8,128)(2,1)S(1)}, u32[]{:S(2)}, u32[]{:S(2)}) collective-permute-start(bf16[400,256]{0,1:T(8,128)(2,1)S(1)} %copy.21), channel_id=1, source_target_pairs={{0,130},{1,131},{2,128},{3,129},{4,134},{5,135},{6,132},{7,133},{8... | collective-permute-start | bytes 614408 | tf_op jit(solution)/shard_map/ppermute | solution.py:34
  30.1 46.2 %collective-permute-start.6 = (bf16[400,512]{1,0:T(8,128)(2,1)S(1)}, bf16[400,512]{1,0:T(8,128)(2,1)S(1)}, u32[]{:S(2)}, u32[]{:S(2)}) collective-permute-start(bf16[400,512]{1,0:T(8,128)(2,1)S(1)} %get-tuple-element.49), channel_id=1, source_target_pairs={{0,130},{1,131},{2,128},{3,129},{4,134},{5,135},{6,132},{7,133},{8... | collective-permute-start | bytes 1228808 | tf_op jit(solution)/shard_map/ppermute | solution.py:34
  42.4 33.4 %collective-permute-start.2 = (bf16[400,256]{0,1:T(8,128)(2,1)S(1)}, bf16[400,256]{0,1:T(8,128)(2,1)S(1)}, u32[]{:S(2)}, u32[]{:S(2)}) collective-permute-start(bf16[400,256]{0,1:T(8,128)(2,1)S(1)} %collective-permute-done.1), channel_id=1, source_target_pairs={{0,2},{1,3},{2,0},{3,1},{4,6},{5,7},{6,4},{7,5},{8,10},{9,11},{10,... | collective-permute-start | bytes 614408 | tf_op jit(solution)/shard_map/ppermute | solution.py:24
  53.5 24.2 %collective-permute-start.3 = (bf16[400,256]{0,1:T(8,128)(2,1)S(1)}, bf16[400,256]{0,1:T(8,128)(2,1)S(1)}, u32[]{:S(2)}, u32[]{:S(2)}) collective-permute-start(bf16[400,256]{0,1:T(8,128)(2,1)S(1)} %collective-permute-done.1), channel_id=1, source_target_pairs={{0,1},{1,0},{2,3},{3,2},{4,5},{5,4},{6,7},{7,6},{8,9},{9,8},{10,11... | collective-permute-start | bytes 614408 | tf_op jit(solution)/shard_map/ppermute | solution.py:24
  63.2 30.9 %collective-permute-start.7 = (bf16[400,512]{1,0:T(8,128)(2,1)}, bf16[400,512]{1,0:T(8,128)(2,1)S(1)}, u32[]{:S(2)}, u32[]{:S(2)}) collective-permute-start(bf16[400,512]{1,0:T(8,128)(2,1)} %collective-permute-done.5.refs_2_), channel_id=1, source_target_pairs={{0,2},{1,3},{2,0},{3,1},{4,6},{5,7},{6,4},{7,5},{8,10},{9,11},{10,... | collective-permute-start | bytes 1228808 | tf_op jit(solution)/shard_map/ppermute | solution.py:24
  75.7 22.2 %collective-permute-start.9 = (bf16[400,512]{1,0:T(8,128)(2,1)}, bf16[400,512]{1,0:T(8,128)(2,1)S(1)}, u32[]{:S(2)}, u32[]{:S(2)}) collective-permute-start(bf16[400,512]{1,0:T(8,128)(2,1)} %collective-permute-done.5.refs_2_), channel_id=1, source_target_pairs={{0,1},{1,0},{2,3},{3,2},{4,5},{5,4},{6,7},{7,6},{8,9},{9,8},{10,11... | collective-permute-start | bytes 1228808 | tf_op jit(solution)/shard_map/ppermute | solution.py:24
  75.8 2.6 %collective-permute-start.4 = (bf16[400,256]{0,1:T(8,128)(2,1)S(1)}, bf16[400,256]{0,1:T(8,128)(2,1)S(1)}, u32[]{:S(2)}, u32[]{:S(2)}) collective-permute-start(bf16[400,256]{0,1:T(8,128)(2,1)S(1)} %collective-permute-done.2), channel_id=1, source_target_pairs={{0,1},{1,0},{2,3},{3,2},{4,5},{5,4},{6,7},{7,6},{8,9},{9,8},{10,11... | collective-permute-start | bytes 614408 | tf_op jit(solution)/shard_map/ppermute | solution.py:24
  76.3 3.3 %copy-start.5 = (bf16[400,512]{1,0:T(8,128)(2,1)}, bf16[400,512]{1,0:T(8,128)(2,1)S(1)}, u32[]{:S(2)}) copy-start(bf16[400,512]{1,0:T(8,128)(2,1)S(1)} %collective-permute-done.6.refs_3_) | copy-start | bytes 1228804
  76.3 20.8 %collective-permute-start.8 = (bf16[400,512]{1,0:T(8,128)(2,1)S(1)}, bf16[400,512]{1,0:T(8,128)(2,1)S(1)}, u32[]{:S(2)}, u32[]{:S(2)}) collective-permute-start(bf16[400,512]{1,0:T(8,128)(2,1)S(1)} %collective-permute-done.6.refs_3_), channel_id=1, source_target_pairs={{0,2},{1,3},{2,0},{3,1},{4,6},{5,7},{6,4},{7,5},{8,10},{9,11},{10,... | collective-permute-start | bytes 1228808 | tf_op jit(solution)/shard_map/ppermute | solution.py:24
  77.7 20.2 %collective-permute-start.10 = (bf16[400,512]{1,0:T(8,128)(2,1)S(1)}, bf16[400,512]{1,0:T(8,128)(2,1)S(1)}, u32[]{:S(2)}, u32[]{:S(2)}) collective-permute-start(bf16[400,512]{1,0:T(8,128)(2,1)S(1)} %collective-permute-done.6.refs_3_), channel_id=1, source_target_pairs={{0,1},{1,0},{2,3},{3,2},{4,5},{5,4},{6,7},{7,6},{8,9},{9,8},{10,11... | collective-permute-start | bytes 1228808 | tf_op jit(solution)/shard_map/ppermute | solution.py:24
  80.7 16.5 %copy-start.18 = (s32[1024]{0:T(1024)S(1)}, s32[1024]{0:T(1024)}, u32[]{:S(2)}) copy-start(s32[1024]{0:T(1024)} %param.17) | copy-start | bytes 12292
  94.1 4.9 %copy-start.6 = (bf16[400,512]{1,0:T(8,128)(2,1)}, bf16[400,512]{1,0:T(8,128)(2,1)S(1)}, u32[]{:S(2)}) copy-start(bf16[400,512]{1,0:T(8,128)(2,1)S(1)} %collective-permute-done.7.refs_4_) | copy-start | bytes 1228804
  94.1 4.3 %collective-permute-start.11 = (bf16[400,512]{1,0:T(8,128)(2,1)S(1)}, bf16[400,512]{1,0:T(8,128)(2,1)S(1)}, u32[]{:S(2)}, u32[]{:S(2)}) collective-permute-start(bf16[400,512]{1,0:T(8,128)(2,1)S(1)} %collective-permute-done.7.refs_4_), channel_id=1, source_target_pairs={{0,1},{1,0},{2,3},{3,2},{4,5},{5,4},{6,7},{7,6},{8,9},{9,8},{10,11... | collective-permute-start | bytes 1228808 | tf_op jit(solution)/shard_map/ppermute | solution.py:24
  97.1 2.0 copy-start.8
  97.1 2.0 collective-permute-start.12
  124.0 6.3 %collective-permute-start.13 = (bf16[2,400,1024]{2,1,0:T(8,128)(2,1)}, bf16[2,400,1024]{2,1,0:T(8,128)(2,1)S(1)}, u32[]{:S(2)}, u32[]{:S(2)}) collective-permute-start(bf16[2,400,1024]{2,1,0:T(8,128)(2,1)} %get-tuple-element.58), channel_id=1, source_target_pairs={{0,1},{1,0},{2,3},{3,2},{4,5},{5,4},{6,7},{7,6},{8,9},{9,8},{10,11... | collective-permute-start | bytes 4915208 | tf_op jit(solution)/shard_map/ppermute | solution.py:24
  133.2 12.5 %collective-permute-start.14 = (bf16[400,512]{1,0:T(8,128)(2,1)S(1)}, bf16[400,512]{1,0:T(8,128)(2,1)S(1)}, u32[]{:S(2)}, u32[]{:S(2)}) collective-permute-start(bf16[400,512]{1,0:T(8,128)(2,1)S(1)} %get-tuple-element.82), channel_id=1, source_target_pairs={{0,2},{1,3},{2,0},{3,1},{4,6},{5,7},{6,4},{7,5},{8,10},{9,11},{10,... | collective-permute-start | bytes 1228808 | tf_op jit(solution)/shard_map/ppermute | solution.py:24
  133.3 19.4 %collective-permute-start.15 = (bf16[400,512]{1,0:T(8,128)(2,1)S(1)}, bf16[400,512]{1,0:T(8,128)(2,1)S(1)}, u32[]{:S(2)}, u32[]{:S(2)}) collective-permute-start(bf16[400,512]{1,0:T(8,128)(2,1)S(1)} %get-tuple-element.83), channel_id=1, source_target_pairs={{0,2},{1,3},{2,0},{3,1},{4,6},{5,7},{6,4},{7,5},{8,10},{9,11},{10,... | collective-permute-start | bytes 1228808 | tf_op jit(solution)/shard_map/ppermute | solution.py:24
  142.5 24.5 %collective-permute-start.17 = (f32[16,152,128]{2,1,0:T(8,128)}, f32[16,152,128]{2,1,0:T(8,128)S(1)}, u32[]{:S(2)}, u32[]{:S(2)}) collective-permute-start(f32[16,152,128]{2,1,0:T(8,128)} %get-tuple-element.67), channel_id=1, source_target_pairs={{0,1},{1,0},{2,3},{3,2},{4,5},{5,4},{6,7},{7,6},{8,9},{9,8},{10,11... | collective-permute-start | bytes 3735560 | tf_op jit(solution)/shard_map/ppermute | solution.py:24
  153.0 14.0 %collective-permute-start.18 = (bf16[400,512]{1,0:T(8,128)(2,1)S(1)}, bf16[400,512]{1,0:T(8,128)(2,1)S(1)}, u32[]{:S(2)}, u32[]{:S(2)}) collective-permute-start(bf16[400,512]{1,0:T(8,128)(2,1)S(1)} %get-tuple-element.84), channel_id=1, source_target_pairs={{0,130},{1,131},{2,128},{3,129},{4,134},{5,135},{6,132},{7,133},{8... | collective-permute-start | bytes 1228808 | tf_op jit(solution)/shard_map/ppermute | solution.py:34
  153.6 13.5 %copy-start.3 = (f32[16,152,128]{2,1,0:T(8,128)S(1)}, f32[16,152,128]{2,1,0:T(8,128)}, u32[]{:S(2)}) copy-start(f32[16,152,128]{2,1,0:T(8,128)} %get-tuple-element.61) | copy-start | bytes 3735556
  166.4 51.6 %collective-permute-start.16 = (bf16[2,400,1024]{2,1,0:T(8,128)(2,1)}, bf16[2,400,1024]{2,1,0:T(8,128)(2,1)S(1)}, u32[]{:S(2)}, u32[]{:S(2)}) collective-permute-start(bf16[2,400,1024]{2,1,0:T(8,128)(2,1)} %get-tuple-element.66), channel_id=1, source_target_pairs={{0,1},{1,0},{2,3},{3,2},{4,5},{5,4},{6,7},{7,6},{8,9},{9,8},{10,11... | collective-permute-start | bytes 4915208 | tf_op jit(solution)/shard_map/ppermute | solution.py:24
  167.3 17.3 %collective-permute-start.19 = (bf16[4,152,128]{2,1,0:T(8,128)(2,1)S(1)}, bf16[4,152,128]{2,1,0:T(8,128)(2,1)S(1)}, u32[]{:S(2)}, u32[]{:S(2)}) collective-permute-start(bf16[4,152,128]{2,1,0:T(8,128)(2,1)S(1)} %get-tuple-element.88), channel_id=1, source_target_pairs={{0,4},{4,0},{8,12},{12,8},{16,20},{20,16},{24,28},{28,24},{32,36},... | collective-permute-start | bytes 466952 | tf_op jit(solution)/shard_map/ppermute | solution.py:24
  172.0 19.0 %collective-permute-start.20 = (bf16[4,152,128]{2,1,0:T(8,128)(2,1)S(1)}, bf16[4,152,128]{2,1,0:T(8,128)(2,1)S(1)}, u32[]{:S(2)}, u32[]{:S(2)}) collective-permute-start(bf16[4,152,128]{2,1,0:T(8,128)(2,1)S(1)} %get-tuple-element.90), channel_id=1, source_target_pairs={{0,8},{4,12},{8,0},{12,4},{16,24},{20,28},{24,16},{28,20},{32,40},... | collective-permute-start | bytes 466952 | tf_op jit(solution)/shard_map/ppermute | solution.py:24
  184.0 9.6 %collective-permute-start.21 = (bf16[4,152,128]{2,1,0:T(8,128)(2,1)S(1)}, bf16[4,152,128]{2,1,0:T(8,128)(2,1)S(1)}, u32[]{:S(2)}, u32[]{:S(2)}) collective-permute-start(bf16[4,152,128]{2,1,0:T(8,128)(2,1)S(1)} %get-tuple-element.89), channel_id=1, source_target_pairs={{0,12},{4,8},{8,4},{12,0},{16,28},{20,24},{24,20},{28,16},{32,44},... | collective-permute-start | bytes 466952 | tf_op jit(solution)/shard_map/ppermute | solution.py:24
  184.0 21.6 %collective-permute-start.25 = (bf16[400,512]{1,0:T(8,128)(2,1)S(1)}, bf16[400,512]{1,0:T(8,128)(2,1)S(1)}, u32[]{:S(2)}, u32[]{:S(2)}) collective-permute-start(bf16[400,512]{1,0:T(8,128)(2,1)S(1)} %get-tuple-element.85), channel_id=1, source_target_pairs={{0,130},{1,131},{2,128},{3,129},{4,134},{5,135},{6,132},{7,133},{8... | collective-permute-start | bytes 1228808 | tf_op jit(solution)/shard_map/ppermute | solution.py:34
  184.5 33.5 %copy-start.1 = (f32[2,400,1024]{2,1,0:T(8,128)S(1)}, f32[2,400,1024]{2,1,0:T(8,128)}, u32[]{:S(2)}) copy-start(f32[2,400,1024]{2,1,0:T(8,128)} %get-tuple-element.65) | copy-start | bytes 9830404
  193.7 3.9 %collective-permute-start.22 = (f32[152,128]{1,0:T(8,128)S(1)}, f32[152,128]{1,0:T(8,128)S(1)}, u32[]{:S(2)}, u32[]{:S(2)}) collective-permute-start(f32[152,128]{1,0:T(8,128)S(1)} %get-tuple-element.93), channel_id=1, source_target_pairs={{0,16},{4,20},{8,24},{12,28},{16,0},{20,4},{24,8},{28,12},{32,48},... | collective-permute-start | bytes 233480 | tf_op jit(solution)/shard_map/ppermute | solution.py:24
  193.8 5.8 %collective-permute-start.23 = (f32[152,128]{1,0:T(8,128)S(1)}, f32[152,128]{1,0:T(8,128)S(1)}, u32[]{:S(2)}, u32[]{:S(2)}) collective-permute-start(f32[152,128]{1,0:T(8,128)S(1)} %get-tuple-element.92), channel_id=1, source_target_pairs={{0,32},{4,36},{8,40},{12,44},{16,48},{20,52},{24,56},{28,60},{32,0... | collective-permute-start | bytes 233480 | tf_op jit(solution)/shard_map/ppermute | solution.py:24
  196.8 5.5 %collective-permute-start.24 = (f32[152,128]{1,0:T(8,128)S(1)}, f32[152,128]{1,0:T(8,128)S(1)}, u32[]{:S(2)}, u32[]{:S(2)}) collective-permute-start(f32[152,128]{1,0:T(8,128)S(1)} %get-tuple-element.91), channel_id=1, source_target_pairs={{0,48},{4,52},{8,56},{12,60},{16,32},{20,36},{24,40},{28,44},{32,1... | collective-permute-start | bytes 233480 | tf_op jit(solution)/shard_map/ppermute | solution.py:24
  205.6 3.2 %collective-permute-start.26 = (f32[152,128]{1,0:T(8,128)S(1)}, f32[152,128]{1,0:T(8,128)S(1)}, u32[]{:S(2)}, u32[]{:S(2)}) collective-permute-start(f32[152,128]{1,0:T(8,128)S(1)} %fusion.8), channel_id=1, source_target_pairs={{0,2},{1,3},{2,0},{3,1},{4,6},{5,7},{6,4},{7,5},{8,10},{9,11},{10,... | collective-permute-start | bytes 233480 | tf_op jit(solution)/shard_map/ppermute | solution.py:24
  208.9 5.9 %collective-permute-start.27 = (f32[152,128]{1,0:T(8,128)S(1)}, f32[152,128]{1,0:T(8,128)S(1)}, u32[]{:S(2)}, u32[]{:S(2)}) collective-permute-start(f32[152,128]{1,0:T(8,128)S(1)} %add.97), channel_id=1, source_target_pairs={{0,64},{4,68},{8,72},{12,76},{16,80},{20,84},{24,88},{28,92},{32,9... | collective-permute-start | bytes 233480 | tf_op jit(solution)/shard_map/ppermute | solution.py:24
  209.0 8.7 %collective-permute-start.28 = (f32[152,128]{1,0:T(8,128)S(1)}, f32[152,128]{1,0:T(8,128)S(1)}, u32[]{:S(2)}, u32[]{:S(2)}) collective-permute-start(f32[152,128]{1,0:T(8,128)S(1)} %add.97), channel_id=1, source_target_pairs={{0,128},{4,132},{8,136},{12,140},{16,144},{20,148},{24,152},{28,15... | collective-permute-start | bytes 233480 | tf_op jit(solution)/shard_map/ppermute | solution.py:24
  211.0 7.0 %collective-permute-start.29 = (f32[152,128]{1,0:T(8,128)S(1)}, f32[152,128]{1,0:T(8,128)S(1)}, u32[]{:S(2)}, u32[]{:S(2)}) collective-permute-start(f32[152,128]{1,0:T(8,128)S(1)} %add.97), channel_id=1, source_target_pairs={{0,192},{4,196},{8,200},{12,204},{16,208},{20,212},{24,216},{28,22... | collective-permute-start | bytes 233480 | tf_op jit(solution)/shard_map/ppermute | solution.py:24
  218.8 17.8 %copy-start.17 = (f32[1345]{0:T(1024)S(1)}, f32[1345]{0:T(1024)}, u32[]{:S(2)}) copy-start(f32[1345]{0:T(1024)} %param.12) | copy-start | bytes 16144
  219.0 22.4 %collective-permute-start.30 = (bf16[400,1024]{1,0:T(8,128)(2,1)S(1)}, bf16[400,1024]{1,0:T(8,128)(2,1)S(1)}, u32[]{:S(2)}, u32[]{:S(2)}) collective-permute-start(bf16[400,1024]{1,0:T(8,128)(2,1)S(1)} %slice_bitcast_fusion), channel_id=1, source_target_pairs={{0,2},{1,3},{2,0},{3,1},{4,6},{5,7},{6,4},{7,5},{8,10},{9,11},{10,... | collective-permute-start | bytes 2457608 | tf_op jit(solution)/shard_map/ppermute | solution.py:24
  221.3 7.4 %collective-permute-start.31 = (bf16[152,128]{1,0:T(8,128)(2,1)S(1)}, bf16[152,128]{1,0:T(8,128)(2,1)S(1)}, u32[]{:S(2)}, u32[]{:S(2)}) collective-permute-start(bf16[152,128]{1,0:T(8,128)(2,1)S(1)} %add_convert_fusion), channel_id=1, source_target_pairs={{0,16},{4,20},{8,24},{12,28},{16,0},{20,4},{24,8},{28,12},{32,48},... | collective-permute-start | bytes 116744 | tf_op jit(solution)/shard_map/ppermute | solution.py:24
  225.3 5.1 %collective-permute-start.32 = (bf16[152,128]{1,0:T(8,128)(2,1)S(1)}, bf16[152,128]{1,0:T(8,128)(2,1)S(1)}, u32[]{:S(2)}, u32[]{:S(2)}) collective-permute-start(bf16[152,128]{1,0:T(8,128)(2,1)S(1)} %add_convert_fusion), channel_id=1, source_target_pairs={{0,32},{4,36},{8,40},{12,44},{16,48},{20,52},{24,56},{28,60},{32,0... | collective-permute-start | bytes 116744 | tf_op jit(solution)/shard_map/ppermute | solution.py:24
  228.6 4.0 %collective-permute-start.33 = (bf16[152,128]{1,0:T(8,128)(2,1)S(1)}, bf16[152,128]{1,0:T(8,128)(2,1)S(1)}, u32[]{:S(2)}, u32[]{:S(2)}) collective-permute-start(bf16[152,128]{1,0:T(8,128)(2,1)S(1)} %add_convert_fusion), channel_id=1, source_target_pairs={{0,48},{4,52},{8,56},{12,60},{16,32},{20,36},{24,40},{28,44},{32,1... | collective-permute-start | bytes 116744 | tf_op jit(solution)/shard_map/ppermute | solution.py:24
  232.7 4.5 %collective-permute-start.34 = (bf16[4,152,128]{2,1,0:T(8,128)(2,1)S(1)}, bf16[4,152,128]{2,1,0:T(8,128)(2,1)S(1)}, u32[]{:S(2)}, u32[]{:S(2)}) collective-permute-start(bf16[4,152,128]{2,1,0:T(8,128)(2,1)S(1)} %get-tuple-element.95), channel_id=1, source_target_pairs={{0,4},{4,0},{8,12},{12,8},{16,20},{20,16},{24,28},{28,24},{32,36},... | collective-permute-start | bytes 466952 | tf_op jit(solution)/shard_map/ppermute | solution.py:24
  233.0 6.9 %collective-permute-start.35 = (bf16[4,152,128]{2,1,0:T(8,128)(2,1)S(1)}, bf16[4,152,128]{2,1,0:T(8,128)(2,1)S(1)}, u32[]{:S(2)}, u32[]{:S(2)}) collective-permute-start(bf16[4,152,128]{2,1,0:T(8,128)(2,1)S(1)} %get-tuple-element.95), channel_id=1, source_target_pairs={{0,8},{4,12},{8,0},{12,4},{16,24},{20,28},{24,16},{28,20},{32,40},... | collective-permute-start | bytes 466952 | tf_op jit(solution)/shard_map/ppermute | solution.py:24
  235.3 6.0 %collective-permute-start.36 = (bf16[4,152,128]{2,1,0:T(8,128)(2,1)S(1)}, bf16[4,152,128]{2,1,0:T(8,128)(2,1)S(1)}, u32[]{:S(2)}, u32[]{:S(2)}) collective-permute-start(bf16[4,152,128]{2,1,0:T(8,128)(2,1)S(1)} %get-tuple-element.95), channel_id=1, source_target_pairs={{0,12},{4,8},{8,4},{12,0},{16,28},{20,24},{24,20},{28,16},{32,44},... | collective-permute-start | bytes 466952 | tf_op jit(solution)/shard_map/ppermute | solution.py:24
  241.4 4.7 %copy-start.2 = (bf16[4,4,152,128]{3,2,1,0:T(8,128)(2,1)}, bf16[4,4,152,128]{3,2,1,0:T(8,128)(2,1)S(1)}, u32[]{:S(2)}) copy-start(bf16[4,4,152,128]{3,2,1,0:T(8,128)(2,1)S(1)} %pad_maximum_fusion.1.near_ref) | copy-start | bytes 1867780
  241.4 4.7 %copy-start.19 = (f32[1024]{0:T(1024)S(1)}, f32[1024]{0:T(1024)}, u32[]{:S(2)}) copy-start(f32[1024]{0:T(1024)} %param.10) | copy-start | bytes 12292
  241.4 7.8 %collective-permute-start.37 = (bf16[4,4,152,128]{3,2,1,0:T(8,128)(2,1)S(1)}, bf16[4,4,152,128]{3,2,1,0:T(8,128)(2,1)S(1)}, u32[]{:S(2)}, u32[]{:S(2)}) collective-permute-start(bf16[4,4,152,128]{3,2,1,0:T(8,128)(2,1)S(1)} %pad_maximum_fusion.1.near_ref), channel_id=1, source_target_pairs={{0,1},{1,0},{2,3},{3,2},{4,5},{5,4},{6,7},{7,6},{8,9},{9,8},{10,11... | collective-permute-start | bytes 1867784 | tf_op jit(solution)/shard_map/ppermute | solution.py:24
  (10 other events, 10.7 us)

commit v3 on v2

--- a/solution.py
+++ b/solution.py
@@ -14,7 +14,6 @@
 LANES = 128
 SUBLANES = 8
 PIECES = 2
-RETURNS = 2
 VMEM_BYTES = 56 << 20
 RATE = 0.1
 BF16, F32, I32 = jnp.bfloat16, jnp.float32, jnp.int32
@@ -47,7 +46,7 @@
     return lax.dot_general(a, b, (((1,), (1,)), ((), ())), preferred_element_type=F32)
 
 
-def call(kernel, name, grid, in_specs, out_specs, out_shape, scratch, *args):
+def call(kernel, name, grid, in_specs, out_specs, out_shape, scratch, *args, flops=0):
     return pl.pallas_call(
         kernel,
         grid_spec=pltpu.PrefetchScalarGridSpec(
@@ -59,7 +58,7 @@
         ),
         out_shape=out_shape,
         compiler_params=pltpu.CompilerParams(vmem_limit_bytes=VMEM_BYTES),
-        cost_estimate=pl.CostEstimate(flops=0, bytes_accessed=0, transcendentals=0),
+        cost_estimate=pl.CostEstimate(flops=flops, bytes_accessed=0, transcendentals=0),
         name=name,
     )(*args)
 
@@ -502,17 +501,15 @@
         scal,
         after(grad_r, dst_sum),
         rel,
+        flops=2 * width * wide * edges,
     )
     sent = [
         swapped(dst_sum[0, :, k * step : (k + 1) * step].astype(BF16), "rep", 2)
         for k in range(PIECES)
     ]
-    sent = jnp.concatenate([after(x, rel_keep) for x in sent], axis=1)
-    mine = (dst_sum[1] + sent.astype(F32)).astype(BF16)
-    small = quarter // RETURNS
-    returned = [
-        swapped_far(mine[:, k * small : (k + 1) * small], half, 2) for k in range(RETURNS)
-    ]
+    first = dst_sum[1, :, :step] + after(sent[0], rel_keep).astype(F32)
+    first = first.astype(BF16)
+    returned = [swapped_far(first, half, 2)]
     src_keep, src_send = call(
         scatter_kernel,
         "source_grads",
@@ -522,15 +519,20 @@
         [f32_of(*half_parts), bf16_of(*half_parts)],
         [pltpu.VMEM((width, rows_part), F32)],
         scal,
-        after(grad_s, mine),
+        after(grad_s, first),
         src,
-    )
-
-    grid = rel_keep + after(swapped(rel_send, "rep", 1), src_keep, *returned[: RETURNS // 2])
+        flops=width * rows_part * edges,
+    )
+
+    last = dst_sum[1, :, step:] + after(sent[1], src_keep).astype(F32)
+    last = last.astype(BF16)
+    returned.append(swapped_far(last, half, 2))
+
+    grid = rel_keep + after(swapped(rel_send, "rep", 1), src_keep, returned[0], last)
     grid = grid.reshape(4, 4, *packed[2:]).swapaxes(0, 1)
     line = summed([grid[0], *(grid[k].astype(BF16) for k in (1, 2, 3))], "dom", 1)
     cell = summed(line, "dom", 4)
-    cell = after(cell, *returned[RETURNS // 2 :])
+    cell = after(cell, *returned[1:])
     cell = cell + swapped(cell, "rep", 2)
     total = summed([cell] * 4, "dom", 16).astype(BF16)
     src_sum = src_keep + swapped(src_send, "rep", 1).astype(F32)

time: 260 us -> 250 us (0.962)
  waiting for transfers between devices: 43 us -> 33.6 us
    ppermute x5, starting transfers between devices: 5.71 us -> 19.1 us  [swapped_far(): return lax.ppermute(x, ('dom', 'rep'), pairs)]
    ppermute x33, starting transfers between devices: 89.2 us -> 78.2 us  [swapped(): lax.ppermute(x, axis, [(i, i ^ mask) for i in range(lax.axis_size(axis))])]
    ppermute x33, waiting for transfers between devices: 39.7 us -> 29.7 us  [swapped(): lax.ppermute(x, axis, [(i, i ^ mask) for i in range(lax.axis_size(axis))])]
where the time goes in v3:
time: 250 us; the launch traced here: 247 us
  starting transfers between devices  97.4 us (39%)
  Pallas kernels  86.7 us (35%)
  waiting for transfers between devices  33.6 us (13%)
  other arithmetic  19.8 us (8%)
  local copies, waits for them, and re-layouts  7.83 us (3%)
    pallas_call x8, Pallas kernels, call(): pl.pallas_call(kernel, grid_spec=pltpu.PrefetchScalarGridSpec(num_scalar_...  86.7 us
    ppermute x33, starting transfers between devices, swapped(): lax.ppermute(x, axis, [(i, i ^ mask) for i in range(lax.axis_size(axis))])  78.2 us
    ppermute x33, waiting for transfers between devices, swapped(): lax.ppermute(x, axis, [(i, i ^ mask) for i in range(lax.axis_size(axis))])  29.7 us
    ppermute x5, starting transfers between devices, swapped_far(): return lax.ppermute(x, ('dom', 'rep'), pairs)  19.1 us
    sort x1, other arithmetic, body(): lax.sort((key, edge_source, edge_target, edge_relation), num_keys=1)  6 us
  transfers between devices with their start and end apart: 38, of which 16 were waited for; matrix products, arithmetic and copies ran while one was open for 8% of the time, Pallas kernels for 23%

profile of v3, /device:TPU:1, one launch (start us, length us, event | category | flops | bytes accessed | tf_op | source)
XLA Modules:
  0.0 247.3 jit_solution(6372836140206939775)
XLA Ops:
  0.6 7.8 %collective-permute-start = (s32[1024]{0:T(1024)}, s32[1024]{0:T(1024)S(1)}, u32[]{:S(2)}, u32[]{:S(2)}) collective-permute-start(s32[1024]{0:T(1024)} %param.17), channel_id=1, source_target_pairs={{0,128},{4,132},{8,136},{12,140},{16,144},{20,148},{24,152},{28,15... | collective-permute-start | bytes 12296 | tf_op jit(solution)/shard_map/ppermute | solution.py:23
  8.5 1.3 dynamic-slice_bitcast_fusion
  11.4 6.0 %sort.39 = (s32[4096]{0:T(1024)}, s32[4096]{0:T(1024)S(1)}, s32[4096]{0:T(1024)S(1)}, s32[4096]{0:T(1024)}, s32[4096]{0:T(1024)}) sort(s32[4096]{0:T(1024)S(1)} %fusion.15, s32[4096]{0:T(1024)S(1)} %copy-done.13, s32[4096]{0:T(1024)S(1)} %copy-done.14, s32[4096]{0:T(1024)S(1)} %copy-done.16, s32[4096]{0:T(1024)S(1)} %iota.25), dimensions={0}, to_apply=%region_0.1 | sort | flops 49152 | bytes 163840 | tf_op jit(solution)/shard_map/sort | solution.py:371
  17.4 1.7 pad_maximum_fusion.table_ref
  20.5 4.3 %partner_negatives.1 = bf16[400,256]{1,0:T(8,128)(2,1)} custom-call(s32[3]{0:T(128)} %pad_add_fusion.3.scal, s32[1,256]{1,0:T(1,128)} %bitcast.115, bf16[400,4096]{1,0:T(8,128)(2,1)} %bitcast.93), custom_call_target="tpu_custom_call" | custom-call | tf_op jit(solution)/shard_map/partner_negatives/pallas_call | solution.py:50
  25.8 4.2 %collective-permute-start.1 = (bf16[400,256]{0,1:T(8,128)(2,1)S(1)}, bf16[400,256]{0,1:T(8,128)(2,1)S(1)}, u32[]{:S(2)}, u32[]{:S(2)}) collective-permute-start(bf16[400,256]{0,1:T(8,128)(2,1)S(1)} %copy.21), channel_id=1, source_target_pairs={{0,130},{1,131},{2,128},{3,129},{4,134},{5,135},{6,132},{7,133},{8... | collective-permute-start | bytes 614408 | tf_op jit(solution)/shard_map/ppermute | solution.py:33
  31.3 11.7 %source_rows.1.s_ref = bf16[400,4096]{1,0:T(8,128)(2,1)} custom-call(s32[67]{0:T(128)} %pad_add_fusion.2.scal, s32[1,4096]{1,0:T(1,128)} %bitcast.106, bf16[400,4096]{1,0:T(8,128)(2,1)} %bitcast.94), custom_call_target="tpu_custom_call" | custom-call | tf_op jit(solution)/shard_map/source_rows/pallas_call | solution.py:50
  43.3 9.4 %relation_rows.1.r_ref = f32[400,4096]{1,0:T(8,128)} custom-call(s32[67]{0:T(128)} %pad_add_fusion.2.scal, s32[1,4096]{1,0:T(1,128)} %bitcast.112, bf16[800,1536]{1,0:T(8,128)(2,1)} %pad_maximum_fusion.table_ref), custom_call_target="tpu_custom_call" | custom-call | tf_op jit(solution)/shard_map/relation_rows/pallas_call | solution.py:50
  52.7 6.7 %collective-permute-start.3 = (bf16[400,256]{0,1:T(8,128)(2,1)S(1)}, bf16[400,256]{0,1:T(8,128)(2,1)S(1)}, u32[]{:S(2)}, u32[]{:S(2)}) collective-permute-start(bf16[400,256]{0,1:T(8,128)(2,1)S(1)} %collective-permute-done.1), channel_id=1, source_target_pairs={{0,1},{1,0},{2,3},{3,2},{4,5},{5,4},{6,7},{7,6},{8,9},{9,8},{10,11... | collective-permute-start | bytes 614408 | tf_op jit(solution)/shard_map/ppermute | solution.py:23
  59.4 12.5 %collective-permute-start.7 = (bf16[400,512]{1,0:T(8,128)(2,1)}, bf16[400,512]{1,0:T(8,128)(2,1)S(1)}, u32[]{:S(2)}, u32[]{:S(2)}) collective-permute-start(bf16[400,512]{1,0:T(8,128)(2,1)} %collective-permute-done.5.refs_2_), channel_id=1, source_target_pairs={{0,2},{1,3},{2,0},{3,1},{4,6},{5,7},{6,4},{7,5},{8,10},{9,11},{10,... | collective-permute-start | bytes 1228808 | tf_op jit(solution)/shard_map/ppermute | solution.py:23
  72.5 1.4 collective-permute-start.8
  74.6 1.2 copy.22.neg_t_ref
  76.9 13.3 %negative_scores.1 = (f32[400,4096]{1,0:T(8,128)}, bf16[400,1024]{1,0:T(8,128)(2,1)}) custom-call(s32[67]{0:T(128)} %pad_add_fusion.2.scal, bf16[400,4096]{1,0:T(8,128)(2,1)} %source_rows.1.s_ref, f32[400,4096]{1,0:T(8,128)} %relation_rows.1.r_ref, bf16[400,1024]{1,0:T(8,128)(2,1)} %copy.22.neg_t_ref, bf16[1024,400]{1,0:T(8,128)(2,1)} %multiply_bitcast_fusion.half_neg_ref), custom_call_target="tpu_custom_call" | custom-call | tf_op jit(solution)/shard_map/negative_scores/pallas_call | solution.py:50
  90.4 1.6 collective-permute-done.8.refs_5_
  94.9 24.1 %targets.1 = (bf16[400,4096]{1,0:T(8,128)(2,1)}, bf16[400,4096]{1,0:T(8,128)(2,1)}, f32[2,400,1024]{2,1,0:T(8,128)}, bf16[2,400,1024]{2,1,0:T(8,128)(2,1)}) custom-call(s32[67]{0:T(128)} %pad_add_fusion.2.scal, bf16[400,4096]{1,0:T(8,128)(2,1)} %source_rows.1.s_ref, f32[400,4096]{1,0:T(8,128)} %relation_rows.1.r_ref, f32[400,4096]{1,0:T(8,128)} %get-tuple-element.52.gun_ref, ...), custom_call_target="tpu_custom_call" | custom-call | tf_op jit(solution)/shard_map/targets/pallas_call | solution.py:50
  119.6 3.3 %collective-permute-done.13 = bf16[2,400,1024]{2,1,0:T(8,128)(2,1)S(1)} collective-permute-done((bf16[2,400,1024]{2,1,0:T(8,128)(2,1)}, bf16[2,400,1024]{2,1,0:T(8,128)(2,1)S(1)}, u32[]{:S(2)}, u32[]{:S(2)}) %collective-permute-start.13) | collective-permute-done | bytes 1638432 | tf_op jit(solution)/shard_map/ppermute | solution.py:23
  122.9 2.6 %fusion.21 = (bf16[2,400,1024]{2,1,0:T(8,128)(2,1)S(1)}, f32[2,400,1024]{2,1,0:T(8,128)S(1)}) fusion(f32[2,400,1024]{2,1,0:T(8,128)} %get-tuple-element.57, bf16[2,400,1024]{2,1,0:T(8,128)(2,1)S(1)} %collective-permute-done.13), kind=kLoop, calls=%fused_computation.72 | loop fusion | flops 2457600 | bytes 9830400 | tf_op jit(solution)/shard_map/convert.4
  125.7 2.2 collective-permute-start.14
  127.9 6.5 %relation_grads.1 = (f32[16,152,128]{2,1,0:T(8,128)}, f32[16,152,128]{2,1,0:T(8,128)}) custom-call(s32[67]{0:T(128)} %pad_add_fusion.2.scal, bf16[400,4096]{1,0:T(8,128)(2,1)} %get-tuple-element.60.g_ref, s32[1,4096]{1,0:T(1,128)} %bitcast.113), custom_call_target="tpu_custom_call" | custom-call | flops 5033164800 | tf_op jit(solution)/shard_map/relation_grads/pallas_call | solution.py:50
  134.4 1.7 collective-permute-start.16
  136.5 1.1 collective-permute-done.14
  137.7 11.3 %collective-permute-start.17 = (bf16[400,512]{1,0:T(8,128)(2,1)S(1)}, bf16[400,512]{1,0:T(8,128)(2,1)S(1)}, u32[]{:S(2)}, u32[]{:S(2)}) collective-permute-start(bf16[400,512]{1,0:T(8,128)(2,1)S(1)} %fusion.5), channel_id=1, source_target_pairs={{0,130},{1,131},{2,128},{3,129},{4,134},{5,135},{6,132},{7,133},{8... | collective-permute-start | bytes 1228808 | tf_op jit(solution)/shard_map/ppermute | solution.py:33
  149.0 12.9 %source_grads.1 = (f32[2,400,1024]{2,1,0:T(8,128)}, bf16[2,400,1024]{2,1,0:T(8,128)(2,1)}) custom-call(s32[67]{0:T(128)} %pad_add_fusion.2.scal, bf16[400,4096]{1,0:T(8,128)(2,1)} %get-tuple-element.63.g_ref, s32[1,4096]{1,0:T(1,128)} %bitcast.107), custom_call_target="tpu_custom_call" | custom-call | flops 6710886400 | tf_op jit(solution)/shard_map/source_grads/pallas_call | solution.py:50
  162.6 3.8 %collective-permute-done.17 = bf16[400,512]{1,0:T(8,128)(2,1)S(1)} collective-permute-done((bf16[400,512]{1,0:T(8,128)(2,1)S(1)}, bf16[400,512]{1,0:T(8,128)(2,1)S(1)}, u32[]{:S(2)}, u32[]{:S(2)}) %collective-permute-start.17) | collective-permute-done | bytes 409632 | tf_op jit(solution)/shard_map/ppermute | solution.py:33
  166.7 3.5 %collective-permute-start.19 = (bf16[4,152,128]{2,1,0:T(8,128)(2,1)S(1)}, bf16[4,152,128]{2,1,0:T(8,128)(2,1)S(1)}, u32[]{:S(2)}, u32[]{:S(2)}) collective-permute-start(bf16[4,152,128]{2,1,0:T(8,128)(2,1)S(1)} %get-tuple-element.86), channel_id=1, source_target_pairs={{0,4},{4,0},{8,12},{12,8},{16,20},{20,16},{24,28},{28,24},{32,36},... | collective-permute-start | bytes 466952 | tf_op jit(solution)/shard_map/ppermute | solution.py:23
  170.2 2.5 %collective-permute-start.21 = (bf16[4,152,128]{2,1,0:T(8,128)(2,1)S(1)}, bf16[4,152,128]{2,1,0:T(8,128)(2,1)S(1)}, u32[]{:S(2)}, u32[]{:S(2)}) collective-permute-start(bf16[4,152,128]{2,1,0:T(8,128)(2,1)S(1)} %get-tuple-element.87), channel_id=1, source_target_pairs={{0,12},{4,8},{8,4},{12,0},{16,28},{20,24},{24,20},{28,16},{32,44},... | collective-permute-start | bytes 466952 | tf_op jit(solution)/shard_map/ppermute | solution.py:23
  172.7 3.2 %collective-permute-start.25 = (bf16[400,512]{1,0:T(8,128)(2,1)S(1)}, bf16[400,512]{1,0:T(8,128)(2,1)S(1)}, u32[]{:S(2)}, u32[]{:S(2)}) collective-permute-start(bf16[400,512]{1,0:T(8,128)(2,1)S(1)} %fusion.3), channel_id=1, source_target_pairs={{0,130},{1,131},{2,128},{3,129},{4,134},{5,135},{6,132},{7,133},{8... | collective-permute-start | bytes 1228808 | tf_op jit(solution)/shard_map/ppermute | solution.py:33
  177.2 6.7 %collective-permute-start.22 = (f32[152,128]{1,0:T(8,128)S(1)}, f32[152,128]{1,0:T(8,128)S(1)}, u32[]{:S(2)}, u32[]{:S(2)}) collective-permute-start(f32[152,128]{1,0:T(8,128)S(1)} %get-tuple-element.91), channel_id=1, source_target_pairs={{0,16},{4,20},{8,24},{12,28},{16,0},{20,4},{24,8},{28,12},{32,48},... | collective-permute-start | bytes 233480 | tf_op jit(solution)/shard_map/ppermute | solution.py:23
  183.9 5.2 %collective-permute-start.23 = (f32[152,128]{1,0:T(8,128)S(1)}, f32[152,128]{1,0:T(8,128)S(1)}, u32[]{:S(2)}, u32[]{:S(2)}) collective-permute-start(f32[152,128]{1,0:T(8,128)S(1)} %get-tuple-element.90), channel_id=1, source_target_pairs={{0,32},{4,36},{8,40},{12,44},{16,48},{20,52},{24,56},{28,60},{32,0... | collective-permute-start | bytes 233480 | tf_op jit(solution)/shard_map/ppermute | solution.py:23
  189.1 2.6 %collective-permute-done.23 = f32[152,128]{1,0:T(8,128)S(1)} collective-permute-done((f32[152,128]{1,0:T(8,128)S(1)}, f32[152,128]{1,0:T(8,128)S(1)}, u32[]{:S(2)}, u32[]{:S(2)}) %collective-permute-start.23) | collective-permute-done | bytes 77856 | tf_op jit(solution)/shard_map/ppermute | solution.py:23
  191.7 2.5 %collective-permute-done.24 = f32[152,128]{1,0:T(8,128)S(1)} collective-permute-done((f32[152,128]{1,0:T(8,128)S(1)}, f32[152,128]{1,0:T(8,128)S(1)}, u32[]{:S(2)}, u32[]{:S(2)}) %collective-permute-start.24) | collective-permute-done | bytes 77856 | tf_op jit(solution)/shard_map/ppermute | solution.py:23
  194.2 3.5 %collective-permute-start.26 = (f32[152,128]{1,0:T(8,128)S(1)}, f32[152,128]{1,0:T(8,128)S(1)}, u32[]{:S(2)}, u32[]{:S(2)}) collective-permute-start(f32[152,128]{1,0:T(8,128)S(1)} %fusion.10), channel_id=1, source_target_pairs={{0,2},{1,3},{2,0},{3,1},{4,6},{5,7},{6,4},{7,5},{8,10},{9,11},{10,... | collective-permute-start | bytes 233480 | tf_op jit(solution)/shard_map/ppermute | solution.py:23
  197.7 2.2 collective-permute-done.26
  200.0 2.6 %collective-permute-start.28 = (f32[152,128]{1,0:T(8,128)S(1)}, f32[152,128]{1,0:T(8,128)S(1)}, u32[]{:S(2)}, u32[]{:S(2)}) collective-permute-start(f32[152,128]{1,0:T(8,128)S(1)} %add.101), channel_id=1, source_target_pairs={{0,128},{4,132},{8,136},{12,140},{16,144},{20,148},{24,152},{28,15... | collective-permute-start | bytes 233480 | tf_op jit(solution)/shard_map/ppermute | solution.py:23
  202.6 3.2 %collective-permute-start.29 = (f32[152,128]{1,0:T(8,128)S(1)}, f32[152,128]{1,0:T(8,128)S(1)}, u32[]{:S(2)}, u32[]{:S(2)}) collective-permute-start(f32[152,128]{1,0:T(8,128)S(1)} %add.101), channel_id=1, source_target_pairs={{0,192},{4,196},{8,200},{12,204},{16,208},{20,212},{24,216},{28,22... | collective-permute-start | bytes 233480 | tf_op jit(solution)/shard_map/ppermute | solution.py:23
  205.8 2.1 collective-permute-done.28
  207.9 3.6 %collective-permute-done.29 = f32[152,128]{1,0:T(8,128)S(1)} collective-permute-done((f32[152,128]{1,0:T(8,128)S(1)}, f32[152,128]{1,0:T(8,128)S(1)}, u32[]{:S(2)}, u32[]{:S(2)}) %collective-permute-start.29) | collective-permute-done | bytes 77856 | tf_op jit(solution)/shard_map/ppermute | solution.py:23
  212.4 3.2 %collective-permute-start.30 = (bf16[400,1024]{1,0:T(8,128)(2,1)S(1)}, bf16[400,1024]{1,0:T(8,128)(2,1)S(1)}, u32[]{:S(2)}, u32[]{:S(2)}) collective-permute-start(bf16[400,1024]{1,0:T(8,128)(2,1)S(1)} %slice_bitcast_fusion), channel_id=1, source_target_pairs={{0,2},{1,3},{2,0},{3,1},{4,6},{5,7},{6,4},{7,5},{8,10},{9,11},{10,... | collective-permute-start | bytes 2457608 | tf_op jit(solution)/shard_map/ppermute | solution.py:23
  215.6 5.3 %collective-permute-start.32 = (bf16[152,128]{1,0:T(8,128)(2,1)S(1)}, bf16[152,128]{1,0:T(8,128)(2,1)S(1)}, u32[]{:S(2)}, u32[]{:S(2)}) collective-permute-start(bf16[152,128]{1,0:T(8,128)(2,1)S(1)} %add_convert_fusion), channel_id=1, source_target_pairs={{0,32},{4,36},{8,40},{12,44},{16,48},{20,52},{24,56},{28,60},{32,0... | collective-permute-start | bytes 116744 | tf_op jit(solution)/shard_map/ppermute | solution.py:23
  220.9 1.8 collective-permute-done.32
  222.7 2.3 collective-permute-done.33
  225.3 3.6 %collective-permute-start.36 = (bf16[4,152,128]{2,1,0:T(8,128)(2,1)S(1)}, bf16[4,152,128]{2,1,0:T(8,128)(2,1)S(1)}, u32[]{:S(2)}, u32[]{:S(2)}) collective-permute-start(bf16[4,152,128]{2,1,0:T(8,128)(2,1)S(1)} %get-tuple-element.93), channel_id=1, source_target_pairs={{0,12},{4,8},{8,4},{12,0},{16,28},{20,24},{24,20},{28,16},{32,44},... | collective-permute-start | bytes 466952 | tf_op jit(solution)/shard_map/ppermute | solution.py:23
  229.5 2.4 collective-permute-done.35
  231.9 2.5 %collective-permute-done.36 = bf16[4,152,128]{2,1,0:T(8,128)(2,1)S(1)} collective-permute-done((bf16[4,152,128]{2,1,0:T(8,128)(2,1)S(1)}, bf16[4,152,128]{2,1,0:T(8,128)(2,1)S(1)}, u32[]{:S(2)}, u32[]{:S(2)}) %collective-permute-start.36) | collective-permute-done | bytes 155680 | tf_op jit(solution)/shard_map/ppermute | solution.py:23
  234.5 2.3 collective-permute-start.37
  237.8 2.6 %fusion.6 = bf16[1024,400]{0,1:T(8,128)(2,1)} fusion(f32[1024]{0:T(1024)S(1)} %get-tuple-element.78, bf16[400,512]{1,0:T(8,128)(2,1)S(1)} %collective-permute-done.25, bf16[400,512]{1,0:T(8,128)(2,1)S(1)} %collective-permute-done.17, bf16[400,1024]{1,0:T(8,128)(2,1)S(1)} %collective-permute-done.30, f32[2,400,1024]{2,1,0:T(8,128)S(1)} %convert_add_fusion, ...), kind=kLoop, calls=%fused_computation.20 | loop fusion | flops 4915200 | bytes 4919300 | tf_op jit(solution)/shard_map/transpose | solution.py:563
  241.2 4.6 %relation_update.1 = (f32[400,1345]{1,0:T(8,128)}, f32[1,1345]{1,0:T(1,128)}) custom-call(s32[3]{0:T(128)} %pad_add_fusion.3.scal, f32[400,1345]{1,0:T(8,128)} %bitcast.95, f32[1,1345]{1,0:T(1,128)} %reshape.57.state_ref, bf16[4,4,152,128]{3,2,1,0:T(8,128)(2,1)} %copy-done.2, bf16[4,4,152,128]{3,2,1,0:T(8,128)(2,1)} %copy-done.4), custom_call_target="tpu_custom_call" | custom-call | tf_op jit(solution)/shard_map/relation_update/pallas_call | solution.py:50
  245.8 1.3 reduce
  (124 shorter events, 17.8 us)
Async XLA Ops:
  0.6 19.2 %collective-permute-start = (s32[1024]{0:T(1024)}, s32[1024]{0:T(1024)S(1)}, u32[]{:S(2)}, u32[]{:S(2)}) collective-permute-start(s32[1024]{0:T(1024)} %param.17), channel_id=1, source_target_pairs={{0,128},{4,132},{8,136},{12,140},{16,144},{20,148},{24,152},{28,15... | collective-permute-start | bytes 12296 | tf_op jit(solution)/shard_map/ppermute | solution.py:23
  8.5 1.9 copy-start
  9.9 49.5 %collective-permute-start.5 = (bf16[400,512]{1,0:T(8,128)(2,1)S(1)}, bf16[400,512]{1,0:T(8,128)(2,1)}, u32[]{:S(2)}, u32[]{:S(2)}) collective-permute-start(bf16[400,512]{1,0:T(8,128)(2,1)S(1)} %get-tuple-element.85), channel_id=1, source_target_pairs={{0,130},{1,131},{2,128},{3,129},{4,134},{5,135},{6,132},{7,133},{8... | collective-permute-start | bytes 1228808 | tf_op jit(solution)/shard_map/ppermute | solution.py:33
  25.8 17.1 %collective-permute-start.1 = (bf16[400,256]{0,1:T(8,128)(2,1)S(1)}, bf16[400,256]{0,1:T(8,128)(2,1)S(1)}, u32[]{:S(2)}, u32[]{:S(2)}) collective-permute-start(bf16[400,256]{0,1:T(8,128)(2,1)S(1)} %copy.21), channel_id=1, source_target_pairs={{0,130},{1,131},{2,128},{3,129},{4,134},{5,135},{6,132},{7,133},{8... | collective-permute-start | bytes 614408 | tf_op jit(solution)/shard_map/ppermute | solution.py:33
  30.0 42.5 %collective-permute-start.6 = (bf16[400,512]{1,0:T(8,128)(2,1)S(1)}, bf16[400,512]{1,0:T(8,128)(2,1)S(1)}, u32[]{:S(2)}, u32[]{:S(2)}) collective-permute-start(bf16[400,512]{1,0:T(8,128)(2,1)S(1)} %get-tuple-element.49), channel_id=1, source_target_pairs={{0,130},{1,131},{2,128},{3,129},{4,134},{5,135},{6,132},{7,133},{8... | collective-permute-start | bytes 1228808 | tf_op jit(solution)/shard_map/ppermute | solution.py:33
  42.9 29.1 %collective-permute-start.2 = (bf16[400,256]{0,1:T(8,128)(2,1)S(1)}, bf16[400,256]{0,1:T(8,128)(2,1)S(1)}, u32[]{:S(2)}, u32[]{:S(2)}) collective-permute-start(bf16[400,256]{0,1:T(8,128)(2,1)S(1)} %collective-permute-done.1), channel_id=1, source_target_pairs={{0,2},{1,3},{2,0},{3,1},{4,6},{5,7},{6,4},{7,5},{8,10},{9,11},{10,... | collective-permute-start | bytes 614408 | tf_op jit(solution)/shard_map/ppermute | solution.py:23
  52.7 21.3 %collective-permute-start.3 = (bf16[400,256]{0,1:T(8,128)(2,1)S(1)}, bf16[400,256]{0,1:T(8,128)(2,1)S(1)}, u32[]{:S(2)}, u32[]{:S(2)}) collective-permute-start(bf16[400,256]{0,1:T(8,128)(2,1)S(1)} %collective-permute-done.1), channel_id=1, source_target_pairs={{0,1},{1,0},{2,3},{3,2},{4,5},{5,4},{6,7},{7,6},{8,9},{9,8},{10,11... | collective-permute-start | bytes 614408 | tf_op jit(solution)/shard_map/ppermute | solution.py:23
  59.4 30.8 %collective-permute-start.7 = (bf16[400,512]{1,0:T(8,128)(2,1)}, bf16[400,512]{1,0:T(8,128)(2,1)S(1)}, u32[]{:S(2)}, u32[]{:S(2)}) collective-permute-start(bf16[400,512]{1,0:T(8,128)(2,1)} %collective-permute-done.5.refs_2_), channel_id=1, source_target_pairs={{0,2},{1,3},{2,0},{3,1},{4,6},{5,7},{6,4},{7,5},{8,10},{9,11},{10,... | collective-permute-start | bytes 1228808 | tf_op jit(solution)/shard_map/ppermute | solution.py:23
  71.9 21.6 %collective-permute-start.9 = (bf16[400,512]{1,0:T(8,128)(2,1)}, bf16[400,512]{1,0:T(8,128)(2,1)S(1)}, u32[]{:S(2)}, u32[]{:S(2)}) collective-permute-start(bf16[400,512]{1,0:T(8,128)(2,1)} %collective-permute-done.5.refs_2_), channel_id=1, source_target_pairs={{0,1},{1,0},{2,3},{3,2},{4,5},{5,4},{6,7},{7,6},{8,9},{9,8},{10,11... | collective-permute-start | bytes 1228808 | tf_op jit(solution)/shard_map/ppermute | solution.py:23
  72.0 2.6 %collective-permute-start.4 = (bf16[400,256]{0,1:T(8,128)(2,1)S(1)}, bf16[400,256]{0,1:T(8,128)(2,1)S(1)}, u32[]{:S(2)}, u32[]{:S(2)}) collective-permute-start(bf16[400,256]{0,1:T(8,128)(2,1)S(1)} %collective-permute-done.2), channel_id=1, source_target_pairs={{0,1},{1,0},{2,3},{3,2},{4,5},{5,4},{6,7},{7,6},{8,9},{9,8},{10,11... | collective-permute-start | bytes 614408 | tf_op jit(solution)/shard_map/ppermute | solution.py:23
  72.5 3.3 %copy-start.5 = (bf16[400,512]{1,0:T(8,128)(2,1)}, bf16[400,512]{1,0:T(8,128)(2,1)S(1)}, u32[]{:S(2)}) copy-start(bf16[400,512]{1,0:T(8,128)(2,1)S(1)} %collective-permute-done.6.refs_3_) | copy-start | bytes 1228804
  72.5 19.5 %collective-permute-start.8 = (bf16[400,512]{1,0:T(8,128)(2,1)S(1)}, bf16[400,512]{1,0:T(8,128)(2,1)S(1)}, u32[]{:S(2)}, u32[]{:S(2)}) collective-permute-start(bf16[400,512]{1,0:T(8,128)(2,1)S(1)} %collective-permute-done.6.refs_3_), channel_id=1, source_target_pairs={{0,2},{1,3},{2,0},{3,1},{4,6},{5,7},{6,4},{7,5},{8,10},{9,11},{10,... | collective-permute-start | bytes 1228808 | tf_op jit(solution)/shard_map/ppermute | solution.py:23
  73.9 19.6 %collective-permute-start.10 = (bf16[400,512]{1,0:T(8,128)(2,1)S(1)}, bf16[400,512]{1,0:T(8,128)(2,1)S(1)}, u32[]{:S(2)}, u32[]{:S(2)}) collective-permute-start(bf16[400,512]{1,0:T(8,128)(2,1)S(1)} %collective-permute-done.6.refs_3_), channel_id=1, source_target_pairs={{0,1},{1,0},{2,3},{3,2},{4,5},{5,4},{6,7},{7,6},{8,9},{9,8},{10,11... | collective-permute-start | bytes 1228808 | tf_op jit(solution)/shard_map/ppermute | solution.py:23
  76.9 15.9 %copy-start.18 = (s32[1024]{0:T(1024)S(1)}, s32[1024]{0:T(1024)}, u32[]{:S(2)}) copy-start(s32[1024]{0:T(1024)} %param.17) | copy-start | bytes 12292
  90.2 4.0 %copy-start.6 = (bf16[400,512]{1,0:T(8,128)(2,1)}, bf16[400,512]{1,0:T(8,128)(2,1)S(1)}, u32[]{:S(2)}) copy-start(bf16[400,512]{1,0:T(8,128)(2,1)S(1)} %collective-permute-done.7.refs_4_) | copy-start | bytes 1228804
  90.2 3.3 %collective-permute-start.11 = (bf16[400,512]{1,0:T(8,128)(2,1)S(1)}, bf16[400,512]{1,0:T(8,128)(2,1)S(1)}, u32[]{:S(2)}, u32[]{:S(2)}) collective-permute-start(bf16[400,512]{1,0:T(8,128)(2,1)S(1)} %collective-permute-done.7.refs_4_), channel_id=1, source_target_pairs={{0,1},{1,0},{2,3},{3,2},{4,5},{5,4},{6,7},{7,6},{8,9},{9,8},{10,11... | collective-permute-start | bytes 1228808 | tf_op jit(solution)/shard_map/ppermute | solution.py:23
  92.0 2.2 copy-start.8
  92.0 2.2 collective-permute-start.12
  119.0 3.9 %collective-permute-start.13 = (bf16[2,400,1024]{2,1,0:T(8,128)(2,1)}, bf16[2,400,1024]{2,1,0:T(8,128)(2,1)S(1)}, u32[]{:S(2)}, u32[]{:S(2)}) collective-permute-start(bf16[2,400,1024]{2,1,0:T(8,128)(2,1)} %get-tuple-element.58), channel_id=1, source_target_pairs={{0,1},{1,0},{2,3},{3,2},{4,5},{5,4},{6,7},{7,6},{8,9},{9,8},{10,11... | collective-permute-start | bytes 4915208 | tf_op jit(solution)/shard_map/ppermute | solution.py:23
  125.7 11.9 %collective-permute-start.14 = (bf16[400,512]{1,0:T(8,128)(2,1)S(1)}, bf16[400,512]{1,0:T(8,128)(2,1)S(1)}, u32[]{:S(2)}, u32[]{:S(2)}) collective-permute-start(bf16[400,512]{1,0:T(8,128)(2,1)S(1)} %get-tuple-element.82), channel_id=1, source_target_pairs={{0,2},{1,3},{2,0},{3,1},{4,6},{5,7},{6,4},{7,5},{8,10},{9,11},{10,... | collective-permute-start | bytes 1228808 | tf_op jit(solution)/shard_map/ppermute | solution.py:23
  134.4 32.0 %collective-permute-start.16 = (f32[16,152,128]{2,1,0:T(8,128)}, f32[16,152,128]{2,1,0:T(8,128)S(1)}, u32[]{:S(2)}, u32[]{:S(2)}) collective-permute-start(f32[16,152,128]{2,1,0:T(8,128)} %get-tuple-element.66), channel_id=1, source_target_pairs={{0,1},{1,0},{2,3},{3,2},{4,5},{5,4},{6,7},{7,6},{8,9},{9,8},{10,11... | collective-permute-start | bytes 3735560 | tf_op jit(solution)/shard_map/ppermute | solution.py:23
  136.1 25.9 %collective-permute-start.18 = (bf16[400,512]{1,0:T(8,128)(2,1)S(1)}, bf16[400,512]{1,0:T(8,128)(2,1)S(1)}, u32[]{:S(2)}, u32[]{:S(2)}) collective-permute-start(bf16[400,512]{1,0:T(8,128)(2,1)S(1)} %get-tuple-element.83), channel_id=1, source_target_pairs={{0,2},{1,3},{2,0},{3,1},{4,6},{5,7},{6,4},{7,5},{8,10},{9,11},{10,... | collective-permute-start | bytes 1228808 | tf_op jit(solution)/shard_map/ppermute | solution.py:23
  137.7 28.7 %collective-permute-start.17 = (bf16[400,512]{1,0:T(8,128)(2,1)S(1)}, bf16[400,512]{1,0:T(8,128)(2,1)S(1)}, u32[]{:S(2)}, u32[]{:S(2)}) collective-permute-start(bf16[400,512]{1,0:T(8,128)(2,1)S(1)} %fusion.5), channel_id=1, source_target_pairs={{0,130},{1,131},{2,128},{3,129},{4,134},{5,135},{6,132},{7,133},{8... | collective-permute-start | bytes 1228808 | tf_op jit(solution)/shard_map/ppermute | solution.py:33
  161.9 4.5 %copy-start.3 = (f32[16,152,128]{2,1,0:T(8,128)S(1)}, f32[16,152,128]{2,1,0:T(8,128)}, u32[]{:S(2)}) copy-start(f32[16,152,128]{2,1,0:T(8,128)} %get-tuple-element.61) | copy-start | bytes 3735556
  162.0 49.5 %collective-permute-start.15 = (bf16[2,400,1024]{2,1,0:T(8,128)(2,1)}, bf16[2,400,1024]{2,1,0:T(8,128)(2,1)S(1)}, u32[]{:S(2)}, u32[]{:S(2)}) collective-permute-start(bf16[2,400,1024]{2,1,0:T(8,128)(2,1)} %get-tuple-element.65), channel_id=1, source_target_pairs={{0,1},{1,0},{2,3},{3,2},{4,5},{5,4},{6,7},{7,6},{8,9},{9,8},{10,11... | collective-permute-start | bytes 4915208 | tf_op jit(solution)/shard_map/ppermute | solution.py:23
  166.7 9.2 %collective-permute-start.19 = (bf16[4,152,128]{2,1,0:T(8,128)(2,1)S(1)}, bf16[4,152,128]{2,1,0:T(8,128)(2,1)S(1)}, u32[]{:S(2)}, u32[]{:S(2)}) collective-permute-start(bf16[4,152,128]{2,1,0:T(8,128)(2,1)S(1)} %get-tuple-element.86), channel_id=1, source_target_pairs={{0,4},{4,0},{8,12},{12,8},{16,20},{20,16},{24,28},{28,24},{32,36},... | collective-permute-start | bytes 466952 | tf_op jit(solution)/shard_map/ppermute | solution.py:23
  170.2 5.9 %collective-permute-start.20 = (bf16[4,152,128]{2,1,0:T(8,128)(2,1)S(1)}, bf16[4,152,128]{2,1,0:T(8,128)(2,1)S(1)}, u32[]{:S(2)}, u32[]{:S(2)}) collective-permute-start(bf16[4,152,128]{2,1,0:T(8,128)(2,1)S(1)} %get-tuple-element.88), channel_id=1, source_target_pairs={{0,8},{4,12},{8,0},{12,4},{16,24},{20,28},{24,16},{28,20},{32,40},... | collective-permute-start | bytes 466952 | tf_op jit(solution)/shard_map/ppermute | solution.py:23
  170.2 7.0 %collective-permute-start.21 = (bf16[4,152,128]{2,1,0:T(8,128)(2,1)S(1)}, bf16[4,152,128]{2,1,0:T(8,128)(2,1)S(1)}, u32[]{:S(2)}, u32[]{:S(2)}) collective-permute-start(bf16[4,152,128]{2,1,0:T(8,128)(2,1)S(1)} %get-tuple-element.87), channel_id=1, source_target_pairs={{0,12},{4,8},{8,4},{12,0},{16,28},{20,24},{24,20},{28,16},{32,44},... | collective-permute-start | bytes 466952 | tf_op jit(solution)/shard_map/ppermute | solution.py:23
  172.7 21.6 %collective-permute-start.25 = (bf16[400,512]{1,0:T(8,128)(2,1)S(1)}, bf16[400,512]{1,0:T(8,128)(2,1)S(1)}, u32[]{:S(2)}, u32[]{:S(2)}) collective-permute-start(bf16[400,512]{1,0:T(8,128)(2,1)S(1)} %fusion.3), channel_id=1, source_target_pairs={{0,130},{1,131},{2,128},{3,129},{4,134},{5,135},{6,132},{7,133},{8... | collective-permute-start | bytes 1228808 | tf_op jit(solution)/shard_map/ppermute | solution.py:33
  175.8 35.6 %copy-start.1 = (f32[2,400,1024]{2,1,0:T(8,128)S(1)}, f32[2,400,1024]{2,1,0:T(8,128)}, u32[]{:S(2)}) copy-start(f32[2,400,1024]{2,1,0:T(8,128)} %get-tuple-element.64) | copy-start | bytes 9830404
  177.2 11.8 %collective-permute-start.22 = (f32[152,128]{1,0:T(8,128)S(1)}, f32[152,128]{1,0:T(8,128)S(1)}, u32[]{:S(2)}, u32[]{:S(2)}) collective-permute-start(f32[152,128]{1,0:T(8,128)S(1)} %get-tuple-element.91), channel_id=1, source_target_pairs={{0,16},{4,20},{8,24},{12,28},{16,0},{20,4},{24,8},{28,12},{32,48},... | collective-permute-start | bytes 233480 | tf_op jit(solution)/shard_map/ppermute | solution.py:23
  183.9 7.8 %collective-permute-start.23 = (f32[152,128]{1,0:T(8,128)S(1)}, f32[152,128]{1,0:T(8,128)S(1)}, u32[]{:S(2)}, u32[]{:S(2)}) collective-permute-start(f32[152,128]{1,0:T(8,128)S(1)} %get-tuple-element.90), channel_id=1, source_target_pairs={{0,32},{4,36},{8,40},{12,44},{16,48},{20,52},{24,56},{28,60},{32,0... | collective-permute-start | bytes 233480 | tf_op jit(solution)/shard_map/ppermute | solution.py:23
  189.1 5.1 %collective-permute-start.24 = (f32[152,128]{1,0:T(8,128)S(1)}, f32[152,128]{1,0:T(8,128)S(1)}, u32[]{:S(2)}, u32[]{:S(2)}) collective-permute-start(f32[152,128]{1,0:T(8,128)S(1)} %get-tuple-element.89), channel_id=1, source_target_pairs={{0,48},{4,52},{8,56},{12,60},{16,32},{20,36},{24,40},{28,44},{32,1... | collective-permute-start | bytes 233480 | tf_op jit(solution)/shard_map/ppermute | solution.py:23
  194.2 5.6 %collective-permute-start.26 = (f32[152,128]{1,0:T(8,128)S(1)}, f32[152,128]{1,0:T(8,128)S(1)}, u32[]{:S(2)}, u32[]{:S(2)}) collective-permute-start(f32[152,128]{1,0:T(8,128)S(1)} %fusion.10), channel_id=1, source_target_pairs={{0,2},{1,3},{2,0},{3,1},{4,6},{5,7},{6,4},{7,5},{8,10},{9,11},{10,... | collective-permute-start | bytes 233480 | tf_op jit(solution)/shard_map/ppermute | solution.py:23
  199.9 5.9 %collective-permute-start.27 = (f32[152,128]{1,0:T(8,128)S(1)}, f32[152,128]{1,0:T(8,128)S(1)}, u32[]{:S(2)}, u32[]{:S(2)}) collective-permute-start(f32[152,128]{1,0:T(8,128)S(1)} %add.101), channel_id=1, source_target_pairs={{0,64},{4,68},{8,72},{12,76},{16,80},{20,84},{24,88},{28,92},{32,9... | collective-permute-start | bytes 233480 | tf_op jit(solution)/shard_map/ppermute | solution.py:23
  200.0 7.9 %collective-permute-start.28 = (f32[152,128]{1,0:T(8,128)S(1)}, f32[152,128]{1,0:T(8,128)S(1)}, u32[]{:S(2)}, u32[]{:S(2)}) collective-permute-start(f32[152,128]{1,0:T(8,128)S(1)} %add.101), channel_id=1, source_target_pairs={{0,128},{4,132},{8,136},{12,140},{16,144},{20,148},{24,152},{28,15... | collective-permute-start | bytes 233480 | tf_op jit(solution)/shard_map/ppermute | solution.py:23
  202.6 8.8 %collective-permute-start.29 = (f32[152,128]{1,0:T(8,128)S(1)}, f32[152,128]{1,0:T(8,128)S(1)}, u32[]{:S(2)}, u32[]{:S(2)}) collective-permute-start(f32[152,128]{1,0:T(8,128)S(1)} %add.101), channel_id=1, source_target_pairs={{0,192},{4,196},{8,200},{12,204},{16,208},{20,212},{24,216},{28,22... | collective-permute-start | bytes 233480 | tf_op jit(solution)/shard_map/ppermute | solution.py:23
  212.3 16.7 %copy-start.17 = (f32[1345]{0:T(1024)S(1)}, f32[1345]{0:T(1024)}, u32[]{:S(2)}) copy-start(f32[1345]{0:T(1024)} %param.12) | copy-start | bytes 16144
  212.4 22.1 %collective-permute-start.30 = (bf16[400,1024]{1,0:T(8,128)(2,1)S(1)}, bf16[400,1024]{1,0:T(8,128)(2,1)S(1)}, u32[]{:S(2)}, u32[]{:S(2)}) collective-permute-start(bf16[400,1024]{1,0:T(8,128)(2,1)S(1)} %slice_bitcast_fusion), channel_id=1, source_target_pairs={{0,2},{1,3},{2,0},{3,1},{4,6},{5,7},{6,4},{7,5},{8,10},{9,11},{10,... | collective-permute-start | bytes 2457608 | tf_op jit(solution)/shard_map/ppermute | solution.py:23
  215.6 5.3 %collective-permute-start.31 = (bf16[152,128]{1,0:T(8,128)(2,1)S(1)}, bf16[152,128]{1,0:T(8,128)(2,1)S(1)}, u32[]{:S(2)}, u32[]{:S(2)}) collective-permute-start(bf16[152,128]{1,0:T(8,128)(2,1)S(1)} %add_convert_fusion), channel_id=1, source_target_pairs={{0,16},{4,20},{8,24},{12,28},{16,0},{20,4},{24,8},{28,12},{32,48},... | collective-permute-start | bytes 116744 | tf_op jit(solution)/shard_map/ppermute | solution.py:23
  215.6 7.1 %collective-permute-start.32 = (bf16[152,128]{1,0:T(8,128)(2,1)S(1)}, bf16[152,128]{1,0:T(8,128)(2,1)S(1)}, u32[]{:S(2)}, u32[]{:S(2)}) collective-permute-start(bf16[152,128]{1,0:T(8,128)(2,1)S(1)} %add_convert_fusion), channel_id=1, source_target_pairs={{0,32},{4,36},{8,40},{12,44},{16,48},{20,52},{24,56},{28,60},{32,0... | collective-permute-start | bytes 116744 | tf_op jit(solution)/shard_map/ppermute | solution.py:23
  220.9 4.0 %collective-permute-start.33 = (bf16[152,128]{1,0:T(8,128)(2,1)S(1)}, bf16[152,128]{1,0:T(8,128)(2,1)S(1)}, u32[]{:S(2)}, u32[]{:S(2)}) collective-permute-start(bf16[152,128]{1,0:T(8,128)(2,1)S(1)} %add_convert_fusion), channel_id=1, source_target_pairs={{0,48},{4,52},{8,56},{12,60},{16,32},{20,36},{24,40},{28,44},{32,1... | collective-permute-start | bytes 116744 | tf_op jit(solution)/shard_map/ppermute | solution.py:23
  225.0 4.5 %collective-permute-start.34 = (bf16[4,152,128]{2,1,0:T(8,128)(2,1)S(1)}, bf16[4,152,128]{2,1,0:T(8,128)(2,1)S(1)}, u32[]{:S(2)}, u32[]{:S(2)}) collective-permute-start(bf16[4,152,128]{2,1,0:T(8,128)(2,1)S(1)} %get-tuple-element.93), channel_id=1, source_target_pairs={{0,4},{4,0},{8,12},{12,8},{16,20},{20,16},{24,28},{28,24},{32,36},... | collective-permute-start | bytes 466952 | tf_op jit(solution)/shard_map/ppermute | solution.py:23
  225.1 6.9 %collective-permute-start.35 = (bf16[4,152,128]{2,1,0:T(8,128)(2,1)S(1)}, bf16[4,152,128]{2,1,0:T(8,128)(2,1)S(1)}, u32[]{:S(2)}, u32[]{:S(2)}) collective-permute-start(bf16[4,152,128]{2,1,0:T(8,128)(2,1)S(1)} %get-tuple-element.93), channel_id=1, source_target_pairs={{0,8},{4,12},{8,0},{12,4},{16,24},{20,28},{24,16},{28,20},{32,40},... | collective-permute-start | bytes 466952 | tf_op jit(solution)/shard_map/ppermute | solution.py:23
  225.3 9.1 %collective-permute-start.36 = (bf16[4,152,128]{2,1,0:T(8,128)(2,1)S(1)}, bf16[4,152,128]{2,1,0:T(8,128)(2,1)S(1)}, u32[]{:S(2)}, u32[]{:S(2)}) collective-permute-start(bf16[4,152,128]{2,1,0:T(8,128)(2,1)S(1)} %get-tuple-element.93), channel_id=1, source_target_pairs={{0,12},{4,8},{8,4},{12,0},{16,28},{20,24},{24,20},{28,16},{32,44},... | collective-permute-start | bytes 466952 | tf_op jit(solution)/shard_map/ppermute | solution.py:23
  234.5 2.7 %copy-start.2 = (bf16[4,4,152,128]{3,2,1,0:T(8,128)(2,1)}, bf16[4,4,152,128]{3,2,1,0:T(8,128)(2,1)S(1)}, u32[]{:S(2)}) copy-start(bf16[4,4,152,128]{3,2,1,0:T(8,128)(2,1)S(1)} %pad_maximum_fusion.1.near_ref) | copy-start | bytes 1867780
  234.5 2.7 %copy-start.19 = (f32[1024]{0:T(1024)S(1)}, f32[1024]{0:T(1024)}, u32[]{:S(2)}) copy-start(f32[1024]{0:T(1024)} %param.10) | copy-start | bytes 12292
  234.5 5.8 %collective-permute-start.37 = (bf16[4,4,152,128]{3,2,1,0:T(8,128)(2,1)S(1)}, bf16[4,4,152,128]{3,2,1,0:T(8,128)(2,1)S(1)}, u32[]{:S(2)}, u32[]{:S(2)}) collective-permute-start(bf16[4,4,152,128]{3,2,1,0:T(8,128)(2,1)S(1)} %pad_maximum_fusion.1.near_ref), channel_id=1, source_target_pairs={{0,1},{1,0},{2,3},{3,2},{4,5},{5,4},{6,7},{7,6},{8,9},{9,8},{10,11... | collective-permute-start | bytes 1867784 | tf_op jit(solution)/shard_map/ppermute | solution.py:23
  (10 other events, 10.3 us)

commit v4 on v3

--- a/solution.py
+++ b/solution.py
@@ -178,10 +178,11 @@
 
 def target_kernel(order, rows, scal, s_ref, r_ref, gun_ref, idx_ref, *refs):
     gn_ref, n_idx_ref, tables = refs[0], refs[1], refs[2 : 2 + len(order)]
-    gs_ref, gr_ref, keep_ref, send_ref, t_acc, gt_scr, acc = refs[2 + len(order) :]
+    gs_ref, gr_ref, *keep_refs = refs[2 + len(order) : 6 + len(order)]
+    *send_refs, t_acc, gt_scr, acc = refs[6 + len(order) :]
     i = pl.program_id(0)
     parts = 2 * acc.shape[0]
-    sums = [(keep_ref, acc)[apart % 2].at[apart // 2] for apart in range(parts)]
+    sums = [acc.at[k // 2] if k % 2 else keep_refs[k // 2] for k in range(parts)]
     bases = [(scal[1] ^ apart) * rows for apart in range(parts)]
 
     @pl.when(i == 0)
@@ -227,7 +228,8 @@
 
     @pl.when(i == pl.num_programs(0) - 1)
     def _():
-        send_ref[...] = acc[...].astype(BF16)
+        for k, send_ref in enumerate(send_refs):
+            send_ref[...] = acc[k].astype(BF16)
 
 
 def relation_scatter_kernel(scal, g_ref, idx_ref, keep_ref, send_ref, acc):
@@ -465,7 +467,8 @@
     slots = -(-(width // SUBLANES * wide // 2 // LANES) // cells)
     packed = (2, cells, slots * SUBLANES, LANES)
     half_parts = (reps // 2, width, quarter)
-    grad_s, grad_r, dst_keep, dst_send = call(
+    part = (width, quarter)
+    grad_s, grad_r, keep_on, keep_back, send_on, send_back = call(
         functools.partial(target_kernel, order, quarter),
         "targets",
         edges // BLOCK,
@@ -473,8 +476,8 @@
         + [edge_block(1)]
         + [whole((width, n_neg)), whole((1, n_neg))]
         + [whole(t.shape) for t in tables],
-        [edge_block(width)] * 2 + [whole(half_parts)] * 2,
-        [bf16_of(width, edges)] * 2 + [f32_of(*half_parts), bf16_of(*half_parts)],
+        [edge_block(width)] * 2 + [whole(part)] * 4,
+        [bf16_of(width, edges)] * 2 + [f32_of(*part)] * 2 + [bf16_of(*part)] * 2,
         [
             pltpu.VMEM((width, BLOCK), F32),
             pltpu.VMEM((width, BLOCK), BF16),
@@ -489,7 +492,8 @@
         neg_idx,
         *tables,
     )
-    dst_sum = dst_keep + swapped(dst_send, "rep", 1).astype(F32)
+    on = (keep_on + swapped(send_on, "rep", 1).astype(F32)).astype(BF16)
+    sent = [swapped(on[:, k * step : (k + 1) * step], "rep", 2) for k in range(PIECES)]
     rel_keep, rel_send = call(
         relation_scatter_kernel,
         "relation_grads",
@@ -499,15 +503,12 @@
         [f32_of(*packed[1:])] * 2,
         [pltpu.VMEM((width, wide), F32)],
         scal,
-        after(grad_r, dst_sum),
+        after(grad_r, on),
         rel,
         flops=2 * width * wide * edges,
     )
-    sent = [
-        swapped(dst_sum[0, :, k * step : (k + 1) * step].astype(BF16), "rep", 2)
-        for k in range(PIECES)
-    ]
-    first = dst_sum[1, :, :step] + after(sent[0], rel_keep).astype(F32)
+    back = keep_back + after(swapped(send_back, "rep", 1), rel_keep).astype(F32)
+    first = back[:, :step] + after(sent[0], rel_keep).astype(F32)
     first = first.astype(BF16)
     returned = [swapped_far(first, half, 2)]
     src_keep, src_send = call(
@@ -524,7 +525,7 @@
         flops=width * rows_part * edges,
     )
 
-    last = dst_sum[1, :, step:] + after(sent[1], src_keep).astype(F32)
+    last = back[:, step:] + after(sent[1], src_keep).astype(F32)
     last = last.astype(BF16)
     returned.append(swapped_far(last, half, 2))
 
@@ -534,7 +535,8 @@
     cell = summed(line, "dom", 4)
     cell = after(cell, *returned[1:])
     cell = cell + swapped(cell, "rep", 2)
-    total = summed([cell] * 4, "dom", 16).astype(BF16)
+    cell = cell + swapped(cell, "dom", 16)
+    total = (cell + swapped(cell, "dom", 32)).astype(BF16)
     src_sum = src_keep + swapped(src_send, "rep", 1).astype(F32)
     src_got = swapped(after(src_sum[1], total).astype(BF16), "rep", 2)
     line = collected(total, "dom", 4)

time: 250 us -> 252 us (level)
  Pallas kernels: 86.7 us -> 91 us
    ppermute x5, starting transfers between devices: 19.1 us -> 9.32 us  [swapped_far(): return lax.ppermute(x, ('dom', 'rep'), pairs)]
    ppermute x33, starting transfers between devices: 78.2 us -> 86.4 us  [swapped(): lax.ppermute(x, axis, [(i, i ^ mask) for i in range(lax.axis_size(axis))])]
    pallas_call x8, Pallas kernels: 86.7 us -> 91 us  [call(): pl.pallas_call(kernel, grid_spec=pltpu.PrefetchScalarGridSpec(num_scalar_...]
    another operation x1 -> x0, other arithmetic: 2.64 us -> none
  transfers between devices with their start and end apart: 38 -> 38, of which waited for: 16 -> 18; matrix products, arithmetic and copies ran while one was open for 8% -> 9% of each run, Pallas kernels for 23% -> 24%
where the time goes in v4:
time: 252 us; the launch traced here: 249 us
  starting transfers between devices  95.8 us (38%)
  Pallas kernels  91 us (36%)
  waiting for transfers between devices  33.6 us (13%)
  other arithmetic  19.3 us (8%)
  local copies, waits for them, and re-layouts  7.85 us (3%)
    pallas_call x8, Pallas kernels, call(): pl.pallas_call(kernel, grid_spec=pltpu.PrefetchScalarGridSpec(num_scalar_...  91 us
    ppermute x33, starting transfers between devices, swapped(): lax.ppermute(x, axis, [(i, i ^ mask) for i in range(lax.axis_size(axis))])  86.4 us
    ppermute x33, waiting for transfers between devices, swapped(): lax.ppermute(x, axis, [(i, i ^ mask) for i in range(lax.axis_size(axis))])  28.6 us
    ppermute x5, starting transfers between devices, swapped_far(): return lax.ppermute(x, ('dom', 'rep'), pairs)  9.32 us
    sort x1, other arithmetic, body(): lax.sort((key, edge_source, edge_target, edge_relation), num_keys=1)  6 us
  transfers between devices with their start and end apart: 38, of which 18 were waited for; matrix products, arithmetic and copies ran while one was open for 9% of the time, Pallas kernels for 24%

profile of v4, /device:TPU:1, one launch (start us, length us, event | category | flops | bytes accessed | tf_op | source)
XLA Modules:
  0.0 249.4 jit_solution(13793280129535133380)
XLA Ops:
  0.6 7.8 %collective-permute-start = (s32[1024]{0:T(1024)}, s32[1024]{0:T(1024)S(1)}, u32[]{:S(2)}, u32[]{:S(2)}) collective-permute-start(s32[1024]{0:T(1024)} %param.17), channel_id=1, source_target_pairs={{0,128},{4,132},{8,136},{12,140},{16,144},{20,148},{24,152},{28,15... | collective-permute-start | bytes 12296 | tf_op jit(solution)/shard_map/ppermute | solution.py:23
  8.5 1.3 dynamic-slice_bitcast_fusion
  11.4 6.0 %sort.39 = (s32[4096]{0:T(1024)}, s32[4096]{0:T(1024)S(1)}, s32[4096]{0:T(1024)S(1)}, s32[4096]{0:T(1024)}, s32[4096]{0:T(1024)}) sort(s32[4096]{0:T(1024)S(1)} %fusion.13, s32[4096]{0:T(1024)S(1)} %copy-done.14, s32[4096]{0:T(1024)S(1)} %copy-done.15, s32[4096]{0:T(1024)S(1)} %copy-done.17, s32[4096]{0:T(1024)S(1)} %iota.25), dimensions={0}, to_apply=%region_0.1 | sort | flops 49152 | bytes 163840 | tf_op jit(solution)/shard_map/sort | solution.py:373
  17.4 1.7 pad_maximum_fusion.table_ref
  20.5 4.3 %partner_negatives.1 = bf16[400,256]{1,0:T(8,128)(2,1)} custom-call(s32[3]{0:T(128)} %pad_add_fusion.3.scal, s32[1,256]{1,0:T(1,128)} %bitcast.99, bf16[400,4096]{1,0:T(8,128)(2,1)} %bitcast.77), custom_call_target="tpu_custom_call" | custom-call | tf_op jit(solution)/shard_map/partner_negatives/pallas_call | solution.py:50
  25.9 4.2 %collective-permute-start.1 = (bf16[400,256]{0,1:T(8,128)(2,1)S(1)}, bf16[400,256]{0,1:T(8,128)(2,1)S(1)}, u32[]{:S(2)}, u32[]{:S(2)}) collective-permute-start(bf16[400,256]{0,1:T(8,128)(2,1)S(1)} %copy.21), channel_id=1, source_target_pairs={{0,130},{1,131},{2,128},{3,129},{4,134},{5,135},{6,132},{7,133},{8... | collective-permute-start | bytes 614408 | tf_op jit(solution)/shard_map/ppermute | solution.py:33
  31.3 10.6 %source_rows.1.s_ref = bf16[400,4096]{1,0:T(8,128)(2,1)} custom-call(s32[67]{0:T(128)} %pad_add_fusion.2.scal, s32[1,4096]{1,0:T(1,128)} %bitcast.90, bf16[400,4096]{1,0:T(8,128)(2,1)} %bitcast.78), custom_call_target="tpu_custom_call" | custom-call | tf_op jit(solution)/shard_map/source_rows/pallas_call | solution.py:50
  43.2 11.1 %relation_rows.1.r_ref = f32[400,4096]{1,0:T(8,128)} custom-call(s32[67]{0:T(128)} %pad_add_fusion.2.scal, s32[1,4096]{1,0:T(1,128)} %bitcast.96, bf16[800,1536]{1,0:T(8,128)(2,1)} %pad_maximum_fusion.table_ref), custom_call_target="tpu_custom_call" | custom-call | tf_op jit(solution)/shard_map/relation_rows/pallas_call | solution.py:50
  54.3 3.4 %collective-permute-start.3 = (bf16[400,256]{0,1:T(8,128)(2,1)S(1)}, bf16[400,256]{0,1:T(8,128)(2,1)S(1)}, u32[]{:S(2)}, u32[]{:S(2)}) collective-permute-start(bf16[400,256]{0,1:T(8,128)(2,1)S(1)} %collective-permute-done.1), channel_id=1, source_target_pairs={{0,1},{1,0},{2,3},{3,2},{4,5},{5,4},{6,7},{7,6},{8,9},{9,8},{10,11... | collective-permute-start | bytes 614408 | tf_op jit(solution)/shard_map/ppermute | solution.py:23
  57.7 13.9 %collective-permute-start.7 = (bf16[400,512]{1,0:T(8,128)(2,1)}, bf16[400,512]{1,0:T(8,128)(2,1)S(1)}, u32[]{:S(2)}, u32[]{:S(2)}) collective-permute-start(bf16[400,512]{1,0:T(8,128)(2,1)} %collective-permute-done.5.refs_2_), channel_id=1, source_target_pairs={{0,2},{1,3},{2,0},{3,1},{4,6},{5,7},{6,4},{7,5},{8,10},{9,11},{10,... | collective-permute-start | bytes 1228808 | tf_op jit(solution)/shard_map/ppermute | solution.py:23
  74.1 1.2 copy.22.neg_t_ref
  76.4 14.8 %negative_scores.1 = (f32[400,4096]{1,0:T(8,128)}, bf16[400,1024]{1,0:T(8,128)(2,1)}) custom-call(s32[67]{0:T(128)} %pad_add_fusion.2.scal, bf16[400,4096]{1,0:T(8,128)(2,1)} %source_rows.1.s_ref, f32[400,4096]{1,0:T(8,128)} %relation_rows.1.r_ref, bf16[400,1024]{1,0:T(8,128)(2,1)} %copy.22.neg_t_ref, bf16[1024,400]{1,0:T(8,128)(2,1)} %multiply_bitcast_fusion.half_neg_ref), custom_call_target="tpu_custom_call" | custom-call | tf_op jit(solution)/shard_map/negative_scores/pallas_call | solution.py:50
  94.4 25.6 %targets.1 = (bf16[400,4096]{1,0:T(8,128)(2,1)}, bf16[400,4096]{1,0:T(8,128)(2,1)}, f32[400,1024]{1,0:T(8,128)}, f32[400,1024]{1,0:T(8,128)}, bf16[400,1024]{1,0:T(8,128)(2,1)}, /*index=5*/bf16[400,1024]{1,0:T(8,128)(2,1)}) custom-call(s32[67]{0:T(128)} %pad_add_fusion.2.scal, bf16[400,4096]{1,0:T(8,128)(2,1)} %source_rows.1.s_ref, ...), custom_call_target="tpu_custom_call" | custom-call | tf_op jit(solution)/shard_map/targets/pallas_call | solution.py:50
  120.6 2.0 collective-permute-done.14
  122.6 1.7 add_convert_fusion
  124.4 6.8 %collective-permute-start.15 = (bf16[400,512]{1,0:T(8,128)(2,1)S(1)}, bf16[400,512]{1,0:T(8,128)(2,1)S(1)}, u32[]{:S(2)}, u32[]{:S(2)}) collective-permute-start(bf16[400,512]{1,0:T(8,128)(2,1)S(1)} %get-tuple-element.86), channel_id=1, source_target_pairs={{0,2},{1,3},{2,0},{3,1},{4,6},{5,7},{6,4},{7,5},{8,10},{9,11},{10,... | collective-permute-start | bytes 1228808 | tf_op jit(solution)/shard_map/ppermute | solution.py:23
  131.2 7.8 %relation_grads.1 = (f32[16,152,128]{2,1,0:T(8,128)}, f32[16,152,128]{2,1,0:T(8,128)}) custom-call(s32[67]{0:T(128)} %pad_add_fusion.2.scal, bf16[400,4096]{1,0:T(8,128)(2,1)} %get-tuple-element.65.g_ref, s32[1,4096]{1,0:T(1,128)} %bitcast.97), custom_call_target="tpu_custom_call" | custom-call | flops 5033164800 | tf_op jit(solution)/shard_map/relation_grads/pallas_call | solution.py:50
  139.0 2.0 collective-permute-start.19
  142.0 12.3 %source_grads.1 = (f32[2,400,1024]{2,1,0:T(8,128)}, bf16[2,400,1024]{2,1,0:T(8,128)(2,1)}) custom-call(s32[67]{0:T(128)} %pad_add_fusion.2.scal, bf16[400,4096]{1,0:T(8,128)(2,1)} %get-tuple-element.69.g_ref, s32[1,4096]{1,0:T(1,128)} %bitcast.91), custom_call_target="tpu_custom_call" | custom-call | flops 6710886400 | tf_op jit(solution)/shard_map/source_grads/pallas_call | solution.py:50
  155.9 6.1 %collective-permute-start.20 = (bf16[4,152,128]{2,1,0:T(8,128)(2,1)S(1)}, bf16[4,152,128]{2,1,0:T(8,128)(2,1)S(1)}, u32[]{:S(2)}, u32[]{:S(2)}) collective-permute-start(bf16[4,152,128]{2,1,0:T(8,128)(2,1)S(1)} %get-tuple-element.90), channel_id=1, source_target_pairs={{0,4},{4,0},{8,12},{12,8},{16,20},{20,16},{24,28},{28,24},{32,36},... | collective-permute-start | bytes 466952 | tf_op jit(solution)/shard_map/ppermute | solution.py:23
  162.0 10.4 %collective-permute-start.21 = (bf16[4,152,128]{2,1,0:T(8,128)(2,1)S(1)}, bf16[4,152,128]{2,1,0:T(8,128)(2,1)S(1)}, u32[]{:S(2)}, u32[]{:S(2)}) collective-permute-start(bf16[4,152,128]{2,1,0:T(8,128)(2,1)S(1)} %get-tuple-element.92), channel_id=1, source_target_pairs={{0,8},{4,12},{8,0},{12,4},{16,24},{20,28},{24,16},{28,20},{32,40},... | collective-permute-start | bytes 466952 | tf_op jit(solution)/shard_map/ppermute | solution.py:23
  172.5 4.6 %collective-permute-start.26 = (bf16[400,512]{1,0:T(8,128)(2,1)S(1)}, bf16[400,512]{1,0:T(8,128)(2,1)S(1)}, u32[]{:S(2)}, u32[]{:S(2)}) collective-permute-start(bf16[400,512]{1,0:T(8,128)(2,1)S(1)} %fusion.2), channel_id=1, source_target_pairs={{0,130},{1,131},{2,128},{3,129},{4,134},{5,135},{6,132},{7,133},{8... | collective-permute-start | bytes 1228808 | tf_op jit(solution)/shard_map/ppermute | solution.py:33
  177.2 1.7 collective-permute-done.21
  178.9 2.7 %collective-permute-done.22 = bf16[4,152,128]{2,1,0:T(8,128)(2,1)S(1)} collective-permute-done((bf16[4,152,128]{2,1,0:T(8,128)(2,1)S(1)}, bf16[4,152,128]{2,1,0:T(8,128)(2,1)S(1)}, u32[]{:S(2)}, u32[]{:S(2)}) %collective-permute-start.22) | collective-permute-done | bytes 155680 | tf_op jit(solution)/shard_map/ppermute | solution.py:23
  181.8 1.2 collective-permute-start.23
  182.9 2.6 %collective-permute-start.24 = (f32[152,128]{1,0:T(8,128)S(1)}, f32[152,128]{1,0:T(8,128)S(1)}, u32[]{:S(2)}, u32[]{:S(2)}) collective-permute-start(f32[152,128]{1,0:T(8,128)S(1)} %get-tuple-element.94), channel_id=1, source_target_pairs={{0,32},{4,36},{8,40},{12,44},{16,48},{20,52},{24,56},{28,60},{32,0... | collective-permute-start | bytes 233480 | tf_op jit(solution)/shard_map/ppermute | solution.py:23
  185.7 3.0 %collective-permute-done.24 = f32[152,128]{1,0:T(8,128)S(1)} collective-permute-done((f32[152,128]{1,0:T(8,128)S(1)}, f32[152,128]{1,0:T(8,128)S(1)}, u32[]{:S(2)}, u32[]{:S(2)}) %collective-permute-start.24) | collective-permute-done | bytes 77856 | tf_op jit(solution)/shard_map/ppermute | solution.py:23
  188.7 1.9 collective-permute-done.25
  190.7 3.1 %collective-permute-done.26 = bf16[400,512]{1,0:T(8,128)(2,1)S(1)} collective-permute-done((bf16[400,512]{1,0:T(8,128)(2,1)S(1)}, bf16[400,512]{1,0:T(8,128)(2,1)S(1)}, u32[]{:S(2)}, u32[]{:S(2)}) %collective-permute-start.26) | collective-permute-done | bytes 409632 | tf_op jit(solution)/shard_map/ppermute | solution.py:33
  193.8 2.0 collective-permute-start.27
  195.8 1.8 collective-permute-done.27
  197.6 2.3 collective-permute-start.28
  199.8 2.0 collective-permute-done.28
  201.8 4.8 %collective-permute-start.29 = (f32[152,128]{1,0:T(8,128)S(1)}, f32[152,128]{1,0:T(8,128)S(1)}, u32[]{:S(2)}, u32[]{:S(2)}) collective-permute-start(f32[152,128]{1,0:T(8,128)S(1)} %add.103), channel_id=1, source_target_pairs={{0,128},{4,132},{8,136},{12,140},{16,144},{20,148},{24,152},{28,15... | collective-permute-start | bytes 233480 | tf_op jit(solution)/shard_map/ppermute | solution.py:23
  206.6 3.3 %collective-permute-done.29 = f32[152,128]{1,0:T(8,128)S(1)} collective-permute-done((f32[152,128]{1,0:T(8,128)S(1)}, f32[152,128]{1,0:T(8,128)S(1)}, u32[]{:S(2)}, u32[]{:S(2)}) %collective-permute-start.29) | collective-permute-done | bytes 77856 | tf_op jit(solution)/shard_map/ppermute | solution.py:23
  210.9 1.6 collective-permute-start.30
  212.5 1.4 collective-permute-start.31
  213.9 2.2 collective-permute-start.32
  216.4 1.9 collective-permute-done.32
  218.2 1.9 collective-permute-done.33
  220.2 1.5 collective-permute-start.34
  221.7 1.5 collective-permute-start.35
  224.8 2.7 %collective-permute-done.35 = bf16[4,152,128]{2,1,0:T(8,128)(2,1)S(1)} collective-permute-done((bf16[4,152,128]{2,1,0:T(8,128)(2,1)S(1)}, bf16[4,152,128]{2,1,0:T(8,128)(2,1)S(1)}, u32[]{:S(2)}, u32[]{:S(2)}) %collective-permute-start.35) | collective-permute-done | bytes 155680 | tf_op jit(solution)/shard_map/ppermute | solution.py:23
  227.5 1.6 collective-permute-done.36
  229.2 9.7 %collective-permute-start.37 = (bf16[4,4,152,128]{3,2,1,0:T(8,128)(2,1)S(1)}, bf16[4,4,152,128]{3,2,1,0:T(8,128)(2,1)S(1)}, u32[]{:S(2)}, u32[]{:S(2)}) collective-permute-start(bf16[4,4,152,128]{3,2,1,0:T(8,128)(2,1)S(1)} %pad_maximum_fusion.1.near_ref), channel_id=1, source_target_pairs={{0,1},{1,0},{2,3},{3,2},{4,5},{5,4},{6,7},{7,6},{8,9},{9,8},{10,11... | collective-permute-start | bytes 1867784 | tf_op jit(solution)/shard_map/ppermute | solution.py:23
  239.9 2.6 %fusion.4 = bf16[1024,400]{0,1:T(8,128)(2,1)} fusion(f32[1024]{0:T(1024)S(1)} %get-tuple-element.84, bf16[400,512]{1,0:T(8,128)(2,1)S(1)} %collective-permute-done.26, bf16[400,512]{1,0:T(8,128)(2,1)S(1)} %collective-permute-done.18, bf16[400,1024]{1,0:T(8,128)(2,1)S(1)} %collective-permute-done.30, f32[2,400,1024]{2,1,0:T(8,128)S(1)} %convert_add_fusion, ...), kind=kLoop, calls=%fused_computation.19 | loop fusion | flops 4915200 | bytes 4919300 | tf_op jit(solution)/shard_map/transpose | solution.py:565
  243.3 4.6 %relation_update.1 = (f32[400,1345]{1,0:T(8,128)}, f32[1,1345]{1,0:T(1,128)}) custom-call(s32[3]{0:T(128)} %pad_add_fusion.3.scal, f32[400,1345]{1,0:T(8,128)} %bitcast.79, f32[1,1345]{1,0:T(1,128)} %reshape.55.state_ref, bf16[4,4,152,128]{3,2,1,0:T(8,128)(2,1)} %copy-done.2, bf16[4,4,152,128]{3,2,1,0:T(8,128)(2,1)} %copy-done.5), custom_call_target="tpu_custom_call" | custom-call | tf_op jit(solution)/shard_map/relation_update/pallas_call | solution.py:50
  247.9 1.3 reduce
  (128 shorter events, 21.0 us)
Async XLA Ops:
  0.6 19.3 %collective-permute-start = (s32[1024]{0:T(1024)}, s32[1024]{0:T(1024)S(1)}, u32[]{:S(2)}, u32[]{:S(2)}) collective-permute-start(s32[1024]{0:T(1024)} %param.17), channel_id=1, source_target_pairs={{0,128},{4,132},{8,136},{12,140},{16,144},{20,148},{24,152},{28,15... | collective-permute-start | bytes 12296 | tf_op jit(solution)/shard_map/ppermute | solution.py:23
  8.5 1.9 copy-start
  9.9 47.8 %collective-permute-start.5 = (bf16[400,512]{1,0:T(8,128)(2,1)S(1)}, bf16[400,512]{1,0:T(8,128)(2,1)}, u32[]{:S(2)}, u32[]{:S(2)}) collective-permute-start(bf16[400,512]{1,0:T(8,128)(2,1)S(1)} %get-tuple-element.89), channel_id=1, source_target_pairs={{0,130},{1,131},{2,128},{3,129},{4,134},{5,135},{6,132},{7,133},{8... | collective-permute-start | bytes 1228808 | tf_op jit(solution)/shard_map/ppermute | solution.py:33
  25.9 16.8 %collective-permute-start.1 = (bf16[400,256]{0,1:T(8,128)(2,1)S(1)}, bf16[400,256]{0,1:T(8,128)(2,1)S(1)}, u32[]{:S(2)}, u32[]{:S(2)}) collective-permute-start(bf16[400,256]{0,1:T(8,128)(2,1)S(1)} %copy.21), channel_id=1, source_target_pairs={{0,130},{1,131},{2,128},{3,129},{4,134},{5,135},{6,132},{7,133},{8... | collective-permute-start | bytes 614408 | tf_op jit(solution)/shard_map/ppermute | solution.py:33
  30.1 42.3 %collective-permute-start.6 = (bf16[400,512]{1,0:T(8,128)(2,1)S(1)}, bf16[400,512]{1,0:T(8,128)(2,1)S(1)}, u32[]{:S(2)}, u32[]{:S(2)}) collective-permute-start(bf16[400,512]{1,0:T(8,128)(2,1)S(1)} %get-tuple-element.52), channel_id=1, source_target_pairs={{0,130},{1,131},{2,128},{3,129},{4,134},{5,135},{6,132},{7,133},{8... | collective-permute-start | bytes 1228808 | tf_op jit(solution)/shard_map/ppermute | solution.py:33
  42.7 29.7 %collective-permute-start.2 = (bf16[400,256]{0,1:T(8,128)(2,1)S(1)}, bf16[400,256]{0,1:T(8,128)(2,1)S(1)}, u32[]{:S(2)}, u32[]{:S(2)}) collective-permute-start(bf16[400,256]{0,1:T(8,128)(2,1)S(1)} %collective-permute-done.1), channel_id=1, source_target_pairs={{0,2},{1,3},{2,0},{3,1},{4,6},{5,7},{6,4},{7,5},{8,10},{9,11},{10,... | collective-permute-start | bytes 614408 | tf_op jit(solution)/shard_map/ppermute | solution.py:23
  54.3 18.3 %collective-permute-start.3 = (bf16[400,256]{0,1:T(8,128)(2,1)S(1)}, bf16[400,256]{0,1:T(8,128)(2,1)S(1)}, u32[]{:S(2)}, u32[]{:S(2)}) collective-permute-start(bf16[400,256]{0,1:T(8,128)(2,1)S(1)} %collective-permute-done.1), channel_id=1, source_target_pairs={{0,1},{1,0},{2,3},{3,2},{4,5},{5,4},{6,7},{7,6},{8,9},{9,8},{10,11... | collective-permute-start | bytes 614408 | tf_op jit(solution)/shard_map/ppermute | solution.py:23
  57.7 33.4 %collective-permute-start.7 = (bf16[400,512]{1,0:T(8,128)(2,1)}, bf16[400,512]{1,0:T(8,128)(2,1)S(1)}, u32[]{:S(2)}, u32[]{:S(2)}) collective-permute-start(bf16[400,512]{1,0:T(8,128)(2,1)} %collective-permute-done.5.refs_2_), channel_id=1, source_target_pairs={{0,2},{1,3},{2,0},{3,1},{4,6},{5,7},{6,4},{7,5},{8,10},{9,11},{10,... | collective-permute-start | bytes 1228808 | tf_op jit(solution)/shard_map/ppermute | solution.py:23
  71.6 20.8 %collective-permute-start.9 = (bf16[400,512]{1,0:T(8,128)(2,1)}, bf16[400,512]{1,0:T(8,128)(2,1)S(1)}, u32[]{:S(2)}, u32[]{:S(2)}) collective-permute-start(bf16[400,512]{1,0:T(8,128)(2,1)} %collective-permute-done.5.refs_2_), channel_id=1, source_target_pairs={{0,1},{1,0},{2,3},{3,2},{4,5},{5,4},{6,7},{7,6},{8,9},{9,8},{10,11... | collective-permute-start | bytes 1228808 | tf_op jit(solution)/shard_map/ppermute | solution.py:23
  72.4 1.6 collective-permute-start.4
  72.4 2.9 %copy-start.6 = (bf16[400,512]{1,0:T(8,128)(2,1)}, bf16[400,512]{1,0:T(8,128)(2,1)S(1)}, u32[]{:S(2)}) copy-start(bf16[400,512]{1,0:T(8,128)(2,1)S(1)} %collective-permute-done.6.refs_3_) | copy-start | bytes 1228804
  72.4 18.8 %collective-permute-start.8 = (bf16[400,512]{1,0:T(8,128)(2,1)S(1)}, bf16[400,512]{1,0:T(8,128)(2,1)S(1)}, u32[]{:S(2)}, u32[]{:S(2)}) collective-permute-start(bf16[400,512]{1,0:T(8,128)(2,1)S(1)} %collective-permute-done.6.refs_3_), channel_id=1, source_target_pairs={{0,2},{1,3},{2,0},{3,1},{4,6},{5,7},{6,4},{7,5},{8,10},{9,11},{10,... | collective-permute-start | bytes 1228808 | tf_op jit(solution)/shard_map/ppermute | solution.py:23
  72.6 19.9 %collective-permute-start.10 = (bf16[400,512]{1,0:T(8,128)(2,1)S(1)}, bf16[400,512]{1,0:T(8,128)(2,1)S(1)}, u32[]{:S(2)}, u32[]{:S(2)}) collective-permute-start(bf16[400,512]{1,0:T(8,128)(2,1)S(1)} %collective-permute-done.6.refs_3_), channel_id=1, source_target_pairs={{0,1},{1,0},{2,3},{3,2},{4,5},{5,4},{6,7},{7,6},{8,9},{9,8},{10,11... | collective-permute-start | bytes 1228808 | tf_op jit(solution)/shard_map/ppermute | solution.py:23
  76.4 15.4 %copy-start.19 = (s32[1024]{0:T(1024)S(1)}, s32[1024]{0:T(1024)}, u32[]{:S(2)}) copy-start(s32[1024]{0:T(1024)} %param.17) | copy-start | bytes 12292
  91.2 2.4 copy-start.7
  91.2 1.8 collective-permute-start.11
  91.3 2.3 copy-start.9
  91.3 2.3 collective-permute-start.12
  120.0 2.6 %collective-permute-start.14 = (bf16[400,1024]{1,0:T(8,128)(2,1)}, bf16[400,1024]{1,0:T(8,128)(2,1)S(1)}, u32[]{:S(2)}, u32[]{:S(2)}) collective-permute-start(bf16[400,1024]{1,0:T(8,128)(2,1)} %get-tuple-element.64), channel_id=1, source_target_pairs={{0,1},{1,0},{2,3},{3,2},{4,5},{5,4},{6,7},{7,6},{8,9},{9,8},{10,11... | collective-permute-start | bytes 2457608 | tf_op jit(solution)/shard_map/ppermute | solution.py:23
  120.1 18.9 %collective-permute-start.13 = (bf16[400,1024]{1,0:T(8,128)(2,1)}, bf16[400,1024]{1,0:T(8,128)(2,1)S(1)}, u32[]{:S(2)}, u32[]{:S(2)}) collective-permute-start(bf16[400,1024]{1,0:T(8,128)(2,1)} %get-tuple-element.61), channel_id=1, source_target_pairs={{0,1},{1,0},{2,3},{3,2},{4,5},{5,4},{6,7},{7,6},{8,9},{9,8},{10,11... | collective-permute-start | bytes 2457608 | tf_op jit(solution)/shard_map/ppermute | solution.py:23
  124.4 17.0 %copy-start.3 = (f32[400,1024]{1,0:T(8,128)S(1)}, f32[400,1024]{1,0:T(8,128)}, u32[]{:S(2)}) copy-start(f32[400,1024]{1,0:T(8,128)} %get-tuple-element.60) | copy-start | bytes 4915204
  124.4 17.4 %collective-permute-start.15 = (bf16[400,512]{1,0:T(8,128)(2,1)S(1)}, bf16[400,512]{1,0:T(8,128)(2,1)S(1)}, u32[]{:S(2)}, u32[]{:S(2)}) collective-permute-start(bf16[400,512]{1,0:T(8,128)(2,1)S(1)} %get-tuple-element.86), channel_id=1, source_target_pairs={{0,2},{1,3},{2,0},{3,1},{4,6},{5,7},{6,4},{7,5},{8,10},{9,11},{10,... | collective-permute-start | bytes 1228808 | tf_op jit(solution)/shard_map/ppermute | solution.py:23
  139.0 15.3 %collective-permute-start.19 = (bf16[400,512]{1,0:T(8,128)(2,1)S(1)}, bf16[400,512]{1,0:T(8,128)(2,1)S(1)}, u32[]{:S(2)}, u32[]{:S(2)}) collective-permute-start(bf16[400,512]{1,0:T(8,128)(2,1)S(1)} %get-tuple-element.87), channel_id=1, source_target_pairs={{0,2},{1,3},{2,0},{3,1},{4,6},{5,7},{6,4},{7,5},{8,10},{9,11},{10,... | collective-permute-start | bytes 1228808 | tf_op jit(solution)/shard_map/ppermute | solution.py:23
  141.0 14.6 %collective-permute-start.17 = (f32[16,152,128]{2,1,0:T(8,128)}, f32[16,152,128]{2,1,0:T(8,128)S(1)}, u32[]{:S(2)}, u32[]{:S(2)}) collective-permute-start(f32[16,152,128]{2,1,0:T(8,128)} %get-tuple-element.72), channel_id=1, source_target_pairs={{0,1},{1,0},{2,3},{3,2},{4,5},{5,4},{6,7},{7,6},{8,9},{9,8},{10,11... | collective-permute-start | bytes 3735560 | tf_op jit(solution)/shard_map/ppermute | solution.py:23
  141.9 13.7 %collective-permute-start.18 = (bf16[400,512]{1,0:T(8,128)(2,1)S(1)}, bf16[400,512]{1,0:T(8,128)(2,1)S(1)}, u32[]{:S(2)}, u32[]{:S(2)}) collective-permute-start(bf16[400,512]{1,0:T(8,128)(2,1)S(1)} %fusion.3), channel_id=1, source_target_pairs={{0,130},{1,131},{2,128},{3,129},{4,134},{5,135},{6,132},{7,133},{8... | collective-permute-start | bytes 1228808 | tf_op jit(solution)/shard_map/ppermute | solution.py:33
  154.3 55.7 %collective-permute-start.16 = (bf16[2,400,1024]{2,1,0:T(8,128)(2,1)}, bf16[2,400,1024]{2,1,0:T(8,128)(2,1)S(1)}, u32[]{:S(2)}, u32[]{:S(2)}) collective-permute-start(bf16[2,400,1024]{2,1,0:T(8,128)(2,1)} %get-tuple-element.71), channel_id=1, source_target_pairs={{0,1},{1,0},{2,3},{3,2},{4,5},{5,4},{6,7},{7,6},{8,9},{9,8},{10,11... | collective-permute-start | bytes 4915208 | tf_op jit(solution)/shard_map/ppermute | solution.py:23
  155.9 21.3 %collective-permute-start.20 = (bf16[4,152,128]{2,1,0:T(8,128)(2,1)S(1)}, bf16[4,152,128]{2,1,0:T(8,128)(2,1)S(1)}, u32[]{:S(2)}, u32[]{:S(2)}) collective-permute-start(bf16[4,152,128]{2,1,0:T(8,128)(2,1)S(1)} %get-tuple-element.90), channel_id=1, source_target_pairs={{0,4},{4,0},{8,12},{12,8},{16,20},{20,16},{24,28},{28,24},{32,36},... | collective-permute-start | bytes 466952 | tf_op jit(solution)/shard_map/ppermute | solution.py:23
  162.0 16.9 %collective-permute-start.21 = (bf16[4,152,128]{2,1,0:T(8,128)(2,1)S(1)}, bf16[4,152,128]{2,1,0:T(8,128)(2,1)S(1)}, u32[]{:S(2)}, u32[]{:S(2)}) collective-permute-start(bf16[4,152,128]{2,1,0:T(8,128)(2,1)S(1)} %get-tuple-element.92), channel_id=1, source_target_pairs={{0,8},{4,12},{8,0},{12,4},{16,24},{20,28},{24,16},{28,20},{32,40},... | collective-permute-start | bytes 466952 | tf_op jit(solution)/shard_map/ppermute | solution.py:23
  172.4 9.3 %collective-permute-start.22 = (bf16[4,152,128]{2,1,0:T(8,128)(2,1)S(1)}, bf16[4,152,128]{2,1,0:T(8,128)(2,1)S(1)}, u32[]{:S(2)}, u32[]{:S(2)}) collective-permute-start(bf16[4,152,128]{2,1,0:T(8,128)(2,1)S(1)} %get-tuple-element.91), channel_id=1, source_target_pairs={{0,12},{4,8},{8,4},{12,0},{16,28},{20,24},{24,20},{28,16},{32,44},... | collective-permute-start | bytes 466952 | tf_op jit(solution)/shard_map/ppermute | solution.py:23
  172.5 21.2 %collective-permute-start.26 = (bf16[400,512]{1,0:T(8,128)(2,1)S(1)}, bf16[400,512]{1,0:T(8,128)(2,1)S(1)}, u32[]{:S(2)}, u32[]{:S(2)}) collective-permute-start(bf16[400,512]{1,0:T(8,128)(2,1)S(1)} %fusion.2), channel_id=1, source_target_pairs={{0,130},{1,131},{2,128},{3,129},{4,134},{5,135},{6,132},{7,133},{8... | collective-permute-start | bytes 1228808 | tf_op jit(solution)/shard_map/ppermute | solution.py:33
  177.1 32.8 %copy-start.1 = (f32[2,400,1024]{2,1,0:T(8,128)S(1)}, f32[2,400,1024]{2,1,0:T(8,128)}, u32[]{:S(2)}) copy-start(f32[2,400,1024]{2,1,0:T(8,128)} %get-tuple-element.70) | copy-start | bytes 9830404
  181.8 3.9 %collective-permute-start.23 = (f32[152,128]{1,0:T(8,128)S(1)}, f32[152,128]{1,0:T(8,128)S(1)}, u32[]{:S(2)}, u32[]{:S(2)}) collective-permute-start(f32[152,128]{1,0:T(8,128)S(1)} %get-tuple-element.95), channel_id=1, source_target_pairs={{0,16},{4,20},{8,24},{12,28},{16,0},{20,4},{24,8},{28,12},{32,48},... | collective-permute-start | bytes 233480 | tf_op jit(solution)/shard_map/ppermute | solution.py:23
  182.9 5.8 %collective-permute-start.24 = (f32[152,128]{1,0:T(8,128)S(1)}, f32[152,128]{1,0:T(8,128)S(1)}, u32[]{:S(2)}, u32[]{:S(2)}) collective-permute-start(f32[152,128]{1,0:T(8,128)S(1)} %get-tuple-element.94), channel_id=1, source_target_pairs={{0,32},{4,36},{8,40},{12,44},{16,48},{20,52},{24,56},{28,60},{32,0... | collective-permute-start | bytes 233480 | tf_op jit(solution)/shard_map/ppermute | solution.py:23
  185.5 5.1 %collective-permute-start.25 = (f32[152,128]{1,0:T(8,128)S(1)}, f32[152,128]{1,0:T(8,128)S(1)}, u32[]{:S(2)}, u32[]{:S(2)}) collective-permute-start(f32[152,128]{1,0:T(8,128)S(1)} %get-tuple-element.93), channel_id=1, source_target_pairs={{0,48},{4,52},{8,56},{12,60},{16,32},{20,36},{24,40},{28,44},{32,1... | collective-permute-start | bytes 233480 | tf_op jit(solution)/shard_map/ppermute | solution.py:23
  193.8 3.8 %collective-permute-start.27 = (f32[152,128]{1,0:T(8,128)S(1)}, f32[152,128]{1,0:T(8,128)S(1)}, u32[]{:S(2)}, u32[]{:S(2)}) collective-permute-start(f32[152,128]{1,0:T(8,128)S(1)} %fusion.8), channel_id=1, source_target_pairs={{0,2},{1,3},{2,0},{3,1},{4,6},{5,7},{6,4},{7,5},{8,10},{9,11},{10,... | collective-permute-start | bytes 233480 | tf_op jit(solution)/shard_map/ppermute | solution.py:23
  197.6 4.2 %collective-permute-start.28 = (f32[152,128]{1,0:T(8,128)S(1)}, f32[152,128]{1,0:T(8,128)S(1)}, u32[]{:S(2)}, u32[]{:S(2)}) collective-permute-start(f32[152,128]{1,0:T(8,128)S(1)} %add.102), channel_id=1, source_target_pairs={{0,64},{4,68},{8,72},{12,76},{16,80},{20,84},{24,88},{28,92},{32,9... | collective-permute-start | bytes 233480 | tf_op jit(solution)/shard_map/ppermute | solution.py:23
  201.8 8.1 %collective-permute-start.29 = (f32[152,128]{1,0:T(8,128)S(1)}, f32[152,128]{1,0:T(8,128)S(1)}, u32[]{:S(2)}, u32[]{:S(2)}) collective-permute-start(f32[152,128]{1,0:T(8,128)S(1)} %add.103), channel_id=1, source_target_pairs={{0,128},{4,132},{8,136},{12,140},{16,144},{20,148},{24,152},{28,15... | collective-permute-start | bytes 233480 | tf_op jit(solution)/shard_map/ppermute | solution.py:23
  210.7 13.4 %copy-start.18 = (f32[1345]{0:T(1024)S(1)}, f32[1345]{0:T(1024)}, u32[]{:S(2)}) copy-start(f32[1345]{0:T(1024)} %param.12) | copy-start | bytes 16144
  210.9 18.3 %collective-permute-start.30 = (bf16[400,1024]{1,0:T(8,128)(2,1)S(1)}, bf16[400,1024]{1,0:T(8,128)(2,1)S(1)}, u32[]{:S(2)}, u32[]{:S(2)}) collective-permute-start(bf16[400,1024]{1,0:T(8,128)(2,1)S(1)} %slice_bitcast_fusion), channel_id=1, source_target_pairs={{0,2},{1,3},{2,0},{3,1},{4,6},{5,7},{6,4},{7,5},{8,10},{9,11},{10,... | collective-permute-start | bytes 2457608 | tf_op jit(solution)/shard_map/ppermute | solution.py:23
  212.5 3.9 %collective-permute-start.31 = (bf16[152,128]{1,0:T(8,128)(2,1)S(1)}, bf16[152,128]{1,0:T(8,128)(2,1)S(1)}, u32[]{:S(2)}, u32[]{:S(2)}) collective-permute-start(bf16[152,128]{1,0:T(8,128)(2,1)S(1)} %add_convert_fusion.1), channel_id=1, source_target_pairs={{0,16},{4,20},{8,24},{12,28},{16,0},{20,4},{24,8},{28,12},{32,48},... | collective-permute-start | bytes 116744 | tf_op jit(solution)/shard_map/ppermute | solution.py:23
  213.9 4.3 %collective-permute-start.32 = (bf16[152,128]{1,0:T(8,128)(2,1)S(1)}, bf16[152,128]{1,0:T(8,128)(2,1)S(1)}, u32[]{:S(2)}, u32[]{:S(2)}) collective-permute-start(bf16[152,128]{1,0:T(8,128)(2,1)S(1)} %add_convert_fusion.1), channel_id=1, source_target_pairs={{0,32},{4,36},{8,40},{12,44},{16,48},{20,52},{24,56},{28,60},{32,0... | collective-permute-start | bytes 116744 | tf_op jit(solution)/shard_map/ppermute | solution.py:23
  216.1 4.0 %collective-permute-start.33 = (bf16[152,128]{1,0:T(8,128)(2,1)S(1)}, bf16[152,128]{1,0:T(8,128)(2,1)S(1)}, u32[]{:S(2)}, u32[]{:S(2)}) collective-permute-start(bf16[152,128]{1,0:T(8,128)(2,1)S(1)} %add_convert_fusion.1), channel_id=1, source_target_pairs={{0,48},{4,52},{8,56},{12,60},{16,32},{20,36},{24,40},{28,44},{32,1... | collective-permute-start | bytes 116744 | tf_op jit(solution)/shard_map/ppermute | solution.py:23
  220.2 4.6 %collective-permute-start.34 = (bf16[4,152,128]{2,1,0:T(8,128)(2,1)S(1)}, bf16[4,152,128]{2,1,0:T(8,128)(2,1)S(1)}, u32[]{:S(2)}, u32[]{:S(2)}) collective-permute-start(bf16[4,152,128]{2,1,0:T(8,128)(2,1)S(1)} %get-tuple-element.97), channel_id=1, source_target_pairs={{0,4},{4,0},{8,12},{12,8},{16,20},{20,16},{24,28},{28,24},{32,36},... | collective-permute-start | bytes 466952 | tf_op jit(solution)/shard_map/ppermute | solution.py:23
  221.7 5.8 %collective-permute-start.35 = (bf16[4,152,128]{2,1,0:T(8,128)(2,1)S(1)}, bf16[4,152,128]{2,1,0:T(8,128)(2,1)S(1)}, u32[]{:S(2)}, u32[]{:S(2)}) collective-permute-start(bf16[4,152,128]{2,1,0:T(8,128)(2,1)S(1)} %get-tuple-element.97), channel_id=1, source_target_pairs={{0,8},{4,12},{8,0},{12,4},{16,24},{20,28},{24,16},{28,20},{32,40},... | collective-permute-start | bytes 466952 | tf_op jit(solution)/shard_map/ppermute | solution.py:23
  223.2 6.0 %collective-permute-start.36 = (bf16[4,152,128]{2,1,0:T(8,128)(2,1)S(1)}, bf16[4,152,128]{2,1,0:T(8,128)(2,1)S(1)}, u32[]{:S(2)}, u32[]{:S(2)}) collective-permute-start(bf16[4,152,128]{2,1,0:T(8,128)(2,1)S(1)} %get-tuple-element.97), channel_id=1, source_target_pairs={{0,12},{4,8},{8,4},{12,0},{16,28},{20,24},{24,20},{28,16},{32,44},... | collective-permute-start | bytes 466952 | tf_op jit(solution)/shard_map/ppermute | solution.py:23
  229.2 10.1 %copy-start.2 = (bf16[4,4,152,128]{3,2,1,0:T(8,128)(2,1)}, bf16[4,4,152,128]{3,2,1,0:T(8,128)(2,1)S(1)}, u32[]{:S(2)}) copy-start(bf16[4,4,152,128]{3,2,1,0:T(8,128)(2,1)S(1)} %pad_maximum_fusion.1.near_ref) | copy-start | bytes 1867780
  229.2 10.1 %copy-start.20 = (f32[1024]{0:T(1024)S(1)}, f32[1024]{0:T(1024)}, u32[]{:S(2)}) copy-start(f32[1024]{0:T(1024)} %param.10) | copy-start | bytes 12292
  229.2 13.3 %collective-permute-start.37 = (bf16[4,4,152,128]{3,2,1,0:T(8,128)(2,1)S(1)}, bf16[4,4,152,128]{3,2,1,0:T(8,128)(2,1)S(1)}, u32[]{:S(2)}, u32[]{:S(2)}) collective-permute-start(bf16[4,4,152,128]{3,2,1,0:T(8,128)(2,1)S(1)} %pad_maximum_fusion.1.near_ref), channel_id=1, source_target_pairs={{0,1},{1,0},{2,3},{3,2},{4,5},{5,4},{6,7},{7,6},{8,9},{9,8},{10,11... | collective-permute-start | bytes 1867784 | tf_op jit(solution)/shard_map/ppermute | solution.py:23
  (11 other events, 12.0 us)

commit v5 on v4

--- a/solution.py
+++ b/solution.py
@@ -535,8 +535,7 @@
     cell = summed(line, "dom", 4)
     cell = after(cell, *returned[1:])
     cell = cell + swapped(cell, "rep", 2)
-    cell = cell + swapped(cell, "dom", 16)
-    total = (cell + swapped(cell, "dom", 32)).astype(BF16)
+    total = summed([cell] * 4, "dom", 16).astype(BF16)
     src_sum = src_keep + swapped(src_send, "rep", 1).astype(F32)
     src_got = swapped(after(src_sum[1], total).astype(BF16), "rep", 2)
     line = collected(total, "dom", 4)

time: 252 us -> 251 us (level)
  starting transfers between devices: 95.8 us -> 83 us
  Pallas kernels: 91 us -> 98 us
  waiting for transfers between devices: 33.6 us -> 38.5 us
    ppermute x33 -> x34, starting transfers between devices: 86.4 us -> 78.3 us  [swapped(): lax.ppermute(x, axis, [(i, i ^ mask) for i in range(lax.axis_size(axis))])]
    ppermute x33 -> x34, waiting for transfers between devices: 28.6 us -> 36.5 us  [swapped(): lax.ppermute(x, axis, [(i, i ^ mask) for i in range(lax.axis_size(axis))])]
    pallas_call x8, Pallas kernels: 91 us -> 98 us  [call(): pl.pallas_call(kernel, grid_spec=pltpu.PrefetchScalarGridSpec(num_scalar_...]
    ppermute x5, starting transfers between devices: 9.32 us -> 4.75 us  [swapped_far(): return lax.ppermute(x, ('dom', 'rep'), pairs)]
    ppermute x5, waiting for transfers between devices: 4.98 us -> 2.05 us  [swapped_far(): return lax.ppermute(x, ('dom', 'rep'), pairs)]
  transfers between devices with their start and end apart: 38 -> 39, of which waited for: 18 -> 19; matrix products, arithmetic and copies ran while one was open for 9% -> 9% of each run, Pallas kernels for 24% -> 27%
where the time goes in v5:
time: 251 us; the launch traced here: 248 us
  Pallas kernels  98 us (39%)
  starting transfers between devices  83 us (33%)
  waiting for transfers between devices  38.5 us (15%)
  other arithmetic  19.2 us (8%)
  local copies, waits for them, and re-layouts  7.84 us (3%)
    pallas_call x8, Pallas kernels, call(): pl.pallas_call(kernel, grid_spec=pltpu.PrefetchScalarGridSpec(num_scalar_...  98 us
    ppermute x34, starting transfers between devices, swapped(): lax.ppermute(x, axis, [(i, i ^ mask) for i in range(lax.axis_size(axis))])  78.3 us
    ppermute x34, waiting for transfers between devices, swapped(): lax.ppermute(x, axis, [(i, i ^ mask) for i in range(lax.axis_size(axis))])  36.5 us
    sort x1, other arithmetic, body(): lax.sort((key, edge_source, edge_target, edge_relation), num_keys=1)  6 us
  transfers between devices with their start and end apart: 39, of which 19 were waited for; matrix products, arithmetic and copies ran while one was open for 9% of the time, Pallas kernels for 27%

profile of v5, /device:TPU:1, one launch (start us, length us, event | category | flops | bytes accessed | tf_op | source)
XLA Modules:
  0.0 248.5 jit_solution(8339615339731899423)
XLA Ops:
  0.6 7.8 %collective-permute-start = (s32[1024]{0:T(1024)}, s32[1024]{0:T(1024)S(1)}, u32[]{:S(2)}, u32[]{:S(2)}) collective-permute-start(s32[1024]{0:T(1024)} %param.17), channel_id=1, source_target_pairs={{0,128},{4,132},{8,136},{12,140},{16,144},{20,148},{24,152},{28,15... | collective-permute-start | bytes 12296 | tf_op jit(solution)/shard_map/ppermute | solution.py:23
  8.5 1.3 dynamic-slice_bitcast_fusion
  11.4 6.0 %sort.39 = (s32[4096]{0:T(1024)}, s32[4096]{0:T(1024)S(1)}, s32[4096]{0:T(1024)S(1)}, s32[4096]{0:T(1024)}, s32[4096]{0:T(1024)}) sort(s32[4096]{0:T(1024)S(1)} %fusion.13, s32[4096]{0:T(1024)S(1)} %copy-done.14, s32[4096]{0:T(1024)S(1)} %copy-done.15, s32[4096]{0:T(1024)S(1)} %copy-done.17, s32[4096]{0:T(1024)S(1)} %iota.25), dimensions={0}, to_apply=%region_0.1 | sort | flops 49152 | bytes 163840 | tf_op jit(solution)/shard_map/sort | solution.py:373
  17.4 1.7 pad_maximum_fusion.table_ref
  20.5 4.3 %partner_negatives.1 = bf16[400,256]{1,0:T(8,128)(2,1)} custom-call(s32[3]{0:T(128)} %pad_add_fusion.3.scal, s32[1,256]{1,0:T(1,128)} %bitcast.99, bf16[400,4096]{1,0:T(8,128)(2,1)} %bitcast.77), custom_call_target="tpu_custom_call" | custom-call | tf_op jit(solution)/shard_map/partner_negatives/pallas_call | solution.py:50
  24.8 1.1 copy.21
  25.9 4.2 %collective-permute-start.1 = (bf16[400,256]{0,1:T(8,128)(2,1)S(1)}, bf16[400,256]{0,1:T(8,128)(2,1)S(1)}, u32[]{:S(2)}, u32[]{:S(2)}) collective-permute-start(bf16[400,256]{0,1:T(8,128)(2,1)S(1)} %copy.21), channel_id=1, source_target_pairs={{0,130},{1,131},{2,128},{3,129},{4,134},{5,135},{6,132},{7,133},{8... | collective-permute-start | bytes 614408 | tf_op jit(solution)/shard_map/ppermute | solution.py:33
  31.2 10.6 %source_rows.1.s_ref = bf16[400,4096]{1,0:T(8,128)(2,1)} custom-call(s32[67]{0:T(128)} %pad_add_fusion.2.scal, s32[1,4096]{1,0:T(1,128)} %bitcast.90, bf16[400,4096]{1,0:T(8,128)(2,1)} %bitcast.78), custom_call_target="tpu_custom_call" | custom-call | tf_op jit(solution)/shard_map/source_rows/pallas_call | solution.py:50
  41.8 1.0 collective-permute-done.1
  43.2 13.8 %relation_rows.1.r_ref = f32[400,4096]{1,0:T(8,128)} custom-call(s32[67]{0:T(128)} %pad_add_fusion.2.scal, s32[1,4096]{1,0:T(1,128)} %bitcast.96, bf16[800,1536]{1,0:T(8,128)(2,1)} %pad_maximum_fusion.table_ref), custom_call_target="tpu_custom_call" | custom-call | tf_op jit(solution)/shard_map/relation_rows/pallas_call | solution.py:50
  57.0 3.4 %collective-permute-start.3 = (bf16[400,256]{0,1:T(8,128)(2,1)S(1)}, bf16[400,256]{0,1:T(8,128)(2,1)S(1)}, u32[]{:S(2)}, u32[]{:S(2)}) collective-permute-start(bf16[400,256]{0,1:T(8,128)(2,1)S(1)} %collective-permute-done.1), channel_id=1, source_target_pairs={{0,1},{1,0},{2,3},{3,2},{4,5},{5,4},{6,7},{7,6},{8,9},{9,8},{10,11... | collective-permute-start | bytes 614408 | tf_op jit(solution)/shard_map/ppermute | solution.py:23
  60.4 14.9 %collective-permute-start.7 = (bf16[400,512]{1,0:T(8,128)(2,1)}, bf16[400,512]{1,0:T(8,128)(2,1)S(1)}, u32[]{:S(2)}, u32[]{:S(2)}) collective-permute-start(bf16[400,512]{1,0:T(8,128)(2,1)} %collective-permute-done.5.refs_2_), channel_id=1, source_target_pairs={{0,2},{1,3},{2,0},{3,1},{4,6},{5,7},{6,4},{7,5},{8,10},{9,11},{10,... | collective-permute-start | bytes 1228808 | tf_op jit(solution)/shard_map/ppermute | solution.py:23
  76.5 1.0 collective-permute-done.4
  77.5 1.2 copy.22.neg_t_ref
  78.7 1.1 multiply_bitcast_fusion.half_neg_ref
  79.8 16.2 %negative_scores.1 = (f32[400,4096]{1,0:T(8,128)}, bf16[400,1024]{1,0:T(8,128)(2,1)}) custom-call(s32[67]{0:T(128)} %pad_add_fusion.2.scal, bf16[400,4096]{1,0:T(8,128)(2,1)} %source_rows.1.s_ref, f32[400,4096]{1,0:T(8,128)} %relation_rows.1.r_ref, bf16[400,1024]{1,0:T(8,128)(2,1)} %copy.22.neg_t_ref, bf16[1024,400]{1,0:T(8,128)(2,1)} %multiply_bitcast_fusion.half_neg_ref), custom_call_target="tpu_custom_call" | custom-call | tf_op jit(solution)/shard_map/negative_scores/pallas_call | solution.py:50
  99.2 26.7 %targets.1 = (bf16[400,4096]{1,0:T(8,128)(2,1)}, bf16[400,4096]{1,0:T(8,128)(2,1)}, f32[400,1024]{1,0:T(8,128)}, f32[400,1024]{1,0:T(8,128)}, bf16[400,1024]{1,0:T(8,128)(2,1)}, /*index=5*/bf16[400,1024]{1,0:T(8,128)(2,1)}) custom-call(s32[67]{0:T(128)} %pad_add_fusion.2.scal, bf16[400,4096]{1,0:T(8,128)(2,1)} %source_rows.1.s_ref, ...), custom_call_target="tpu_custom_call" | custom-call | tf_op jit(solution)/shard_map/targets/pallas_call | solution.py:50
  126.5 2.0 collective-permute-done.14
  128.5 1.7 add_convert_fusion
  130.3 3.9 %collective-permute-start.15 = (bf16[400,512]{1,0:T(8,128)(2,1)S(1)}, bf16[400,512]{1,0:T(8,128)(2,1)S(1)}, u32[]{:S(2)}, u32[]{:S(2)}) collective-permute-start(bf16[400,512]{1,0:T(8,128)(2,1)S(1)} %get-tuple-element.86), channel_id=1, source_target_pairs={{0,2},{1,3},{2,0},{3,1},{4,6},{5,7},{6,4},{7,5},{8,10},{9,11},{10,... | collective-permute-start | bytes 1228808 | tf_op jit(solution)/shard_map/ppermute | solution.py:23
  134.3 9.7 %relation_grads.1 = (f32[16,152,128]{2,1,0:T(8,128)}, f32[16,152,128]{2,1,0:T(8,128)}) custom-call(s32[67]{0:T(128)} %pad_add_fusion.2.scal, bf16[400,4096]{1,0:T(8,128)(2,1)} %get-tuple-element.65.g_ref, s32[1,4096]{1,0:T(1,128)} %bitcast.97), custom_call_target="tpu_custom_call" | custom-call | flops 5033164800 | tf_op jit(solution)/shard_map/relation_grads/pallas_call | solution.py:50
  145.5 12.2 %source_grads.1 = (f32[2,400,1024]{2,1,0:T(8,128)}, bf16[2,400,1024]{2,1,0:T(8,128)(2,1)}) custom-call(s32[67]{0:T(128)} %pad_add_fusion.2.scal, bf16[400,4096]{1,0:T(8,128)(2,1)} %get-tuple-element.69.g_ref, s32[1,4096]{1,0:T(1,128)} %bitcast.91), custom_call_target="tpu_custom_call" | custom-call | flops 6710886400 | tf_op jit(solution)/shard_map/source_grads/pallas_call | solution.py:50
  157.7 1.0 collective-permute-done.19
  158.8 1.1 collective-permute-done.18
  160.1 10.9 %collective-permute-start.20 = (bf16[4,152,128]{2,1,0:T(8,128)(2,1)S(1)}, bf16[4,152,128]{2,1,0:T(8,128)(2,1)S(1)}, u32[]{:S(2)}, u32[]{:S(2)}) collective-permute-start(bf16[4,152,128]{2,1,0:T(8,128)(2,1)S(1)} %get-tuple-element.90), channel_id=1, source_target_pairs={{0,4},{4,0},{8,12},{12,8},{16,20},{20,16},{24,28},{28,24},{32,36},... | collective-permute-start | bytes 466952 | tf_op jit(solution)/shard_map/ppermute | solution.py:23
  171.0 2.6 %collective-permute-start.21 = (bf16[4,152,128]{2,1,0:T(8,128)(2,1)S(1)}, bf16[4,152,128]{2,1,0:T(8,128)(2,1)S(1)}, u32[]{:S(2)}, u32[]{:S(2)}) collective-permute-start(bf16[4,152,128]{2,1,0:T(8,128)(2,1)S(1)} %get-tuple-element.92), channel_id=1, source_target_pairs={{0,8},{4,12},{8,0},{12,4},{16,24},{20,28},{24,16},{28,20},{32,40},... | collective-permute-start | bytes 466952 | tf_op jit(solution)/shard_map/ppermute | solution.py:23
  174.7 5.7 %collective-permute-done.21 = bf16[4,152,128]{2,1,0:T(8,128)(2,1)S(1)} collective-permute-done((bf16[4,152,128]{2,1,0:T(8,128)(2,1)S(1)}, bf16[4,152,128]{2,1,0:T(8,128)(2,1)S(1)}, u32[]{:S(2)}, u32[]{:S(2)}) %collective-permute-start.21) | collective-permute-done | bytes 155680 | tf_op jit(solution)/shard_map/ppermute | solution.py:23
  180.3 2.7 %collective-permute-done.22 = bf16[4,152,128]{2,1,0:T(8,128)(2,1)S(1)} collective-permute-done((bf16[4,152,128]{2,1,0:T(8,128)(2,1)S(1)}, bf16[4,152,128]{2,1,0:T(8,128)(2,1)S(1)}, u32[]{:S(2)}, u32[]{:S(2)}) %collective-permute-start.22) | collective-permute-done | bytes 155680 | tf_op jit(solution)/shard_map/ppermute | solution.py:23
  184.0 3.4 %collective-permute-start.24 = (f32[152,128]{1,0:T(8,128)S(1)}, f32[152,128]{1,0:T(8,128)S(1)}, u32[]{:S(2)}, u32[]{:S(2)}) collective-permute-start(f32[152,128]{1,0:T(8,128)S(1)} %get-tuple-element.94), channel_id=1, source_target_pairs={{0,32},{4,36},{8,40},{12,44},{16,48},{20,52},{24,56},{28,60},{32,0... | collective-permute-start | bytes 233480 | tf_op jit(solution)/shard_map/ppermute | solution.py:23
  187.6 2.6 %collective-permute-done.24 = f32[152,128]{1,0:T(8,128)S(1)} collective-permute-done((f32[152,128]{1,0:T(8,128)S(1)}, f32[152,128]{1,0:T(8,128)S(1)}, u32[]{:S(2)}, u32[]{:S(2)}) %collective-permute-start.24) | collective-permute-done | bytes 77856 | tf_op jit(solution)/shard_map/ppermute | solution.py:23
  190.2 2.2 collective-permute-done.25
  192.9 3.3 %collective-permute-done.27 = f32[152,128]{1,0:T(8,128)S(1)} collective-permute-done((f32[152,128]{1,0:T(8,128)S(1)}, f32[152,128]{1,0:T(8,128)S(1)}, u32[]{:S(2)}, u32[]{:S(2)}) %collective-permute-start.27) | collective-permute-done | bytes 77856 | tf_op jit(solution)/shard_map/ppermute | solution.py:23
  196.2 4.9 %collective-permute-start.28 = (f32[152,128]{1,0:T(8,128)S(1)}, f32[152,128]{1,0:T(8,128)S(1)}, u32[]{:S(2)}, u32[]{:S(2)}) collective-permute-start(f32[152,128]{1,0:T(8,128)S(1)} %add.105), channel_id=1, source_target_pairs={{0,64},{4,68},{8,72},{12,76},{16,80},{20,84},{24,88},{28,92},{32,9... | collective-permute-start | bytes 233480 | tf_op jit(solution)/shard_map/ppermute | solution.py:23
  201.2 1.8 collective-permute-start.29
  203.0 1.7 collective-permute-start.30
  204.7 4.1 %collective-permute-done.29 = f32[152,128]{1,0:T(8,128)S(1)} collective-permute-done((f32[152,128]{1,0:T(8,128)S(1)}, f32[152,128]{1,0:T(8,128)S(1)}, u32[]{:S(2)}, u32[]{:S(2)}) %collective-permute-start.29) | collective-permute-done | bytes 77856 | tf_op jit(solution)/shard_map/ppermute | solution.py:23
  208.8 1.2 collective-permute-done.30
  211.1 1.1 collective-permute-start.32
  212.2 8.4 %collective-permute-start.33 = (bf16[152,128]{1,0:T(8,128)(2,1)S(1)}, bf16[152,128]{1,0:T(8,128)(2,1)S(1)}, u32[]{:S(2)}, u32[]{:S(2)}) collective-permute-start(bf16[152,128]{1,0:T(8,128)(2,1)S(1)} %add_convert_fusion.1), channel_id=1, source_target_pairs={{0,32},{4,36},{8,40},{12,44},{16,48},{20,52},{24,56},{28,60},{32,0... | collective-permute-start | bytes 116744 | tf_op jit(solution)/shard_map/ppermute | solution.py:23
  220.6 1.8 collective-permute-done.33
  222.4 2.3 collective-permute-done.34
  224.7 3.1 %collective-permute-start.36 = (bf16[4,152,128]{2,1,0:T(8,128)(2,1)S(1)}, bf16[4,152,128]{2,1,0:T(8,128)(2,1)S(1)}, u32[]{:S(2)}, u32[]{:S(2)}) collective-permute-start(bf16[4,152,128]{2,1,0:T(8,128)(2,1)S(1)} %get-tuple-element.97), channel_id=1, source_target_pairs={{0,8},{4,12},{8,0},{12,4},{16,24},{20,28},{24,16},{28,20},{32,40},... | collective-permute-start | bytes 466952 | tf_op jit(solution)/shard_map/ppermute | solution.py:23
  229.2 3.3 %collective-permute-done.36 = bf16[4,152,128]{2,1,0:T(8,128)(2,1)S(1)} collective-permute-done((bf16[4,152,128]{2,1,0:T(8,128)(2,1)S(1)}, bf16[4,152,128]{2,1,0:T(8,128)(2,1)S(1)}, u32[]{:S(2)}, u32[]{:S(2)}) %collective-permute-start.36) | collective-permute-done | bytes 155680 | tf_op jit(solution)/shard_map/ppermute | solution.py:23
  232.5 1.3 collective-permute-done.37
  233.9 4.1 %collective-permute-start.38 = (bf16[4,4,152,128]{3,2,1,0:T(8,128)(2,1)S(1)}, bf16[4,4,152,128]{3,2,1,0:T(8,128)(2,1)S(1)}, u32[]{:S(2)}, u32[]{:S(2)}) collective-permute-start(bf16[4,4,152,128]{3,2,1,0:T(8,128)(2,1)S(1)} %pad_maximum_fusion.1.near_ref), channel_id=1, source_target_pairs={{0,1},{1,0},{2,3},{3,2},{4,5},{5,4},{6,7},{7,6},{8,9},{9,8},{10,11... | collective-permute-start | bytes 1867784 | tf_op jit(solution)/shard_map/ppermute | solution.py:23
  239.0 2.6 %fusion.4 = bf16[1024,400]{0,1:T(8,128)(2,1)} fusion(f32[1024]{0:T(1024)S(1)} %get-tuple-element.84, bf16[400,512]{1,0:T(8,128)(2,1)S(1)} %collective-permute-done.26, bf16[400,512]{1,0:T(8,128)(2,1)S(1)} %collective-permute-done.18, bf16[400,1024]{1,0:T(8,128)(2,1)S(1)} %collective-permute-done.31, f32[2,400,1024]{2,1,0:T(8,128)S(1)} %convert_add_fusion, ...), kind=kLoop, calls=%fused_computation.19 | loop fusion | flops 4915200 | bytes 4919300 | tf_op jit(solution)/shard_map/transpose | solution.py:564
  242.4 4.6 %relation_update.1 = (f32[400,1345]{1,0:T(8,128)}, f32[1,1345]{1,0:T(1,128)}) custom-call(s32[3]{0:T(128)} %pad_add_fusion.3.scal, f32[400,1345]{1,0:T(8,128)} %bitcast.79, f32[1,1345]{1,0:T(1,128)} %reshape.55.state_ref, bf16[4,4,152,128]{3,2,1,0:T(8,128)(2,1)} %copy-done.2, bf16[4,4,152,128]{3,2,1,0:T(8,128)(2,1)} %copy-done.5), custom_call_target="tpu_custom_call" | custom-call | tf_op jit(solution)/shard_map/relation_update/pallas_call | solution.py:50
  247.0 1.3 reduce
  (129 shorter events, 18.0 us)
Async XLA Ops:
  0.6 19.2 %collective-permute-start = (s32[1024]{0:T(1024)}, s32[1024]{0:T(1024)S(1)}, u32[]{:S(2)}, u32[]{:S(2)}) collective-permute-start(s32[1024]{0:T(1024)} %param.17), channel_id=1, source_target_pairs={{0,128},{4,132},{8,136},{12,140},{16,144},{20,148},{24,152},{28,15... | collective-permute-start | bytes 12296 | tf_op jit(solution)/shard_map/ppermute | solution.py:23
  9.9 50.5 %collective-permute-start.5 = (bf16[400,512]{1,0:T(8,128)(2,1)S(1)}, bf16[400,512]{1,0:T(8,128)(2,1)}, u32[]{:S(2)}, u32[]{:S(2)}) collective-permute-start(bf16[400,512]{1,0:T(8,128)(2,1)S(1)} %get-tuple-element.89), channel_id=1, source_target_pairs={{0,130},{1,131},{2,128},{3,129},{4,134},{5,135},{6,132},{7,133},{8... | collective-permute-start | bytes 1228808 | tf_op jit(solution)/shard_map/ppermute | solution.py:33
  25.9 16.8 %collective-permute-start.1 = (bf16[400,256]{0,1:T(8,128)(2,1)S(1)}, bf16[400,256]{0,1:T(8,128)(2,1)S(1)}, u32[]{:S(2)}, u32[]{:S(2)}) collective-permute-start(bf16[400,256]{0,1:T(8,128)(2,1)S(1)} %copy.21), channel_id=1, source_target_pairs={{0,130},{1,131},{2,128},{3,129},{4,134},{5,135},{6,132},{7,133},{8... | collective-permute-start | bytes 614408 | tf_op jit(solution)/shard_map/ppermute | solution.py:33
  30.1 45.8 %collective-permute-start.6 = (bf16[400,512]{1,0:T(8,128)(2,1)S(1)}, bf16[400,512]{1,0:T(8,128)(2,1)S(1)}, u32[]{:S(2)}, u32[]{:S(2)}) collective-permute-start(bf16[400,512]{1,0:T(8,128)(2,1)S(1)} %get-tuple-element.52), channel_id=1, source_target_pairs={{0,130},{1,131},{2,128},{3,129},{4,134},{5,135},{6,132},{7,133},{8... | collective-permute-start | bytes 1228808 | tf_op jit(solution)/shard_map/ppermute | solution.py:33
  42.7 32.9 %collective-permute-start.2 = (bf16[400,256]{0,1:T(8,128)(2,1)S(1)}, bf16[400,256]{0,1:T(8,128)(2,1)S(1)}, u32[]{:S(2)}, u32[]{:S(2)}) collective-permute-start(bf16[400,256]{0,1:T(8,128)(2,1)S(1)} %collective-permute-done.1), channel_id=1, source_target_pairs={{0,2},{1,3},{2,0},{3,1},{4,6},{5,7},{6,4},{7,5},{8,10},{9,11},{10,... | collective-permute-start | bytes 614408 | tf_op jit(solution)/shard_map/ppermute | solution.py:23
  57.0 19.0 %collective-permute-start.3 = (bf16[400,256]{0,1:T(8,128)(2,1)S(1)}, bf16[400,256]{0,1:T(8,128)(2,1)S(1)}, u32[]{:S(2)}, u32[]{:S(2)}) collective-permute-start(bf16[400,256]{0,1:T(8,128)(2,1)S(1)} %collective-permute-done.1), channel_id=1, source_target_pairs={{0,1},{1,0},{2,3},{3,2},{4,5},{5,4},{6,7},{7,6},{8,9},{9,8},{10,11... | collective-permute-start | bytes 614408 | tf_op jit(solution)/shard_map/ppermute | solution.py:23
  60.4 35.5 %collective-permute-start.7 = (bf16[400,512]{1,0:T(8,128)(2,1)}, bf16[400,512]{1,0:T(8,128)(2,1)S(1)}, u32[]{:S(2)}, u32[]{:S(2)}) collective-permute-start(bf16[400,512]{1,0:T(8,128)(2,1)} %collective-permute-done.5.refs_2_), channel_id=1, source_target_pairs={{0,2},{1,3},{2,0},{3,1},{4,6},{5,7},{6,4},{7,5},{8,10},{9,11},{10,... | collective-permute-start | bytes 1228808 | tf_op jit(solution)/shard_map/ppermute | solution.py:23
  75.3 21.9 %collective-permute-start.9 = (bf16[400,512]{1,0:T(8,128)(2,1)}, bf16[400,512]{1,0:T(8,128)(2,1)S(1)}, u32[]{:S(2)}, u32[]{:S(2)}) collective-permute-start(bf16[400,512]{1,0:T(8,128)(2,1)} %collective-permute-done.5.refs_2_), channel_id=1, source_target_pairs={{0,1},{1,0},{2,3},{3,2},{4,5},{5,4},{6,7},{7,6},{8,9},{9,8},{10,11... | collective-permute-start | bytes 1228808 | tf_op jit(solution)/shard_map/ppermute | solution.py:23
  75.6 1.8 collective-permute-start.4
  75.8 2.9 %copy-start.6 = (bf16[400,512]{1,0:T(8,128)(2,1)}, bf16[400,512]{1,0:T(8,128)(2,1)S(1)}, u32[]{:S(2)}) copy-start(bf16[400,512]{1,0:T(8,128)(2,1)S(1)} %collective-permute-done.6.refs_3_) | copy-start | bytes 1228804
  75.8 20.2 %collective-permute-start.8 = (bf16[400,512]{1,0:T(8,128)(2,1)S(1)}, bf16[400,512]{1,0:T(8,128)(2,1)S(1)}, u32[]{:S(2)}, u32[]{:S(2)}) collective-permute-start(bf16[400,512]{1,0:T(8,128)(2,1)S(1)} %collective-permute-done.6.refs_3_), channel_id=1, source_target_pairs={{0,2},{1,3},{2,0},{3,1},{4,6},{5,7},{6,4},{7,5},{8,10},{9,11},{10,... | collective-permute-start | bytes 1228808 | tf_op jit(solution)/shard_map/ppermute | solution.py:23
  76.0 21.3 %collective-permute-start.10 = (bf16[400,512]{1,0:T(8,128)(2,1)S(1)}, bf16[400,512]{1,0:T(8,128)(2,1)S(1)}, u32[]{:S(2)}, u32[]{:S(2)}) collective-permute-start(bf16[400,512]{1,0:T(8,128)(2,1)S(1)} %collective-permute-done.6.refs_3_), channel_id=1, source_target_pairs={{0,1},{1,0},{2,3},{3,2},{4,5},{5,4},{6,7},{7,6},{8,9},{9,8},{10,11... | collective-permute-start | bytes 1228808 | tf_op jit(solution)/shard_map/ppermute | solution.py:23
  79.8 16.8 %copy-start.19 = (s32[1024]{0:T(1024)S(1)}, s32[1024]{0:T(1024)}, u32[]{:S(2)}) copy-start(s32[1024]{0:T(1024)} %param.17) | copy-start | bytes 12292
  96.0 2.4 copy-start.7
  96.0 1.8 collective-permute-start.11
  96.1 2.3 copy-start.9
  96.1 2.3 collective-permute-start.12
  125.9 2.6 %collective-permute-start.14 = (bf16[400,1024]{1,0:T(8,128)(2,1)}, bf16[400,1024]{1,0:T(8,128)(2,1)S(1)}, u32[]{:S(2)}, u32[]{:S(2)}) collective-permute-start(bf16[400,1024]{1,0:T(8,128)(2,1)} %get-tuple-element.64), channel_id=1, source_target_pairs={{0,1},{1,0},{2,3},{3,2},{4,5},{5,4},{6,7},{7,6},{8,9},{9,8},{10,11... | collective-permute-start | bytes 2457608 | tf_op jit(solution)/shard_map/ppermute | solution.py:23
  126.0 18.0 %collective-permute-start.13 = (bf16[400,1024]{1,0:T(8,128)(2,1)}, bf16[400,1024]{1,0:T(8,128)(2,1)S(1)}, u32[]{:S(2)}, u32[]{:S(2)}) collective-permute-start(bf16[400,1024]{1,0:T(8,128)(2,1)} %get-tuple-element.61), channel_id=1, source_target_pairs={{0,1},{1,0},{2,3},{3,2},{4,5},{5,4},{6,7},{7,6},{8,9},{9,8},{10,11... | collective-permute-start | bytes 2457608 | tf_op jit(solution)/shard_map/ppermute | solution.py:23
  130.3 14.6 %copy-start.3 = (f32[400,1024]{1,0:T(8,128)S(1)}, f32[400,1024]{1,0:T(8,128)}, u32[]{:S(2)}) copy-start(f32[400,1024]{1,0:T(8,128)} %get-tuple-element.60) | copy-start | bytes 4915204
  130.3 14.9 %collective-permute-start.15 = (bf16[400,512]{1,0:T(8,128)(2,1)S(1)}, bf16[400,512]{1,0:T(8,128)(2,1)S(1)}, u32[]{:S(2)}, u32[]{:S(2)}) collective-permute-start(bf16[400,512]{1,0:T(8,128)(2,1)S(1)} %get-tuple-element.86), channel_id=1, source_target_pairs={{0,2},{1,3},{2,0},{3,1},{4,6},{5,7},{6,4},{7,5},{8,10},{9,11},{10,... | collective-permute-start | bytes 1228808 | tf_op jit(solution)/shard_map/ppermute | solution.py:23
  144.0 14.7 %collective-permute-start.19 = (bf16[400,512]{1,0:T(8,128)(2,1)S(1)}, bf16[400,512]{1,0:T(8,128)(2,1)S(1)}, u32[]{:S(2)}, u32[]{:S(2)}) collective-permute-start(bf16[400,512]{1,0:T(8,128)(2,1)S(1)} %get-tuple-element.87), channel_id=1, source_target_pairs={{0,2},{1,3},{2,0},{3,1},{4,6},{5,7},{6,4},{7,5},{8,10},{9,11},{10,... | collective-permute-start | bytes 1228808 | tf_op jit(solution)/shard_map/ppermute | solution.py:23
  144.1 15.8 %collective-permute-start.17 = (f32[16,152,128]{2,1,0:T(8,128)}, f32[16,152,128]{2,1,0:T(8,128)S(1)}, u32[]{:S(2)}, u32[]{:S(2)}) collective-permute-start(f32[16,152,128]{2,1,0:T(8,128)} %get-tuple-element.72), channel_id=1, source_target_pairs={{0,1},{1,0},{2,3},{3,2},{4,5},{5,4},{6,7},{7,6},{8,9},{9,8},{10,11... | collective-permute-start | bytes 3735560 | tf_op jit(solution)/shard_map/ppermute | solution.py:23
  145.4 14.4 %collective-permute-start.18 = (bf16[400,512]{1,0:T(8,128)(2,1)S(1)}, bf16[400,512]{1,0:T(8,128)(2,1)S(1)}, u32[]{:S(2)}, u32[]{:S(2)}) collective-permute-start(bf16[400,512]{1,0:T(8,128)(2,1)S(1)} %fusion.3), channel_id=1, source_target_pairs={{0,130},{1,131},{2,128},{3,129},{4,134},{5,135},{6,132},{7,133},{8... | collective-permute-start | bytes 1228808 | tf_op jit(solution)/shard_map/ppermute | solution.py:33
  158.6 51.4 %collective-permute-start.16 = (bf16[2,400,1024]{2,1,0:T(8,128)(2,1)}, bf16[2,400,1024]{2,1,0:T(8,128)(2,1)S(1)}, u32[]{:S(2)}, u32[]{:S(2)}) collective-permute-start(bf16[2,400,1024]{2,1,0:T(8,128)(2,1)} %get-tuple-element.71), channel_id=1, source_target_pairs={{0,1},{1,0},{2,3},{3,2},{4,5},{5,4},{6,7},{7,6},{8,9},{9,8},{10,11... | collective-permute-start | bytes 4915208 | tf_op jit(solution)/shard_map/ppermute | solution.py:23
  160.1 14.5 %collective-permute-start.20 = (bf16[4,152,128]{2,1,0:T(8,128)(2,1)S(1)}, bf16[4,152,128]{2,1,0:T(8,128)(2,1)S(1)}, u32[]{:S(2)}, u32[]{:S(2)}) collective-permute-start(bf16[4,152,128]{2,1,0:T(8,128)(2,1)S(1)} %get-tuple-element.90), channel_id=1, source_target_pairs={{0,4},{4,0},{8,12},{12,8},{16,20},{20,16},{24,28},{28,24},{32,36},... | collective-permute-start | bytes 466952 | tf_op jit(solution)/shard_map/ppermute | solution.py:23
  171.0 9.3 %collective-permute-start.21 = (bf16[4,152,128]{2,1,0:T(8,128)(2,1)S(1)}, bf16[4,152,128]{2,1,0:T(8,128)(2,1)S(1)}, u32[]{:S(2)}, u32[]{:S(2)}) collective-permute-start(bf16[4,152,128]{2,1,0:T(8,128)(2,1)S(1)} %get-tuple-element.92), channel_id=1, source_target_pairs={{0,8},{4,12},{8,0},{12,4},{16,24},{20,28},{24,16},{28,20},{32,40},... | collective-permute-start | bytes 466952 | tf_op jit(solution)/shard_map/ppermute | solution.py:23
  173.6 9.4 %collective-permute-start.22 = (bf16[4,152,128]{2,1,0:T(8,128)(2,1)S(1)}, bf16[4,152,128]{2,1,0:T(8,128)(2,1)S(1)}, u32[]{:S(2)}, u32[]{:S(2)}) collective-permute-start(bf16[4,152,128]{2,1,0:T(8,128)(2,1)S(1)} %get-tuple-element.91), channel_id=1, source_target_pairs={{0,12},{4,8},{8,4},{12,0},{16,28},{20,24},{24,20},{28,16},{32,44},... | collective-permute-start | bytes 466952 | tf_op jit(solution)/shard_map/ppermute | solution.py:23
  173.6 18.9 %collective-permute-start.26 = (bf16[400,512]{1,0:T(8,128)(2,1)S(1)}, bf16[400,512]{1,0:T(8,128)(2,1)S(1)}, u32[]{:S(2)}, u32[]{:S(2)}) collective-permute-start(bf16[400,512]{1,0:T(8,128)(2,1)S(1)} %fusion.2), channel_id=1, source_target_pairs={{0,130},{1,131},{2,128},{3,129},{4,134},{5,135},{6,132},{7,133},{8... | collective-permute-start | bytes 1228808 | tf_op jit(solution)/shard_map/ppermute | solution.py:33
  173.6 36.4 %copy-start.1 = (f32[2,400,1024]{2,1,0:T(8,128)S(1)}, f32[2,400,1024]{2,1,0:T(8,128)}, u32[]{:S(2)}) copy-start(f32[2,400,1024]{2,1,0:T(8,128)} %get-tuple-element.70) | copy-start | bytes 9830404
  183.1 4.5 %collective-permute-start.23 = (f32[152,128]{1,0:T(8,128)S(1)}, f32[152,128]{1,0:T(8,128)S(1)}, u32[]{:S(2)}, u32[]{:S(2)}) collective-permute-start(f32[152,128]{1,0:T(8,128)S(1)} %get-tuple-element.95), channel_id=1, source_target_pairs={{0,16},{4,20},{8,24},{12,28},{16,0},{20,4},{24,8},{28,12},{32,48},... | collective-permute-start | bytes 233480 | tf_op jit(solution)/shard_map/ppermute | solution.py:23
  184.0 6.2 %collective-permute-start.24 = (f32[152,128]{1,0:T(8,128)S(1)}, f32[152,128]{1,0:T(8,128)S(1)}, u32[]{:S(2)}, u32[]{:S(2)}) collective-permute-start(f32[152,128]{1,0:T(8,128)S(1)} %get-tuple-element.94), channel_id=1, source_target_pairs={{0,32},{4,36},{8,40},{12,44},{16,48},{20,52},{24,56},{28,60},{32,0... | collective-permute-start | bytes 233480 | tf_op jit(solution)/shard_map/ppermute | solution.py:23
  187.5 5.0 %collective-permute-start.25 = (f32[152,128]{1,0:T(8,128)S(1)}, f32[152,128]{1,0:T(8,128)S(1)}, u32[]{:S(2)}, u32[]{:S(2)}) collective-permute-start(f32[152,128]{1,0:T(8,128)S(1)} %get-tuple-element.93), channel_id=1, source_target_pairs={{0,48},{4,52},{8,56},{12,60},{16,32},{20,36},{24,40},{28,44},{32,1... | collective-permute-start | bytes 233480 | tf_op jit(solution)/shard_map/ppermute | solution.py:23
  192.5 3.7 %collective-permute-start.27 = (f32[152,128]{1,0:T(8,128)S(1)}, f32[152,128]{1,0:T(8,128)S(1)}, u32[]{:S(2)}, u32[]{:S(2)}) collective-permute-start(f32[152,128]{1,0:T(8,128)S(1)} %fusion.8), channel_id=1, source_target_pairs={{0,2},{1,3},{2,0},{3,1},{4,6},{5,7},{6,4},{7,5},{8,10},{9,11},{10,... | collective-permute-start | bytes 233480 | tf_op jit(solution)/shard_map/ppermute | solution.py:23
  196.2 8.5 %collective-permute-start.28 = (f32[152,128]{1,0:T(8,128)S(1)}, f32[152,128]{1,0:T(8,128)S(1)}, u32[]{:S(2)}, u32[]{:S(2)}) collective-permute-start(f32[152,128]{1,0:T(8,128)S(1)} %add.105), channel_id=1, source_target_pairs={{0,64},{4,68},{8,72},{12,76},{16,80},{20,84},{24,88},{28,92},{32,9... | collective-permute-start | bytes 233480 | tf_op jit(solution)/shard_map/ppermute | solution.py:23
  201.2 7.6 %collective-permute-start.29 = (f32[152,128]{1,0:T(8,128)S(1)}, f32[152,128]{1,0:T(8,128)S(1)}, u32[]{:S(2)}, u32[]{:S(2)}) collective-permute-start(f32[152,128]{1,0:T(8,128)S(1)} %add.105), channel_id=1, source_target_pairs={{0,128},{4,132},{8,136},{12,140},{16,144},{20,148},{24,152},{28,15... | collective-permute-start | bytes 233480 | tf_op jit(solution)/shard_map/ppermute | solution.py:23
  203.0 7.0 %collective-permute-start.30 = (f32[152,128]{1,0:T(8,128)S(1)}, f32[152,128]{1,0:T(8,128)S(1)}, u32[]{:S(2)}, u32[]{:S(2)}) collective-permute-start(f32[152,128]{1,0:T(8,128)S(1)} %add.105), channel_id=1, source_target_pairs={{0,192},{4,196},{8,200},{12,204},{16,208},{20,212},{24,216},{28,22... | collective-permute-start | bytes 233480 | tf_op jit(solution)/shard_map/ppermute | solution.py:23
  210.8 17.8 %copy-start.18 = (f32[1345]{0:T(1024)S(1)}, f32[1345]{0:T(1024)}, u32[]{:S(2)}) copy-start(f32[1345]{0:T(1024)} %param.12) | copy-start | bytes 16144
  211.0 23.0 %collective-permute-start.31 = (bf16[400,1024]{1,0:T(8,128)(2,1)S(1)}, bf16[400,1024]{1,0:T(8,128)(2,1)S(1)}, u32[]{:S(2)}, u32[]{:S(2)}) collective-permute-start(bf16[400,1024]{1,0:T(8,128)(2,1)S(1)} %slice_bitcast_fusion), channel_id=1, source_target_pairs={{0,2},{1,3},{2,0},{3,1},{4,6},{5,7},{6,4},{7,5},{8,10},{9,11},{10,... | collective-permute-start | bytes 2457608 | tf_op jit(solution)/shard_map/ppermute | solution.py:23
  211.1 9.4 %collective-permute-start.32 = (bf16[152,128]{1,0:T(8,128)(2,1)S(1)}, bf16[152,128]{1,0:T(8,128)(2,1)S(1)}, u32[]{:S(2)}, u32[]{:S(2)}) collective-permute-start(bf16[152,128]{1,0:T(8,128)(2,1)S(1)} %add_convert_fusion.1), channel_id=1, source_target_pairs={{0,16},{4,20},{8,24},{12,28},{16,0},{20,4},{24,8},{28,12},{32,48},... | collective-permute-start | bytes 116744 | tf_op jit(solution)/shard_map/ppermute | solution.py:23
  212.2 10.2 %collective-permute-start.33 = (bf16[152,128]{1,0:T(8,128)(2,1)S(1)}, bf16[152,128]{1,0:T(8,128)(2,1)S(1)}, u32[]{:S(2)}, u32[]{:S(2)}) collective-permute-start(bf16[152,128]{1,0:T(8,128)(2,1)S(1)} %add_convert_fusion.1), channel_id=1, source_target_pairs={{0,32},{4,36},{8,40},{12,44},{16,48},{20,52},{24,56},{28,60},{32,0... | collective-permute-start | bytes 116744 | tf_op jit(solution)/shard_map/ppermute | solution.py:23
  220.6 4.0 %collective-permute-start.34 = (bf16[152,128]{1,0:T(8,128)(2,1)S(1)}, bf16[152,128]{1,0:T(8,128)(2,1)S(1)}, u32[]{:S(2)}, u32[]{:S(2)}) collective-permute-start(bf16[152,128]{1,0:T(8,128)(2,1)S(1)} %add_convert_fusion.1), channel_id=1, source_target_pairs={{0,48},{4,52},{8,56},{12,60},{16,32},{20,36},{24,40},{28,44},{32,1... | collective-permute-start | bytes 116744 | tf_op jit(solution)/shard_map/ppermute | solution.py:23
  224.6 4.5 %collective-permute-start.35 = (bf16[4,152,128]{2,1,0:T(8,128)(2,1)S(1)}, bf16[4,152,128]{2,1,0:T(8,128)(2,1)S(1)}, u32[]{:S(2)}, u32[]{:S(2)}) collective-permute-start(bf16[4,152,128]{2,1,0:T(8,128)(2,1)S(1)} %get-tuple-element.97), channel_id=1, source_target_pairs={{0,4},{4,0},{8,12},{12,8},{16,20},{20,16},{24,28},{28,24},{32,36},... | collective-permute-start | bytes 466952 | tf_op jit(solution)/shard_map/ppermute | solution.py:23
  224.7 7.7 %collective-permute-start.36 = (bf16[4,152,128]{2,1,0:T(8,128)(2,1)S(1)}, bf16[4,152,128]{2,1,0:T(8,128)(2,1)S(1)}, u32[]{:S(2)}, u32[]{:S(2)}) collective-permute-start(bf16[4,152,128]{2,1,0:T(8,128)(2,1)S(1)} %get-tuple-element.97), channel_id=1, source_target_pairs={{0,8},{4,12},{8,0},{12,4},{16,24},{20,28},{24,16},{28,20},{32,40},... | collective-permute-start | bytes 466952 | tf_op jit(solution)/shard_map/ppermute | solution.py:23
  227.9 6.0 %collective-permute-start.37 = (bf16[4,152,128]{2,1,0:T(8,128)(2,1)S(1)}, bf16[4,152,128]{2,1,0:T(8,128)(2,1)S(1)}, u32[]{:S(2)}, u32[]{:S(2)}) collective-permute-start(bf16[4,152,128]{2,1,0:T(8,128)(2,1)S(1)} %get-tuple-element.97), channel_id=1, source_target_pairs={{0,12},{4,8},{8,4},{12,0},{16,28},{20,24},{24,20},{28,16},{32,44},... | collective-permute-start | bytes 466952 | tf_op jit(solution)/shard_map/ppermute | solution.py:23
  233.9 4.5 %copy-start.2 = (bf16[4,4,152,128]{3,2,1,0:T(8,128)(2,1)}, bf16[4,4,152,128]{3,2,1,0:T(8,128)(2,1)S(1)}, u32[]{:S(2)}) copy-start(bf16[4,4,152,128]{3,2,1,0:T(8,128)(2,1)S(1)} %pad_maximum_fusion.1.near_ref) | copy-start | bytes 1867780
  233.9 4.5 %copy-start.20 = (f32[1024]{0:T(1024)S(1)}, f32[1024]{0:T(1024)}, u32[]{:S(2)}) copy-start(f32[1024]{0:T(1024)} %param.10) | copy-start | bytes 12292
  233.9 7.7 %collective-permute-start.38 = (bf16[4,4,152,128]{3,2,1,0:T(8,128)(2,1)S(1)}, bf16[4,4,152,128]{3,2,1,0:T(8,128)(2,1)S(1)}, u32[]{:S(2)}, u32[]{:S(2)}) collective-permute-start(bf16[4,4,152,128]{3,2,1,0:T(8,128)(2,1)S(1)} %pad_maximum_fusion.1.near_ref), channel_id=1, source_target_pairs={{0,1},{1,0},{2,3},{3,2},{4,5},{5,4},{6,7},{7,6},{8,9},{9,8},{10,11... | collective-permute-start | bytes 1867784 | tf_op jit(solution)/shard_map/ppermute | solution.py:23
  (12 other events, 14.7 us)
